TPU v7x, 128 devices: a whole 4x4x4 slice. The times are simulated.
128 devices in a mesh: sample: 4 (over x_lo, core), tok: 32 (over x_hi, y, z).
Axes of the slice: x: 4 (x_hi: 2, x_lo: 2; x = x_hi * 2 + x_lo), y: 4, z: 4, core: 2. Of those that a mesh axis runs over, the one named last changes fastest.
Arguments:
- atom_cond: bfloat16 [49152, 128], P('tok'), may hold values from -6 to 6
- atom_pos: float32 [16, 3, 49152], P('sample', None, 'tok'), may hold values from -6 to 6
- atom_token: int32 [49152], P('tok'), may hold values from 0 to 64, as said below
- pos_weight: float32 [3, 128], replicated, may hold values from -4 to 4
- atom_proj: bfloat16 [128, 384], replicated, may hold values from -10 to 10
- atom_output: bfloat16 [128, 128], replicated, may hold values from -0.5 to 0.5
- atom_to_token: bfloat16 [128, 768], replicated, may hold values from -0.5 to 0.5
- tok_single: bfloat16 [2048, 768], P('tok'), may hold values from -6 to 6
- ada_weight: bfloat16 [768, 768], replicated, may hold values from -0.21875 to 0.21875
- pair_rep: bfloat16 [2048, 2048, 128], P('tok', 'sample'), may hold values from -6 to 6
- pair_weight: bfloat16 [128, 16], replicated, may hold values from -0.5 to 0.5
- tok_proj: bfloat16 [768, 3072], replicated, may hold values from -8 to 8
- tok_output: bfloat16 [768, 768], replicated, may hold values from -0.21875 to 0.21875
- transition_in: bfloat16 [768, 3072], replicated, may hold values from -0.21875 to 0.21875
- transition_out: bfloat16 [1536, 768], replicated, may hold values from -0.15625 to 0.15625
- token_to_atom: bfloat16 [768, 128], replicated, may hold values from -0.21875 to 0.21875
- pos_update: float32 [128, 3], replicated, may hold values from -0.5 to 0.5
Outputs:
- token_out: bfloat16 [16, 2048, 768], P('sample', 'tok')
- atom_update: float32 [16, 3, 49152], P('sample', None, 'tok')
Inputs may be any that keep to these rules, and one draw needn't show every extreme that they name: `atom_token`: entry l gives the position, among the 64 tokens of block l // 1536, of the token of slot l; 64 marks an empty slot. Within a block the slots of a token are consecutive, tokens stand in order, empty slots come last, and every token has 4 to 24 slots. Some blocks are full.
All inputs are finite; a program needn't handle non-finite values.
Results may differ from a plain program's by a relative error of at most 0.035.
Values may be sent and summed in bfloat16 or wider, within the bound.
No kernel may reach another device: no remote copies, remote signals or barrier semaphores. Data moves between devices by JAX's collectives and lax.ppermute only.
A program may use at most 256 MiB of HBM per device.

v0:
```python
import jax
import jax.numpy as jnp
import numpy as np
from jax import lax
from jax.sharding import PartitionSpec as P

ATOM_HEADS = 4
QUERY_BLOCK = 32
KEY_WINDOW = 128


NORM_EPSILON = 1e-05
MASKED_SCORE = -1000000000.0


def layer_norm(inputs):
    row_mean = jnp.mean(inputs, axis=-1, keepdims=True)
    centered = inputs - row_mean
    variance = jnp.mean(centered * centered, axis=-1, keepdims=True)
    return centered * lax.rsqrt(variance + NORM_EPSILON)


def band_table(slot_count, group_rows):
    groups = slot_count // group_rows
    query_slot = np.arange(groups)[:, None] * group_rows + np.arange(group_rows)[None, :]
    window_start = np.clip(
        query_slot // QUERY_BLOCK * QUERY_BLOCK - (KEY_WINDOW - QUERY_BLOCK) // 2,
        0,
        slot_count - KEY_WINDOW,
    )
    key_slot = (
        np.arange(groups)[:, None, None] * group_rows
        - group_rows
        + np.arange(3 * group_rows)[None, None, :]
    )
    return (key_slot >= window_start[:, :, None]) & (
        key_slot < window_start[:, :, None] + KEY_WINDOW
    )


def span_blocks(rows, group_rows, groups):
    blocked = (
        rows.reshape(rows.shape[:-2] + (groups + 2, group_rows) + rows.shape[-1:])
        if rows.ndim == 3
        else rows.reshape(groups + 2, group_rows)
    )
    axis = blocked.ndim - 3 if rows.ndim == 3 else 0
    first = lax.slice_in_dim(blocked, 0, groups, axis=axis)
    second = lax.slice_in_dim(blocked, 1, groups + 1, axis=axis)
    third = lax.slice_in_dim(blocked, 2, groups + 2, axis=axis)
    return jnp.concatenate([first, second, third], axis=axis + 1)


def atom_window(atom_normed, atom_proj, filled):
    samples, slot_count, channels = atom_normed.shape
    head_size = channels // ATOM_HEADS
    group_rows = KEY_WINDOW // 2
    groups = slot_count // group_rows
    projected = jnp.einsum(
        "sac,cf->saf", atom_normed, atom_proj, preferred_element_type=jnp.float32
    )
    queries = projected[..., :channels].astype(jnp.bfloat16)
    key_rows = projected[..., channels : 2 * channels].astype(jnp.bfloat16)
    val_rows = projected[..., 2 * channels :].astype(jnp.bfloat16)
    padding = ((0, 0), (group_rows, group_rows), (0, 0))
    key_span = span_blocks(jnp.pad(key_rows, padding), group_rows, groups)
    val_span = span_blocks(jnp.pad(val_rows, padding), group_rows, groups)
    filled_span = span_blocks(jnp.pad(filled, (group_rows, group_rows)), group_rows, groups)
    banded = jnp.asarray(band_table(slot_count, group_rows))
    query_heads = queries.reshape(samples, groups, group_rows, ATOM_HEADS, head_size)
    key_heads = key_span.reshape(samples, groups, 3 * group_rows, ATOM_HEADS, head_size)
    val_heads = val_span.reshape(samples, groups, 3 * group_rows, ATOM_HEADS, head_size)
    scores = jnp.einsum(
        "sgqhd,sgkhd->sghqk", query_heads, key_heads, preferred_element_type=jnp.float32
    ) * head_size ** (-0.5)
    scores = jnp.where(filled_span[None, :, None, None, :], scores, MASKED_SCORE)
    scores = jnp.where(banded[None, :, None, :, :], scores, -jnp.inf)
    row_top = jnp.max(scores, axis=-1, keepdims=True)
    weights = jnp.exp(scores - row_top)
    row_total = jnp.sum(weights, axis=-1, keepdims=True)
    weighted = (
        jnp.einsum(
            "sghqk,sgkhd->sghqd",
            weights.astype(jnp.bfloat16),
            val_heads,
            preferred_element_type=jnp.float32,
        )
        / row_total
    )
    return (
        weighted.transpose(0, 1, 3, 2, 4)
        .reshape(samples, slot_count, channels)
        .astype(jnp.bfloat16)
    )


def attend_piece(query_heads, bias, running, key_rows, val_rows):
    row_top, row_total, weighted = running
    samples, piece_rows, channels = key_rows.shape
    head_count = query_heads.shape[2]
    head_size = query_heads.shape[3]
    piece_bias = bias.astype(jnp.float32)
    key_heads = key_rows.reshape(samples, piece_rows, head_count, head_size)
    val_heads = val_rows.reshape(samples, piece_rows, head_count, head_size)
    scores = (
        jnp.einsum("sqhd,skhd->shqk", query_heads, key_heads, preferred_element_type=jnp.float32)
        * head_size ** (-0.5)
        + piece_bias[None]
    )
    new_top = jnp.max(scores, axis=-1)
    factor = jnp.exp(row_top - new_top)
    weights = jnp.exp(scores - new_top[..., None])
    new_total = row_total * factor + jnp.sum(weights, axis=-1)
    new_weighted = weighted * factor[..., None] + jnp.einsum(
        "shqk,skhd->shqd",
        weights.astype(jnp.bfloat16),
        val_heads,
        preferred_element_type=jnp.float32,
    )
    return (new_top, new_total, new_weighted)


def per_device(
    atom_cond,
    atom_pos,
    atom_token,
    pos_weight,
    atom_proj,
    atom_output,
    atom_to_token,
    tok_single,
    ada_weight,
    pair_rep,
    pair_weight,
    tok_proj,
    tok_output,
    transition_in,
    transition_out,
    token_to_atom,
    pos_update,
):
    tok_rows, channels = tok_single.shape
    head_count = pair_weight.shape[1]
    head_size = channels // head_count
    filled = atom_token < tok_rows
    onehot = (jnp.arange(tok_rows)[:, None] == atom_token[None, :]).astype(jnp.bfloat16)
    atom_act = atom_cond.astype(jnp.float32)[None] + jnp.einsum(
        "sca,cw->saw", atom_pos, pos_weight, precision=lax.Precision.HIGHEST
    )
    atom_normed = layer_norm(atom_act).astype(jnp.bfloat16)
    atom_mixed = atom_window(atom_normed, atom_proj, filled)
    atom_mid = atom_act + jnp.einsum(
        "saw,wv->sav", atom_mixed, atom_output, preferred_element_type=jnp.float32
    )
    atom_feature = jax.nn.relu(
        jnp.einsum(
            "saw,wc->sac",
            atom_mid.astype(jnp.bfloat16),
            atom_to_token,
            preferred_element_type=jnp.float32,
        )
    ).astype(jnp.bfloat16)
    summed = jnp.einsum("ta,sac->stc", onehot, atom_feature, preferred_element_type=jnp.float32)
    members = jnp.sum(onehot.astype(jnp.float32), axis=1)
    token_in = summed / members[None, :, None]
    samples = token_in.shape[0]
    conditioning = jnp.dot(tok_single, ada_weight, preferred_element_type=jnp.float32)
    adapted = (layer_norm(token_in) * (1.0 + conditioning)[None]).astype(jnp.bfloat16)
    pair_normed = layer_norm(pair_rep.astype(jnp.float32)).astype(jnp.bfloat16)
    bias_part = jnp.einsum(
        "ijc,ch->hij", pair_normed, pair_weight, preferred_element_type=jnp.float32
    ).astype(jnp.bfloat16)
    bias = lax.all_gather(bias_part, "sample", axis=2, tiled=True)
    start_top = jnp.full((samples, head_count, tok_rows), -jnp.inf, jnp.float32)
    start_total = jnp.zeros((samples, head_count, tok_rows), jnp.float32)
    start_weighted = jnp.zeros((samples, head_count, tok_rows, head_size), jnp.float32)
    projected = jnp.einsum("stc,cf->stf", adapted, tok_proj, preferred_element_type=jnp.float32)
    queries = projected[..., :channels].astype(jnp.bfloat16)
    key_rows = projected[..., channels : 2 * channels].astype(jnp.bfloat16)
    val_rows = projected[..., 2 * channels : 3 * channels].astype(jnp.bfloat16)
    gating = jax.nn.sigmoid(projected[..., 3 * channels :])
    query_heads = queries.reshape(samples, tok_rows, head_count, head_size)
    row_top, row_total, weighted = attend_piece(
        query_heads,
        bias,
        (start_top, start_total, start_weighted),
        lax.all_gather(key_rows, "tok", axis=1, tiled=True),
        lax.all_gather(val_rows, "tok", axis=1, tiled=True),
    )
    attended = (
        (weighted / row_total[..., None]).transpose(0, 2, 1, 3).reshape(samples, tok_rows, channels)
    )
    gated_out = (gating * attended).astype(jnp.bfloat16)
    after_attn = token_in + jnp.einsum(
        "stc,cf->stf", gated_out, tok_output, preferred_element_type=jnp.float32
    )
    hidden_in = layer_norm(after_attn).astype(jnp.bfloat16)
    expanded = jnp.einsum(
        "stc,cf->stf", hidden_in, transition_in, preferred_element_type=jnp.float32
    )
    hidden_width = expanded.shape[-1] // 2
    hidden = (jax.nn.silu(expanded[..., :hidden_width]) * expanded[..., hidden_width:]).astype(
        jnp.bfloat16
    )
    token_out = (
        after_attn
        + jnp.einsum("stf,fc->stc", hidden, transition_out, preferred_element_type=jnp.float32)
    ).astype(jnp.bfloat16)
    tok_feature = jnp.einsum(
        "stc,cw->stw", token_out, token_to_atom, preferred_element_type=jnp.float32
    ).astype(jnp.bfloat16)
    atom_final = atom_mid + jnp.einsum(
        "ta,stw->saw", onehot, tok_feature, preferred_element_type=jnp.float32
    )
    update = jnp.einsum(
        "saw,wp->spa", layer_norm(atom_final), pos_update, precision=lax.Precision.HIGHEST
    )
    atom_update = update * filled.astype(jnp.float32)[None, None, :]
    return (token_out, atom_update)


def solution(mesh):
    return jax.shard_map(
        per_device,
        mesh=mesh,
        in_specs=(
            P("tok", None),
            P("sample", None, "tok"),
            P("tok"),
            P(),
            P(),
            P(),
            P(),
            P("tok", None),
            P(),
            P("tok", "sample", None),
            P(),
            P(),
            P(),
            P(),
            P(),
            P(),
            P(),
        ),
        out_specs=(P("sample", "tok", None), P("sample", None, "tok")),
        check_vma=False,
    )
```

profile of v0, /device:TPU:0, one launch (start us, length us, event | category | flops | bytes accessed | tf_op | source)
XLA Modules:
  0.0 479.7 jit_solution(739214911984075190)
XLA Ops:
  7.2 5.8 %convert_reduce_fusion = f32[64,512]{1,0:T(8,128)S(1)} fusion(bf16[64,512,128]{2,1,0:T(8,128)(2,1)} %param.27), kind=kLoop, calls=%fused_computation.10 | loop fusion | flops 8355840 | bytes 8519680 | tf_op jit(solution)/shard_map/reduce_sum | solution.py:17
  13.1 10.9 %fusion.7 = f32[64,512]{1,0:T(8,128)S(1)} fusion(bf16[64,512,128]{2,1,0:T(8,128)(2,1)} %param.27, f32[64,512]{1,0:T(8,128)S(1)} %broadcast_multiply_fusion), kind=kLoop, calls=%fused_computation.14 | loop fusion | flops 16744448 | bytes 8650752 | tf_op jit(solution)/shard_map/reduce_sum | solution.py:19
  24.1 12.5 %fusion.61 = bf16[16,64,512]{2,0,1:T(8,128)(2,1)} fusion(bf16[64,512,128]{2,1,0:T(8,128)(2,1)S(1)} %bitcast.108, f32[64,512]{1,0:T(8,128)S(1)} %add_rsqrt_fusion, f32[64,512]{1,0:T(8,128)S(1)} %broadcast_multiply_fusion, bf16[128,16]{0,1:T(8,128)(2,1)S(1)} %copy-done.18), kind=kOutput, calls=%fused_computation.65 | convolution fusion | flops 151519232 | bytes 9703424 | tf_op jit(solution)/shard_map/ijc,ch->hij/dot_general | solution.py:170
  51.2 8.0 %copy.38 = bf16[4,24,192,128]{2,3,1,0:T(8,128)(2,1)} copy(bf16[4,24,192,128]{3,2,1,0:T(8,128)(2,1)} %pad_maximum_fusion) | data formatting | bytes 9437184 | tf_op jit(solution)/shard_map/concatenate | solution.py:51
  61.9 5.1 %reshape.136 = bf16[4,24,64,4,32]{2,1,4,3,0:T(8,128)(2,1)} reshape(bf16[4,1536,128]{1,2,0:T(8,128)(2,1)} %copy.37) | data formatting | bytes 3145728 | tf_op jit(solution)/shard_map/reshape | solution.py:70
  72.4 8.0 %copy.40 = bf16[4,24,192,128]{2,3,1,0:T(8,128)(2,1)} copy(bf16[4,24,192,128]{3,2,1,0:T(8,128)(2,1)} %pad_maximum_fusion.1) | data formatting | bytes 9437184 | tf_op jit(solution)/shard_map/concatenate | solution.py:51
  80.5 14.3 %fusion.14 = (f32[4,24,4,64]{3,2,1,0:T(4,128)S(1)}, f32[4,24,4,64,192]{4,3,2,1,0:T(8,128)}) fusion(pred[24,192]{1,0:T(8,128)(4,1)S(1)} %pad_add_fusion, pred[24,64,192]{2,1,0:T(8,128)(4,1)S(1)} %copy.66, bf16[4,24,192,4,32]{2,4,3,1,0:T(8,128)(2,1)} %bitcast.111, bf16[4,24,64,4,32]{2,1,4,3,0:T(8,128)(2,1)} %reshape.136), kind=kOutput, calls=%fused_computation.20 | convolution fusion | flops 320839680 | bytes 25563648 | tf_op jit(solution)/shard_map/sgqhd,sgkhd->sghqk/dot_general | solution.py:73
  94.9 13.8 %fusion.3 = f32[4,24,4,64]{3,2,1,0:T(4,128)S(1)} fusion(f32[4,24,4,64,192]{4,3,2,1,0:T(8,128)} %get-tuple-element.25, f32[4,24,4,64]{3,2,1,0:T(4,128)S(1)} %get-tuple-element.24, pred[24,192]{1,0:T(8,128)(4,1)S(1)} %pad_add_fusion, pred[24,64,192]{2,1,0:T(8,128)(4,1)S(1)} %copy.66), kind=kLoop, calls=%fused_computation.7 | loop fusion | flops 23568384 | bytes 19370496 | tf_op jit(solution)/shard_map/reduce_sum | solution.py:80
  108.7 12.8 %fusion.27 = bf16[4,24,64,4,32]{2,4,3,1,0:T(8,128)(2,1)S(1)} fusion(f32[4,24,64,4]{2,3,1,0:T(4,128)S(1)} %bitcast.115, bf16[4,24,192,4,32]{2,4,3,1,0:T(8,128)(2,1)S(1)} %bitcast.112, f32[4,24,4,64,192]{4,3,2,1,0:T(8,128)} %get-tuple-element.25, f32[4,24,4,64]{3,2,1,0:T(4,128)S(1)} %get-tuple-element.24, pred[24,192]{1,0:T(8,128)(4,1)S(1)} %pad_add_fusion, ...), kind=kOutput, calls=%fused_computation.31 | convolution fusion | flops 327155712 | bytes 25661952 | tf_op jit(solution)/shard_map/sghqk,sgkhd->sghqd/dot_general | solution.py:82
  121.5 3.7 copy.41
  125.2 5.3 %convert_element_type.81 = bf16[4,1536,128]{1,2,0:T(8,128)(2,1)} reshape(bf16[4,24,64,4,32]{2,1,4,3,0:T(8,128)(2,1)} %copy.41) | data formatting | bytes 3145728 | tf_op jit(solution)/shard_map/convert_element_type | solution.py:93
  130.7 4.8 convolution_add_fusion.1
  135.4 7.0 %fusion.120 = (f32[4,64]{1,0:T(4,128)S(1)}, f32[4,64,768]{2,1,0:T(8,128)S(1)}) fusion(f32[64]{0:T(128)S(1)} %convert_reduce_fusion.1, s32[1536]{0:T(1024)S(1)} %copy-done.12, f32[4,1536,128]{1,2,0:T(8,128)} %convolution_add_fusion.1, bf16[128,768]{1,0:T(8,128)(2,1)S(1)} %copy-done.17), kind=kOutput, calls=%fused_computation.134 | convolution fusion | flops 1822654208 | bytes 4136192 | tf_op jit(solution)/shard_map/ta,sac->stc/dot_general | solution.py:163
  144.3 5.5 %fusion.125 = (bf16[4,64,3072]{2,1,0:T(8,128)(2,1)S(1)}, f32[4,64,3072]{2,1,0:T(8,128)}) fusion(bf16[768,3072]{1,0:T(8,128)(2,1)} %param.29, f32[4,64,768]{2,1,0:T(8,128)S(1)} %get-tuple-element.27, f32[64,768]{1,0:T(8,128)S(1)} %convolution_add_fusion.3, f32[4,64]{1,0:T(4,128)S(1)} %add_rsqrt_fusion.4, f32[4,64]{1,0:T(4,128)S(1)} %broadcast_multiply_fusion.4), kind=kOutput, calls=%fused_computation.135 | convolution fusion | flops 1209532416 | bytes 10422272 | tf_op jit(solution)/shard_map/stc,cf->stf/dot_general | solution.py:177
  152.0 7.8 %copy.46 = f32[16,64,2048]{2,1,0:T(8,128)} copy(bf16[16,64,2048]{2,0,1:T(8,128)(2,1)} %all-gather.6.cloned.1.call-done) | data formatting | bytes 12582912 | tf_op jit(solution)/shard_map/convert_element_type | solution.py:102
  159.8 124.1 %all-gather.4.cloned.1.call-done = bf16[4,2048,768]{2,1,0:T(8,128)(2,1)} async-done(((bf16[4,64,768]{2,1,0:T(8,128)(2,1)}), bf16[4,2048,768]{2,1,0:T(8,128)(2,1)}) %all-gather.4.cloned.1.call-update) | async-done | bytes 12582928 | tf_op jit(solution)/shard_map/all_gather | solution.py:187
  283.9 16.7 %copy.44 = bf16[4,2048,768]{1,2,0:T(8,128)(2,1)} copy(bf16[4,2048,768]{2,1,0:T(8,128)(2,1)} %all-gather.4.cloned.1.call-done) | data formatting | bytes 25165824 | tf_op jit(solution)/shard_map/all_gather | solution.py:187
  300.6 17.8 %fusion = (f32[4,16,64]{2,1,0:T(8,128)S(1)}, f32[4,16,64,2048]{3,2,1,0:T(8,128)}) fusion(f32[16,64,2048]{2,1,0:T(8,128)} %copy.46, bf16[4,64,16,48]{1,3,2,0:T(8,128)(2,1)S(1)} %bitcast.114, bf16[4,2048,16,48]{1,3,2,0:T(8,128)(2,1)} %bitcast.105), kind=kOutput, calls=%fused_computation.2 | convolution fusion | flops 830468096 | bytes 54935552 | tf_op jit(solution)/shard_map/sqhd,skhd->shqk/dot_general | solution.py:106
  318.4 16.0 %fusion.1 = f32[4,16,64]{2,1,0:T(8,128)S(1)} fusion(f32[4,16,64,2048]{3,2,1,0:T(8,128)} %get-tuple-element.31, f32[4,16,64]{2,1,0:T(8,128)S(1)} %get-tuple-element.30, f32[16,64,2048]{2,1,0:T(8,128)} %copy.46), kind=kLoop, calls=%fused_computation.3 | loop fusion | flops 33550336 | bytes 41975808 | tf_op jit(solution)/shard_map/reduce_sum | solution.py:113
  334.4 81.1 %all-gather.8.cloned.1.call-done = bf16[4,2048,768]{2,1,0:T(8,128)(2,1)} async-done(((bf16[4,64,768]{2,1,0:T(8,128)(2,1)}), bf16[4,2048,768]{2,1,0:T(8,128)(2,1)}) %all-gather.8.cloned.1.call-update) | async-done | bytes 12582928 | tf_op jit(solution)/shard_map/all_gather | solution.py:188
  415.5 16.7 %copy.47 = bf16[4,2048,768]{1,2,0:T(8,128)(2,1)} copy(bf16[4,2048,768]{2,1,0:T(8,128)(2,1)} %all-gather.8.cloned.1.call-done) | data formatting | bytes 25165824 | tf_op jit(solution)/shard_map/all_gather | solution.py:188
  432.2 20.6 %fusion.49 = f32[4,64,16,48]{1,3,2,0:T(8,128)} fusion(bf16[4,2048,16,48]{1,3,2,0:T(8,128)(2,1)} %bitcast.106, f32[4,16,64,2048]{3,2,1,0:T(8,128)} %get-tuple-element.31, f32[4,16,64]{2,1,0:T(8,128)S(1)} %get-tuple-element.30, f32[16,64,2048]{2,1,0:T(8,128)} %copy.46, f32[4,64,16]{1,2,0:T(8,128)S(1)} %bitcast_add_fusion.1, ...), kind=kOutput, calls=%fused_computation.58 | convolution fusion | flops 839254016 | bytes 55361536 | tf_op jit(solution)/shard_map/shqk,skhd->shqd/dot_general | solution.py:114
  458.2 3.8 fusion.28
  463.1 4.5 fusion.127
  (93 shorter events, 38.9 us)
Async XLA Ops:
  7.2 454.8 %copy-start = (bf16[1536,768]{1,0:T(8,128)(2,1)S(1)}, bf16[1536,768]{1,0:T(8,128)(2,1)}, u32[]{:S(2)}) copy-start(bf16[1536,768]{1,0:T(8,128)(2,1)} %param.32) | copy-start | bytes 7077892
  7.2 144.8 %all-gather.6.cloned.1.call-start = ((), (), s32[]{:S(2)}) async-start(), calls=%async_computation.1 | async-start | bytes 5242880 | tf_op jit(solution)/shard_map/all_gather | solution.py:173
  7.2 16.8 %slice-start = ((s8[8388608]{0:T(1024)(128)(4,1)}), s8[4194304]{0:T(1024)(128)(4,1)S(1)}, s32[]{:S(2)}) async-start(s8[8388608]{0:T(1024)(128)(4,1)} %bitcast.107), calls=%async_computation.3 | async-start | bytes 8388608
  13.0 11.0 %copy-start.18 = (bf16[128,16]{0,1:T(8,128)(2,1)S(1)}, bf16[128,16]{0,1:T(8,128)(2,1)}, u32[]{:S(2)}) copy-start(bf16[128,16]{0,1:T(8,128)(2,1)} %param.28) | copy-start | bytes 12292
  13.1 11.0 %slice-start.1 = ((s8[8388608]{0:T(1024)(128)(4,1)}), s8[4194304]{0:T(1024)(128)(4,1)S(1)}, s32[]{:S(2)}) async-start(s8[8388608]{0:T(1024)(128)(4,1)} %bitcast.107), calls=%async_computation.4 | async-start | bytes 8388608
  24.0 12.6 %copy-start.12 = (s32[1536]{0:T(1024)S(1)}, s32[1536]{0:T(1024)}, u32[]{:S(2)}) copy-start(s32[1536]{0:T(1024)} %param.20) | copy-start | bytes 18436
  24.1 14.5 %copy-start.9 = (f32[4,3,1536]{2,0,1:T(4,128)S(1)}, f32[4,3,1536]{2,0,1:T(4,128)}, u32[]{:S(2)}) copy-start(f32[4,3,1536]{2,0,1:T(4,128)} %param.19) | copy-start | bytes 221188
  24.1 14.5 %copy-start.15 = (f32[3,128]{1,0:T(4,128)S(1)}, f32[3,128]{1,0:T(4,128)}, u32[]{:S(2)}) copy-start(f32[3,128]{1,0:T(4,128)} %param.21) | copy-start | bytes 4612
  36.5 6.8 %copy-start.10 = (bf16[128,384]{1,0:T(8,128)(2,1)S(1)}, bf16[128,384]{1,0:T(8,128)(2,1)}, u32[]{:S(2)}) copy-start(bf16[128,384]{1,0:T(8,128)(2,1)} %param.22) | copy-start | bytes 294916
  36.6 247.3 %all-gather.4.cloned.1.call-start = ((), (), s32[]{:S(2)}) async-start(), calls=%async_computation | async-start | bytes 12976128 | tf_op jit(solution)/shard_map/all_gather | solution.py:187
  41.7 1.6 copy-start.1
  59.2 7.9 %copy-start.6 = (pred[24,64,192]{2,1,0:T(32,128)(4,1)S(1)}, pred[24,64,192]{2,1,0:T(32,128)(4,1)}, u32[]{:S(2)}) copy-start(pred[24,64,192]{2,1,0:T(32,128)(4,1)} %constant.50.clone) | copy-start | bytes 884740
  94.9 13.9 %copy-start.3 = (bf16[4,24,192,128]{2,3,1,0:T(8,128)(2,1)S(1)}, bf16[4,24,192,128]{2,3,1,0:T(8,128)(2,1)}, u32[]{:S(2)}) copy-start(bf16[4,24,192,128]{2,3,1,0:T(8,128)(2,1)} %copy.40) | copy-start | bytes 14155780
  121.5 9.2 %copy-start.13 = (bf16[128,128]{1,0:T(8,128)(2,1)S(1)}, bf16[128,128]{1,0:T(8,128)(2,1)}, u32[]{:S(2)}) copy-start(bf16[128,128]{1,0:T(8,128)(2,1)} %param.23) | copy-start | bytes 98308
  130.5 4.9 %copy-start.17 = (bf16[128,768]{1,0:T(8,128)(2,1)S(1)}, bf16[128,768]{1,0:T(8,128)(2,1)}, u32[]{:S(2)}) copy-start(bf16[128,768]{1,0:T(8,128)(2,1)} %param.24) | copy-start | bytes 589828
  135.4 7.2 %copy-start.11 = (bf16[64,768]{1,0:T(8,128)(2,1)S(1)}, bf16[64,768]{1,0:T(8,128)(2,1)}, u32[]{:S(2)}) copy-start(bf16[64,768]{1,0:T(8,128)(2,1)} %param.25) | copy-start | bytes 294916
  142.4 7.4 %copy-start.4 = (f32[4,64,768]{2,1,0:T(8,128)}, f32[4,64,768]{2,1,0:T(8,128)S(1)}, u32[]{:S(2)}) copy-start(f32[4,64,768]{2,1,0:T(8,128)S(1)} %get-tuple-element.27) | copy-start | bytes 2359300
  150.9 264.6 %all-gather.8.cloned.1.call-start = ((), (), s32[]{:S(2)}) async-start(), calls=%async_computation.2 | async-start | bytes 12976128 | tf_op jit(solution)/shard_map/all_gather | solution.py:188
  432.2 23.4 %copy-start.5 = (f32[4,64,768]{2,1,0:T(8,128)S(1)}, f32[4,64,768]{2,1,0:T(8,128)}, u32[]{:S(2)}) copy-start(f32[4,64,768]{2,1,0:T(8,128)} %copy-done.4) | copy-start | bytes 2359300
  462.0 1.1 copy-start.8
  463.0 7.0 %copy-start.7 = (bf16[4,64,768]{2,1,0:T(8,128)(2,1)}, bf16[4,64,768]{2,1,0:T(8,128)(2,1)S(1)}, u32[]{:S(2)}) copy-start(bf16[4,64,768]{2,1,0:T(8,128)(2,1)S(1)} %fusion.67) | copy-start | bytes 1179652
  463.0 7.0 %copy-start.14 = (f32[1536]{0:T(1024)S(1)}, f32[1536]{0:T(1024)}, u32[]{:S(2)}) copy-start(f32[1536]{0:T(1024)} %get-tuple-element.6) | copy-start | bytes 18436
  463.1 7.0 %copy-start.16 = (f32[128,3]{0,1:T(4,128)S(1)}, f32[128,3]{0,1:T(4,128)}, u32[]{:S(2)}) copy-start(f32[128,3]{0,1:T(4,128)} %param.34) | copy-start | bytes 4612
  467.6 2.8 copy-start.2
Sparse Core Ops, SparseCore 0:
  36.7 48.4 all-gather.5
  151.0 132.8 all-gather.3
  287.1 128.3 all-gather.7
where the time goes:
time: 489 us; the launch traced here: 480 us
  waiting for transfers between devices  205 us (42%)
  matrix products  115 us (24%)
  local copies, waits for them, and re-layouts  88.6 us (18%)
  other arithmetic  55.6 us (11%)
  between operations  14.4 us (3%)
    all_gather x1, waiting for transfers between devices, per_device(): lax.all_gather(key_rows, 'tok', axis=1, tiled=True)  124 us
    all_gather x1, waiting for transfers between devices, per_device(): lax.all_gather(val_rows, 'tok', axis=1, tiled=True)  81.1 us
    dot_general x1, matrix products, attend_piece(): jnp.einsum('shqk,skhd->shqd', weights.astype(jnp.bfloat16), val_heads, pr...  20.6 us
    dot_general x1, matrix products, attend_piece(): jnp.einsum('sqhd,skhd->shqk', query_heads, key_heads, preferred_element_t...  17.8 us
    all_gather x1, local copies, waits for them, and re-layouts, per_device(): lax.all_gather(val_rows, 'tok', axis=1, tiled=True)  16.7 us
    all_gather x1, local copies, waits for them, and re-layouts, per_device(): lax.all_gather(key_rows, 'tok', axis=1, tiled=True)  16.7 us
    concatenate x2, local copies, waits for them, and re-layouts, span_blocks(): return jnp.concatenate([first, second, third], axis=axis + 1)  16 us
    reduce_sum x1, other arithmetic, attend_piece(): new_total = row_total * factor + jnp.sum(weights, axis=-1)  16 us
  transfers between devices with their start and end apart: 3, of which 2 were waited for; matrix products, arithmetic and copies ran while one was open for 36% of the time, Pallas kernels for 0%

commit v1 on v0

v1 whole, which is shorter than its diff:
```python
import functools

import jax
import jax.numpy as jnp
import numpy as np
from jax import lax
from jax.experimental import pallas as pl
from jax.experimental.pallas import tpu as pltpu
from jax.sharding import Mesh, PartitionSpec as P

ATOM_HEADS = 4
QUERY_BLOCK = 32
KEY_WINDOW = 128
NORM_EPSILON = 1e-05
MASKED_SCORE = -1000000000.0
LOG2E = 1.4426950408889634
F32 = jnp.float32
BF16 = jnp.bfloat16
VMEM_LIMIT = 50 * 1024 * 1024

TN = (((0,), (0,)), ((), ()))
NT = (((1,), (1,)), ((), ()))
NN = (((1,), (0,)), ((), ()))


def mm(a, b, dims=NN):
    return lax.dot_general(a, b, dims, preferred_element_type=F32)


def norm_rows(inputs):
    row_mean = jnp.mean(inputs, axis=-1, keepdims=True)
    centered = inputs - row_mean
    variance = jnp.mean(centered * centered, axis=-1, keepdims=True)
    return centered * lax.rsqrt(variance + NORM_EPSILON)


def params():
    return pltpu.CompilerParams(vmem_limit_bytes=VMEM_LIMIT)


def pair_kernel(pair_ref, center_ref, weight_ref, out_ref):
    rows, cols, width = pair_ref.shape
    heads = weight_ref.shape[0]
    ones = jnp.full((heads, width), 1.0 / width, BF16)
    flat = pair_ref[...].reshape(rows * cols, width)
    centered = mm(flat, center_ref[...])
    top = mm(weight_ref[...], centered.astype(BF16), NT)
    variance = mm(ones, (centered * centered).astype(BF16), NT)
    bias = top * (lax.rsqrt(variance + NORM_EPSILON) * LOG2E)
    for h in range(heads):
        out_ref[h] = bias[h : h + 1].reshape(rows, cols).astype(BF16)


def pair_bias(pair_rep, pair_weight):
    rows, cols, width = pair_rep.shape
    heads = pair_weight.shape[1]
    step = 16
    center = jnp.asarray(np.eye(width) - 1.0 / width, BF16)
    return pl.pallas_call(
        pair_kernel,
        grid=(rows // step,),
        in_specs=[
            pl.BlockSpec((step, cols, width), lambda i: (i, 0, 0)),
            pl.BlockSpec((width, width), lambda i: (0, 0)),
            pl.BlockSpec((heads, width), lambda i: (0, 0)),
        ],
        out_specs=pl.BlockSpec((heads, step, cols), lambda i: (0, i, 0)),
        out_shape=jax.ShapeDtypeStruct((heads, rows, cols), BF16),
        compiler_params=params(),
        cost_estimate=pl.CostEstimate(
            flops=2 * rows * cols * width * (width + 2 * heads),
            bytes_accessed=2 * rows * cols * (width + heads),
            transcendentals=0,
        ),
        name="pair_bias",
    )(pair_rep, center, pair_weight.T)


def atom_kernel(
    cond_ref, pos_ref, token_ref, pos_weight_ref, proj_ref, output_ref, to_token_ref,
    mid_ref, token_in_ref, query_s, key_s, val_s, mixed_s,
):
    slots, width = cond_ref.shape
    tokens = token_in_ref.shape[1]
    head = width // ATOM_HEADS
    owner = token_ref[...]
    count = jnp.sum((owner < tokens).astype(jnp.int32))
    act = cond_ref[...].astype(F32) + lax.dot_general(
        pos_ref[0], pos_weight_ref[...], TN, precision=lax.Precision.HIGHEST, preferred_element_type=F32
    )
    normed = norm_rows(act).astype(BF16)
    projected = mm(normed, proj_ref[...])
    query_s[...] = (projected[:, :width] * (head ** (-0.5) * LOG2E)).astype(BF16)
    key_s[...] = projected[:, width : 2 * width].astype(BF16)
    val_s[:, :width] = projected[:, 2 * width :].astype(BF16)
    val_s[:, width:] = jnp.ones((slots, width), BF16)
    stacked = ATOM_HEADS * QUERY_BLOCK
    of_row = lax.broadcasted_iota(jnp.int32, (stacked, width), 0) // QUERY_BLOCK
    of_lane = lax.broadcasted_iota(jnp.int32, (stacked, width), 1) // head
    own_head = of_row == of_lane
    lane = lax.broadcasted_iota(jnp.int32, (stacked, KEY_WINDOW), 1)
    blocks = slots // QUERY_BLOCK
    group = 8
    for first in range(0, blocks, group):
        starts = [
            min(max(b * QUERY_BLOCK - (KEY_WINDOW - QUERY_BLOCK) // 2, 0), slots - KEY_WINDOW)
            for b in range(first, first + group)
        ]
        scores = []
        for k, start in enumerate(starts):
            low = (first + k) * QUERY_BLOCK
            query = query_s[low : low + QUERY_BLOCK, :]
            query = jnp.concatenate([query] * ATOM_HEADS, axis=0)
            query = jnp.where(own_head, query, jnp.zeros_like(query))
            score = mm(query, key_s[start : start + KEY_WINDOW, :], NT)
            scores.append(jnp.where(lane < count - start, score, MASKED_SCORE))
        weights = [jnp.exp2(s - jnp.max(s, axis=-1, keepdims=True)).astype(BF16) for s in scores]
        for k, start in enumerate(starts):
            low = (first + k) * QUERY_BLOCK
            summed = mm(weights[k], val_s[start : start + KEY_WINDOW, :])
            mixed = jnp.where(own_head, summed[:, :width] / summed[:, width:], 0.0)
            mixed = mixed.reshape(ATOM_HEADS, QUERY_BLOCK, width).sum(axis=0)
            mixed_s[low : low + QUERY_BLOCK, :] = mixed.astype(BF16)
    mid = act + mm(mixed_s[...], output_ref[...])
    mid_ref[0] = mid
    feature = jnp.maximum(mm(mid.astype(BF16), to_token_ref[...]), 0.0).astype(BF16)
    onehot = lax.broadcasted_iota(jnp.int32, (tokens, slots), 0) == owner
    members = jnp.sum(onehot.astype(F32), axis=1, keepdims=True)
    token_in_ref[0] = mm(onehot.astype(BF16), feature) / members


def atom_stage(atom_cond, atom_pos, atom_token, pos_weight, atom_proj, atom_output, atom_to_token, tokens):
    samples = atom_pos.shape[0]
    slots, width = atom_cond.shape
    channels = atom_to_token.shape[1]
    whole = lambda a: pl.BlockSpec(a.shape, lambda s: (0,) * a.ndim)
    atom_token = atom_token.reshape(1, slots)
    return pl.pallas_call(
        atom_kernel,
        grid=(samples,),
        in_specs=[
            whole(atom_cond),
            pl.BlockSpec((1, 3, slots), lambda s: (s, 0, 0)),
            whole(atom_token),
            whole(pos_weight),
            whole(atom_proj),
            whole(atom_output),
            whole(atom_to_token),
        ],
        out_specs=[
            pl.BlockSpec((1, slots, width), lambda s: (s, 0, 0)),
            pl.BlockSpec((1, tokens, channels), lambda s: (s, 0, 0)),
        ],
        out_shape=[
            jax.ShapeDtypeStruct((samples, slots, width), F32),
            jax.ShapeDtypeStruct((samples, tokens, channels), F32),
        ],
        scratch_shapes=[
            pltpu.VMEM((slots, width), BF16),
            pltpu.VMEM((slots, width), BF16),
            pltpu.VMEM((slots, 2 * width), BF16),
            pltpu.VMEM((slots, width), BF16),
        ],
        compiler_params=params(),
        cost_estimate=pl.CostEstimate(flops=20 * 10**9, bytes_accessed=10**7, transcendentals=10**7),
        name="atom_stage",
    )(atom_cond, atom_pos, atom_token, pos_weight, atom_proj, atom_output, atom_to_token)


def project_kernel(token_in_ref, single_ref, ada_ref, proj_ref, heads_ref, gate_ref):
    samples, tokens, channels = token_in_ref.shape
    heads, _, lanes = heads_ref.shape
    head = channels // heads
    conditioning = 1.0 + mm(single_ref[...], ada_ref[...])
    adapted = (norm_rows(token_in_ref[...]) * conditioning[None]).astype(BF16).reshape(lanes, channels)
    for part in range(3):
        rows = mm(adapted, proj_ref[:, part * channels : (part + 1) * channels])
        if part == 0:
            rows = rows * (head ** (-0.5) * LOG2E)
        turned = rows.T.astype(BF16).reshape(heads, head, lanes)
        heads_ref[:, part * head : (part + 1) * head, :] = turned
    gate = mm(adapted, proj_ref[:, 3 * channels :])
    gate_ref[...] = jax.nn.sigmoid(gate)


def project(token_in, tok_single, ada_weight, tok_proj, heads):
    samples, tokens, channels = token_in.shape
    lanes = samples * tokens
    head = channels // heads
    return pl.pallas_call(
        project_kernel,
        out_shape=[
            jax.ShapeDtypeStruct((heads, 3 * head, lanes), BF16),
            jax.ShapeDtypeStruct((lanes, channels), F32),
        ],
        compiler_params=params(),
        cost_estimate=pl.CostEstimate(
            flops=2 * lanes * channels * 4 * channels, bytes_accessed=8 * 10**6, transcendentals=lanes * channels
        ),
        name="project",
    )(token_in, tok_single, ada_weight, tok_proj)


def attend_kernel(
    order_ref, own_ref, far_ref, bias0_ref, bias1_ref, bias2_ref, bias3_ref, out_ref, query_s, key_s, val_s
):
    peers, head, lanes = out_ref.shape[0], out_ref.shape[1], out_ref.shape[2]
    samples = query_s.shape[0]
    tokens = lanes // samples
    width = query_s.shape[2]
    sources = own_ref.shape[0]
    half = sources * tokens
    step = pl.program_id(0)
    mine = order_ref[0]
    x_hi = order_ref[1]

    @pl.when(step == 0)
    def _():
        fill = jnp.zeros((width - head, lanes), F32)
        fill_v = jnp.where(lax.broadcasted_iota(jnp.int32, (width - head, lanes), 0) == 0, 1.0, 0.0)

        def turn(block, below):
            return jnp.concatenate([block.astype(F32), below], axis=0).T.astype(BF16)

        for j in range(sources):
            query = turn(own_ref[j, :head, :], fill)
            for s in range(samples):
                query_s[s, j * tokens : (j + 1) * tokens, :] = query[s * tokens : (s + 1) * tokens]
            for ref, low, which in ((own_ref, head, x_hi), (far_ref, 0, 1 - x_hi)):
                key = turn(ref[j, low : low + head, :], fill)
                val = turn(ref[j, low + head : low + 2 * head, :], fill_v)
                place = pl.ds(pl.multiple_of(which * half + j * tokens, tokens), tokens)
                for s in range(samples):
                    key_s[s, place, :] = key[s * tokens : (s + 1) * tokens]
                    val_s[s, place, :] = val[s * tokens : (s + 1) * tokens]

    rows = peers * tokens
    results = []
    for s in range(samples):
        query = query_s[s, pl.ds(pl.multiple_of(step * rows, rows), rows), :]
        scores = []
        places = []
        for p, bias_ref in enumerate((bias0_ref, bias1_ref, bias2_ref, bias3_ref)):
            cols = bias_ref.shape[1]
            place = pl.ds(pl.multiple_of((mine ^ p) * cols, cols), cols)
            places.append(place)
            scores.append(mm(query, key_s[s, place, :], NT) + bias_ref[...].astype(F32))
        top = functools.reduce(jnp.maximum, [jnp.max(x, axis=-1, keepdims=True) for x in scores])
        total = 0.0
        for x, place in zip(scores, places):
            total = total + mm(jnp.exp2(x - top).astype(BF16), val_s[s, place, :])
        results.append(total / total[:, head : head + 1])
    for j in range(peers):
        block = jnp.concatenate([r[j * tokens : (j + 1) * tokens] for r in results], axis=0)
        out_ref[j] = block.T[:head].astype(BF16)


def attend(order, own, far, biases, samples, head):
    sources, _, lanes = own.shape
    tokens = lanes // samples
    width = 128
    peers = 4
    rows = peers * tokens
    total = sources * tokens
    cols = biases[0].shape[1]
    whole = lambda a: pl.BlockSpec(a.shape, lambda i, *_: (0,) * a.ndim)
    return pl.pallas_call(
        attend_kernel,
        grid_spec=pltpu.PrefetchScalarGridSpec(
            num_scalar_prefetch=1,
            grid=(sources // peers,),
            in_specs=[whole(own), whole(far)] + [pl.BlockSpec((rows, cols), lambda i, *_: (i, 0))] * 4,
            out_specs=pl.BlockSpec((peers, head, lanes), lambda i, *_: (i, 0, 0)),
            scratch_shapes=[
                pltpu.VMEM((samples, total, width), BF16),
                pltpu.VMEM((samples, 2 * total, width), BF16),
                pltpu.VMEM((samples, 2 * total, width), BF16),
            ],
        ),
        out_shape=jax.ShapeDtypeStruct((sources, head, lanes), BF16),
        compiler_params=params(),
        cost_estimate=pl.CostEstimate(flops=10**10, bytes_accessed=8 * 10**6, transcendentals=10**7),
        name="attend",
    )(order, own, far, *biases)


def finish_kernel(
    heads_ref, gate_ref, token_in_ref, output_ref, trans_in_ref, trans_out_ref, to_atom_ref, mid_ref, token_ref,
    update_ref, token_out_ref, atom_ref, feature_s,
):
    samples, tokens, channels = token_in_ref.shape
    lanes = samples * tokens
    step = pl.program_id(0)

    @pl.when(step == 0)
    def _():
        attended = heads_ref[...].reshape(channels, lanes).astype(F32).T
        gated = (gate_ref[...] * attended).astype(BF16)
        after = token_in_ref[...].reshape(lanes, channels) + mm(gated, output_ref[...])
        hidden_in = norm_rows(after).astype(BF16)
        hidden_width = trans_out_ref.shape[0]
        left = mm(hidden_in, trans_in_ref[:, :hidden_width])
        right = mm(hidden_in, trans_in_ref[:, hidden_width:])
        hidden = (jax.nn.silu(left) * right).astype(BF16)
        result = (after + mm(hidden, trans_out_ref[...])).astype(BF16)
        token_out_ref[...] = result.reshape(samples, tokens, channels)
        feature_s[...] = mm(result, to_atom_ref[...]).astype(BF16).reshape(feature_s.shape)

    owner = token_ref[...]
    slots = owner.shape[1]
    onehot = (lax.broadcasted_iota(jnp.int32, (tokens, slots), 0) == owner).astype(BF16)
    final = mid_ref[0] + mm(onehot, feature_s[step], TN)
    update = lax.dot_general(
        update_ref[...], norm_rows(final), NT, precision=lax.Precision.HIGHEST, preferred_element_type=F32
    )
    atom_ref[0] = update[:3] * (owner < tokens).astype(F32)


def finish(heads, gate, token_in, tok_output, transition_in, transition_out, token_to_atom, atom_mid, atom_token, pos_update):
    samples, tokens, channels = token_in.shape
    slots, width = atom_mid.shape[1:]
    atom_token = atom_token.reshape(1, slots)
    turned = jnp.pad(pos_update.T, ((0, 5), (0, 0)))
    whole = lambda a: pl.BlockSpec(a.shape, lambda s: (0,) * a.ndim)
    args = (heads, gate, token_in, tok_output, transition_in, transition_out, token_to_atom)
    return pl.pallas_call(
        finish_kernel,
        grid=(samples,),
        in_specs=[whole(a) for a in args]
        + [pl.BlockSpec((1, slots, width), lambda s: (s, 0, 0)), whole(atom_token), whole(turned)],
        out_specs=[
            pl.BlockSpec((samples, tokens, channels), lambda s: (0, 0, 0)),
            pl.BlockSpec((1, 3, slots), lambda s: (s, 0, 0)),
        ],
        out_shape=[
            jax.ShapeDtypeStruct((samples, tokens, channels), BF16),
            jax.ShapeDtypeStruct((samples, 3, slots), F32),
        ],
        scratch_shapes=[pltpu.VMEM((samples, tokens, width), BF16)],
        compiler_params=params(),
        cost_estimate=pl.CostEstimate(flops=3 * 10**9, bytes_accessed=15 * 10**6, transcendentals=10**6),
        name="finish",
    )(*args, atom_mid, atom_token, turned)


def swap(x, axis):
    return lax.ppermute(x, axis, [(0, 1), (1, 0)])


def per_device(
    atom_cond, atom_pos, atom_token, pos_weight, atom_proj, atom_output, atom_to_token, tok_single, ada_weight,
    pair_rep, pair_weight, tok_proj, tok_output, transition_in, transition_out, token_to_atom, pos_update,
):
    tokens, channels = tok_single.shape
    heads = pair_weight.shape[1]
    head = channels // heads
    samples = atom_pos.shape[0]
    bias = pair_bias(pair_rep, pair_weight)
    bias = lax.all_to_all(bias, ("y", "z"), 0, 0, tiled=True)
    bias = bias.reshape(heads * tokens, bias.shape[2])
    across = swap(bias, "xlo")
    bias = (bias, swap(bias, "core"), across, swap(across, "core"))
    atom_mid, token_in = atom_stage(
        atom_cond, atom_pos, atom_token, pos_weight, atom_proj, atom_output, atom_to_token, tokens
    )
    qkv, gate = project(token_in, tok_single, ada_weight, tok_proj, heads)
    own = lax.all_to_all(qkv, ("y", "z"), 0, 0, tiled=True)
    far = swap(own[:, head:], "xhi")
    order = jnp.stack([lax.axis_index("xlo") * 2 + lax.axis_index("core"), lax.axis_index("xhi")]).astype(jnp.int32)
    attended = attend(order, own, far, bias, samples, head)
    attended = lax.all_to_all(attended, ("y", "z"), 0, 0, tiled=True)
    return finish(
        attended, gate, token_in, tok_output, transition_in, transition_out, token_to_atom, atom_mid, atom_token,
        pos_update,
    )


def solution(mesh):
    fine = Mesh(mesh.devices.reshape(2, 2, 2, 4, 4), ("xlo", "core", "xhi", "y", "z"))
    tok = ("xhi", "y", "z")
    sample = ("xlo", "core")
    return jax.shard_map(
        per_device,
        mesh=fine,
        in_specs=(
            P(tok, None), P(sample, None, tok), P(tok), P(), P(), P(), P(), P(tok, None), P(),
            P(tok, sample, None), P(), P(), P(), P(), P(), P(), P(),
        ),
        out_specs=(P(sample, tok, None), P(sample, None, tok)),
        check_vma=False,
    )
```

time: 489 us -> 156 us (0.32); the launches traced: 480 us -> 155 us
  waiting for transfers between devices: 205 us -> 57.5 us
  matrix products: 115 us -> 0 us
  local copies, waits for them, and re-layouts: 88.6 us -> 5.39 us
  Pallas kernels: 0 us -> 68.8 us
  other arithmetic: 55.6 us -> 0.07 us
  starting transfers between devices: 0.53 us -> 22.5 us
  between operations: 14.4 us -> 0.81 us
    all_gather x3 -> x0, waiting for transfers between devices: 205 us -> none  [the longest x1 124 us: per_device(): lax.all_gather(key_rows, 'tok', axis=1, tiled=True)]
    dot_general x16 -> x0, matrix products: 115 us -> none  [the longest x1 20.6 us: attend_piece(): jnp.einsum('shqk,skhd->shqd', weights.astype(jnp.bfloat16), val_heads, pr...]
    pallas_call x0 -> x5, Pallas kernels: none -> 68.8 us  [the longest x1 24.7 us: atom_stage(): pl.pallas_call(atom_kernel, grid=(samples,), in_specs=[whole(atom_cond),...]
    reduce_sum x9 -> x0, other arithmetic: 49.9 us -> none  [the longest x1 16 us: attend_piece(): new_total = row_total * factor + jnp.sum(weights, axis=-1)]
    all_to_all x0 -> x3, waiting for transfers between devices: none -> 42.5 us  [the longest x1 17.6 us: per_device(): bias = lax.all_to_all(bias, ('y', 'z'), 0, 0, tiled=True)]
    all_gather x2 -> x0, local copies, waits for them, and re-layouts: 33.4 us -> none  [the longest x1 16.7 us: per_device(): lax.all_gather(val_rows, 'tok', axis=1, tiled=True)]
    convert_element_type x4 -> x0, local copies, waits for them, and re-layouts: 18 us -> none  [the longest x2 9.03 us: atom_window(): return weighted.transpose(0, 1, 3, 2, 4).reshape(samples, slot_count, cha...]
    all_to_all x0 -> x3, starting transfers between devices: none -> 17.7 us  [the longest x1 8.13 us: per_device(): bias = lax.all_to_all(bias, ('y', 'z'), 0, 0, tiled=True)]
  transfers between devices with their start and end apart: 3 -> 7, of which waited for: 2 -> 4; matrix products, arithmetic and copies ran while one was open for 36% -> 1% of each run, Pallas kernels for 0% -> 19%
where the time goes in v1:
time: 156 us; the launch traced here: 155 us
  Pallas kernels  68.8 us (44%)
  waiting for transfers between devices  57.5 us (37%)
  starting transfers between devices  22.5 us (14%)
  local copies, waits for them, and re-layouts  5.39 us (3%)
    pallas_call x1, Pallas kernels, atom_stage(): pl.pallas_call(atom_kernel, grid=(samples,), in_specs=[whole(atom_cond),...  24.7 us
    pallas_call x1, Pallas kernels, attend(): pl.pallas_call(attend_kernel, grid_spec=pltpu.PrefetchScalarGridSpec(num_...  17.7 us
    all_to_all x1, waiting for transfers between devices, per_device(): bias = lax.all_to_all(bias, ('y', 'z'), 0, 0, tiled=True)  17.6 us
    all_to_all x1, waiting for transfers between devices, per_device(): own = lax.all_to_all(qkv, ('y', 'z'), 0, 0, tiled=True)  15.7 us
    ppermute x4, waiting for transfers between devices, swap(): return lax.ppermute(x, axis, [(0, 1), (1, 0)])  15 us
    pallas_call x1, Pallas kernels, finish(): pl.pallas_call(finish_kernel, grid=(samples,), in_specs=[whole(a) for a i...  11.1 us
    pallas_call x1, Pallas kernels, pair_bias(): pl.pallas_call(pair_kernel, grid=(rows // step,), in_specs=[pl.BlockSpec(...  10.3 us
    all_to_all x1, waiting for transfers between devices, per_device(): attended = lax.all_to_all(attended, ('y', 'z'), 0, 0, tiled=True)  9.11 us
  transfers between devices with their start and end apart: 7, of which 4 were waited for; matrix products, arithmetic and copies ran while one was open for 1% of the time, Pallas kernels for 19%

profile of v1, /device:TPU:0, one launch (start us, length us, event | category | flops | bytes accessed | tf_op | source)
XLA Modules:
  0.0 155.0 jit_solution(18257316431245178982)
XLA Ops:
  0.6 0.0 copy-start.6
  0.6 0.7 copy-done.6
  1.4 0.7 copy-done.7
  2.1 10.3 %pair_bias.1 = bf16[16,64,512]{2,1,0:T(8,128)(2,1)} custom-call(bf16[64,512,128]{2,1,0:T(8,128)(2,1)} %pair_ref.1, bf16[128,128]{1,0:T(8,128)(2,1)S(1)} %copy-done.6, bf16[16,128]{1,0:T(8,128)(2,1)S(1)} %bitcast.8), custom_call_target="tpu_custom_call" | custom-call | flops 1342177280 | bytes 9437184 | tf_op jit(solution)/shard_map/pair_bias/pallas_call | solution.py:59
  12.5 8.1 %all-to-all-start.1 = ((bf16[16,64,512]{2,1,0:T(8,128)(2,1)}), bf16[16,64,512]{2,1,0:T(8,128)(2,1)S(1)}, u32[]{:S(2)}, u32[]{:S(2)}) async-start(bf16[16,64,512]{2,1,0:T(8,128)(2,1)} %pair_bias.1), calls=%async_computation.1 | async-start | bytes 2097152 | tf_op jit(solution)/shard_map/all_to_all | solution.py:359
  20.7 17.6 %all-to-all-done.1 = bf16[16,64,512]{2,1,0:T(8,128)(2,1)S(1)} async-done(((bf16[16,64,512]{2,1,0:T(8,128)(2,1)}), bf16[16,64,512]{2,1,0:T(8,128)(2,1)S(1)}, u32[]{:S(2)}, u32[]{:S(2)}) %all-to-all-start.1) | async-done | bytes 1048608 | tf_op jit(solution)/shard_map/all_to_all | solution.py:359
  38.3 1.5 collective-permute-start.2
  39.8 24.7 %atom_stage.1 = (f32[4,1536,128]{2,1,0:T(8,128)}, f32[4,64,768]{2,1,0:T(8,128)S(1)}) custom-call(bf16[1536,128]{1,0:T(8,128)(2,1)S(1)} %copy-done.8, f32[4,3,1536]{2,1,0:T(4,128)S(1)} %copy.20.pos_ref, s32[1,1536]{1,0:T(1,128)S(1)} %reshape.11.token_ref, f32[3,128]{1,0:T(4,128)S(1)} %copy-done.12, bf16[128,384]{1,0:T(8,128)(2,1)S(1)} %copy-done.10, ...), custom_call_target="tpu_custom_call" | custom-call | flops 20000000000 | bytes 10000000 | tf_op jit(solution)/shard_map/atom_stage/pallas_call | solution.py:138
  64.5 5.0 %project.1 = (bf16[16,144,256]{2,1,0:T(8,128)(2,1)}, f32[256,768]{1,0:T(8,128)S(1)}) custom-call(f32[4,64,768]{2,1,0:T(8,128)S(1)} %get-tuple-element.6.token_in_ref, bf16[64,768]{1,0:T(8,128)(2,1)S(1)} %copy-done.5, bf16[768,768]{1,0:T(8,128)(2,1)S(1)} %copy-done.1, bf16[768,3072]{1,0:T(8,128)(2,1)} %proj_ref.3), custom_call_target="tpu_custom_call" | custom-call | flops 1207959552 | bytes 8000000 | tf_op jit(solution)/shard_map/project/pallas_call | solution.py:190
  69.5 1.0 copy-done.2
  70.5 3.7 %all-to-all-start = ((bf16[16,144,256]{2,1,0:T(8,128)(2,1)}), bf16[16,144,256]{2,1,0:T(8,128)(2,1)S(1)}, u32[]{:S(2)}, u32[]{:S(2)}) async-start(bf16[16,144,256]{2,1,0:T(8,128)(2,1)} %get-tuple-element.7), calls=%async_computation | async-start | bytes 2359296 | tf_op jit(solution)/shard_map/all_to_all | solution.py:367
  74.2 0.1 collective-permute-start.1
  74.3 0.5 collective-permute-start.3
  74.8 15.7 %all-to-all-done.own_ref = bf16[16,144,256]{2,1,0:T(8,128)(2,1)S(1)} async-done(((bf16[16,144,256]{2,1,0:T(8,128)(2,1)}), bf16[16,144,256]{2,1,0:T(8,128)(2,1)S(1)}, u32[]{:S(2)}, u32[]{:S(2)}) %all-to-all-start) | async-done | bytes 1179680 | tf_op jit(solution)/shard_map/all_to_all | solution.py:367
  90.5 1.1 slice.4
  91.6 2.7 %collective-permute-start = (bf16[16,96,256]{2,1,0:T(8,128)(2,1)}, bf16[16,96,256]{2,1,0:T(8,128)(2,1)}, u32[]{:S(2)}, u32[]{:S(2)}) collective-permute-start(bf16[16,96,256]{2,1,0:T(8,128)(2,1)} %slice.4), channel_id=1, source_target_pairs={{0,16},{16,0},{1,17},{17,1},{2,18},{18,2},{3,19},{19,3},{4,20},{20... | collective-permute-start | bytes 2359304 | tf_op jit(solution)/shard_map/ppermute | solution.py:347
  94.3 0.1 pad_add_fusion.order_ref
  94.4 15.0 %collective-permute-done.far_ref = bf16[16,96,256]{2,1,0:T(8,128)(2,1)} collective-permute-done((bf16[16,96,256]{2,1,0:T(8,128)(2,1)}, bf16[16,96,256]{2,1,0:T(8,128)(2,1)}, u32[]{:S(2)}, u32[]{:S(2)}) %collective-permute-start) | collective-permute-done | bytes 786464 | tf_op jit(solution)/shard_map/ppermute | solution.py:347
  109.4 17.7 %attend.1 = bf16[16,48,256]{2,1,0:T(8,128)(2,1)} custom-call(s32[2]{0:T(128)S(1)} %pad_add_fusion.order_ref, bf16[16,144,256]{2,1,0:T(8,128)(2,1)} %copy-done.13, bf16[16,96,256]{2,1,0:T(8,128)(2,1)} %collective-permute-done.far_ref, bf16[1024,512]{1,0:T(8,128)(2,1)S(1)} %bitcast.7, bf16[1024,512]{1,0:T(8,128)(2,1)} %collective-permute-done.1.bias1_ref, ...), custom_call_target="tpu_custom_call" | custom-call | flops 10000000000 | bytes 8000000 | tf_op jit(solution)/shard_map/attend/pallas_call | solution.py:267
  127.2 5.8 %all-to-all-start.2 = ((bf16[16,48,256]{2,1,0:T(8,128)(2,1)}), bf16[16,48,256]{2,1,0:T(8,128)(2,1)S(1)}, u32[]{:S(2)}, u32[]{:S(2)}) async-start(bf16[16,48,256]{2,1,0:T(8,128)(2,1)} %attend.1), calls=%async_computation.2 | async-start | bytes 786432 | tf_op jit(solution)/shard_map/all_to_all | solution.py:371
  133.0 9.1 %all-to-all-done.2.heads_ref = bf16[16,48,256]{2,1,0:T(8,128)(2,1)S(1)} async-done(((bf16[16,48,256]{2,1,0:T(8,128)(2,1)}), bf16[16,48,256]{2,1,0:T(8,128)(2,1)S(1)}, u32[]{:S(2)}, u32[]{:S(2)}) %all-to-all-start.2) | async-done | bytes 393248 | tf_op jit(solution)/shard_map/all_to_all | solution.py:371
  142.1 1.1 copy-done.3
  143.3 11.1 %finish.1 = (bf16[4,64,768]{2,1,0:T(8,128)(2,1)}, f32[4,3,1536]{2,1,0:T(4,128)S(1)}) custom-call(bf16[16,48,256]{2,1,0:T(8,128)(2,1)S(1)} %all-to-all-done.2.heads_ref, f32[256,768]{1,0:T(8,128)S(1)} %copy-done.3, f32[4,64,768]{2,1,0:T(8,128)S(1)} %get-tuple-element.6.token_in_ref, bf16[768,768]{1,0:T(8,128)(2,1)S(1)} %copy-done, ...), custom_call_target="tpu_custom_call" | custom-call | flops 3000000000 | bytes 15000000 | tf_op jit(solution)/shard_map/finish/pallas_call | solution.py:326
  154.4 0.7 copy.21
  (35 shorter events, 0.1 us)
Async XLA Ops:
  0.6 0.8 copy-start.6
  1.4 0.7 copy-start.7
  2.1 18.5 %copy-start.15 = (s32[1536]{0:T(1024)S(1)}, s32[1536]{0:T(1024)}, u32[]{:S(2)}) copy-start(s32[1536]{0:T(1024)} %param.20) | copy-start | bytes 18436
  2.1 18.5 %copy-start.14 = (f32[4,3,1536]{2,0,1:T(4,128)S(1)}, f32[4,3,1536]{2,0,1:T(4,128)}, u32[]{:S(2)}) copy-start(f32[4,3,1536]{2,0,1:T(4,128)} %param.19) | copy-start | bytes 221188
  2.1 37.7 %copy-start.8 = (bf16[1536,128]{1,0:T(8,128)(2,1)S(1)}, bf16[1536,128]{1,0:T(8,128)(2,1)}, u32[]{:S(2)}) copy-start(bf16[1536,128]{1,0:T(8,128)(2,1)} %cond_ref.1) | copy-start | bytes 1179652
  2.1 37.7 %copy-start.9 = (bf16[128,768]{1,0:T(8,128)(2,1)S(1)}, bf16[128,768]{1,0:T(8,128)(2,1)}, u32[]{:S(2)}) copy-start(bf16[128,768]{1,0:T(8,128)(2,1)} %to_token_ref.1) | copy-start | bytes 589828
  2.1 37.7 %copy-start.10 = (bf16[128,384]{1,0:T(8,128)(2,1)S(1)}, bf16[128,384]{1,0:T(8,128)(2,1)}, u32[]{:S(2)}) copy-start(bf16[128,384]{1,0:T(8,128)(2,1)} %proj_ref.2) | copy-start | bytes 294916
  2.1 37.7 %copy-start.11 = (bf16[128,128]{1,0:T(8,128)(2,1)S(1)}, bf16[128,128]{1,0:T(8,128)(2,1)}, u32[]{:S(2)}) copy-start(bf16[128,128]{1,0:T(8,128)(2,1)} %output_ref.2) | copy-start | bytes 98308
  2.1 37.7 %copy-start.12 = (f32[3,128]{1,0:T(4,128)S(1)}, f32[3,128]{1,0:T(4,128)}, u32[]{:S(2)}) copy-start(f32[3,128]{1,0:T(4,128)} %pos_weight_ref.1) | copy-start | bytes 4612
  12.5 25.8 %all-to-all-start.1 = ((bf16[16,64,512]{2,1,0:T(8,128)(2,1)}), bf16[16,64,512]{2,1,0:T(8,128)(2,1)S(1)}, u32[]{:S(2)}, u32[]{:S(2)}) async-start(bf16[16,64,512]{2,1,0:T(8,128)(2,1)} %pair_bias.1), calls=%async_computation.1 | async-start | bytes 2097152 | tf_op jit(solution)/shard_map/all_to_all | solution.py:359
  38.3 26.2 %copy-start.1 = (bf16[768,768]{1,0:T(8,128)(2,1)S(1)}, bf16[768,768]{1,0:T(8,128)(2,1)}, u32[]{:S(2)}) copy-start(bf16[768,768]{1,0:T(8,128)(2,1)} %ada_ref.1) | copy-start | bytes 3538948
  38.3 26.2 %copy-start.5 = (bf16[64,768]{1,0:T(8,128)(2,1)S(1)}, bf16[64,768]{1,0:T(8,128)(2,1)}, u32[]{:S(2)}) copy-start(bf16[64,768]{1,0:T(8,128)(2,1)} %single_ref.1) | copy-start | bytes 294916
  38.3 36.0 %collective-permute-start.2 = (bf16[1024,512]{1,0:T(8,128)(2,1)S(1)}, bf16[1024,512]{1,0:T(8,128)(2,1)}, u32[]{:S(2)}, u32[]{:S(2)}) collective-permute-start(bf16[1024,512]{1,0:T(8,128)(2,1)S(1)} %bitcast.5), channel_id=1, source_target_pairs={{0,64},{64,0},{1,65},{65,1},{2,66},{66,2},{3,67},{67,3},{4,68},{68... | collective-permute-start | bytes 3145736 | tf_op jit(solution)/shard_map/ppermute | solution.py:347
  69.5 1.0 copy-start.2
  70.5 20.0 %all-to-all-start = ((bf16[16,144,256]{2,1,0:T(8,128)(2,1)}), bf16[16,144,256]{2,1,0:T(8,128)(2,1)S(1)}, u32[]{:S(2)}, u32[]{:S(2)}) async-start(bf16[16,144,256]{2,1,0:T(8,128)(2,1)} %get-tuple-element.7), calls=%async_computation | async-start | bytes 2359296 | tf_op jit(solution)/shard_map/all_to_all | solution.py:367
  74.2 35.3 %collective-permute-start.1 = (bf16[1024,512]{1,0:T(8,128)(2,1)S(1)}, bf16[1024,512]{1,0:T(8,128)(2,1)}, u32[]{:S(2)}, u32[]{:S(2)}) collective-permute-start(bf16[1024,512]{1,0:T(8,128)(2,1)S(1)} %bitcast.6), channel_id=1, source_target_pairs={{0,32},{32,0},{1,33},{33,1},{2,34},{34,2},{3,35},{35,3},{4,36},{36... | collective-permute-start | bytes 3145736 | tf_op jit(solution)/shard_map/ppermute | solution.py:347
  74.3 35.2 %collective-permute-start.3 = (bf16[1024,512]{1,0:T(8,128)(2,1)}, bf16[1024,512]{1,0:T(8,128)(2,1)}, u32[]{:S(2)}, u32[]{:S(2)}) collective-permute-start(bf16[1024,512]{1,0:T(8,128)(2,1)} %collective-permute-done.2.bias2_ref), channel_id=1, source_target_pairs={{0,32},{32,0},{1,33},{33,1},{2,34},{34,2},{3,35},{35,3},{4,36},{36... | collective-permute-start | bytes 3145736 | tf_op jit(solution)/shard_map/ppermute | solution.py:347
  90.5 3.8 %copy-start.13 = (bf16[16,144,256]{2,1,0:T(8,128)(2,1)}, bf16[16,144,256]{2,1,0:T(8,128)(2,1)S(1)}, u32[]{:S(2)}) copy-start(bf16[16,144,256]{2,1,0:T(8,128)(2,1)S(1)} %all-to-all-done.own_ref) | copy-start | bytes 3538948
  91.6 17.8 %collective-permute-start = (bf16[16,96,256]{2,1,0:T(8,128)(2,1)}, bf16[16,96,256]{2,1,0:T(8,128)(2,1)}, u32[]{:S(2)}, u32[]{:S(2)}) collective-permute-start(bf16[16,96,256]{2,1,0:T(8,128)(2,1)} %slice.4), channel_id=1, source_target_pairs={{0,16},{16,0},{1,17},{17,1},{2,18},{18,2},{3,19},{19,3},{4,20},{20... | collective-permute-start | bytes 2359304 | tf_op jit(solution)/shard_map/ppermute | solution.py:347
  94.4 38.6 %copy-start.16 = (f32[128,3]{0,1:T(4,128)S(1)}, f32[128,3]{0,1:T(4,128)}, u32[]{:S(2)}) copy-start(f32[128,3]{0,1:T(4,128)} %param.34) | copy-start | bytes 4612
  94.4 47.8 %copy-start = (bf16[768,768]{1,0:T(8,128)(2,1)S(1)}, bf16[768,768]{1,0:T(8,128)(2,1)}, u32[]{:S(2)}) copy-start(bf16[768,768]{1,0:T(8,128)(2,1)} %output_ref.3) | copy-start | bytes 3538948
  94.4 47.8 %copy-start.4 = (bf16[768,128]{1,0:T(8,128)(2,1)S(1)}, bf16[768,128]{1,0:T(8,128)(2,1)}, u32[]{:S(2)}) copy-start(bf16[768,128]{1,0:T(8,128)(2,1)} %to_atom_ref.1) | copy-start | bytes 589828
  127.2 15.0 %all-to-all-start.2 = ((bf16[16,48,256]{2,1,0:T(8,128)(2,1)}), bf16[16,48,256]{2,1,0:T(8,128)(2,1)S(1)}, u32[]{:S(2)}, u32[]{:S(2)}) async-start(bf16[16,48,256]{2,1,0:T(8,128)(2,1)} %attend.1), calls=%async_computation.2 | async-start | bytes 786432 | tf_op jit(solution)/shard_map/all_to_all | solution.py:371
  142.1 1.1 copy-start.3

commit v2 on v1

v2 whole, which is shorter than its diff:
```python
import functools

import jax
import jax.numpy as jnp
import numpy as np
from jax import lax
from jax.experimental import pallas as pl
from jax.experimental.pallas import tpu as pltpu
from jax.sharding import Mesh, PartitionSpec as P

ATOM_HEADS = 4
QUERY_BLOCK = 32
KEY_WINDOW = 128
NORM_EPSILON = 1e-05
MASKED_SCORE = -1000000000.0
LOG2E = 1.4426950408889634
F32 = jnp.float32
BF16 = jnp.bfloat16
VMEM_LIMIT = 60 * 1024 * 1024

TN = (((0,), (0,)), ((), ()))
NT = (((1,), (1,)), ((), ()))
NN = (((1,), (0,)), ((), ()))


def mm(a, b, dims=NN):
    return lax.dot_general(a, b, dims, preferred_element_type=F32)


def norm_rows(inputs):
    row_mean = jnp.mean(inputs, axis=-1, keepdims=True)
    centered = inputs - row_mean
    variance = jnp.mean(centered * centered, axis=-1, keepdims=True)
    return centered * lax.rsqrt(variance + NORM_EPSILON)


def params():
    return pltpu.CompilerParams(vmem_limit_bytes=VMEM_LIMIT)


def pair_kernel(pair_ref, weight_ref, out_ref, center_s):
    rows, cols, width = pair_ref.shape
    heads = weight_ref.shape[0]

    @pl.when(pl.program_id(0) == 0)
    def _():
        same = lax.broadcasted_iota(jnp.int32, (width, width), 0) == lax.broadcasted_iota(jnp.int32, (width, width), 1)
        center_s[...] = (same.astype(F32) - 1.0 / width).astype(BF16)

    ones = jnp.full((heads, width), 1.0 / width, BF16)
    flat = pair_ref[...].reshape(rows * cols, width)
    centered = mm(flat, center_s[...])
    top = mm(weight_ref[...], centered.astype(BF16), NT)
    variance = mm(ones, (centered * centered).astype(BF16), NT)
    bias = top * (lax.rsqrt(variance + NORM_EPSILON) * LOG2E)
    for h in range(heads):
        block = bias[h : h + 1].reshape(rows, cols).astype(BF16)
        for k in range(out_ref.shape[0]):
            out_ref[k, h] = block


def pair_bias(pair_rep, pair_weight, copies):
    rows, cols, width = pair_rep.shape
    heads = pair_weight.shape[1]
    step = 16
    return pl.pallas_call(
        pair_kernel,
        grid=(rows // step,),
        in_specs=[
            pl.BlockSpec((step, cols, width), lambda i: (i, 0, 0)),
            pl.BlockSpec((heads, width), lambda i: (0, 0)),
        ],
        out_specs=pl.BlockSpec((copies, heads, step, cols), lambda i: (0, 0, i, 0)),
        out_shape=jax.ShapeDtypeStruct((copies, heads, rows, cols), BF16),
        scratch_shapes=[pltpu.VMEM((width, width), BF16)],
        compiler_params=params(),
        cost_estimate=pl.CostEstimate(flops=10**10, bytes_accessed=10**7, transcendentals=0),
        name="pair_bias",
    )(pair_rep, pair_weight.T)


def split_three(value, order):
    first = value.astype(BF16).astype(F32)
    second = (value - first).astype(BF16).astype(F32)
    third = value - first - second
    terms = (first, second, third)
    return [terms[k] for k in order]


def atom_kernel(
    base, cond_ref, pos_ref, token_ref, pos_weight_ref, proj_ref, output_ref, to_token_ref,
    *refs,
):
    mid_ref, token_in_ref, query_s, key_s, val_s, mixed_s, pos_s, weight_s = refs[-8:]
    slots, width = cond_ref.shape
    tokens = token_in_ref.shape[1]
    head = width // ATOM_HEADS
    owner = token_ref[...]
    count = jnp.sum((owner < tokens).astype(jnp.int32))

    @pl.when(pl.program_id(0) == 0)
    def _():
        pos_s[...] = jnp.zeros_like(pos_s)
        weight_s[...] = jnp.zeros_like(weight_s)
        for k, piece in enumerate(split_three(pos_weight_ref[...], (0, 0, 0, 1, 1, 2))):
            weight_s[8 * k : 8 * k + 3, :] = piece
        val_s[:, width:] = jnp.ones((slots, width), BF16)

    position = pos_ref[:, pl.ds(base + pl.program_id(0), 1), :].reshape(3, slots)
    for k, piece in enumerate(split_three(position, (0, 1, 2, 0, 1, 0))):
        pos_s[8 * k : 8 * k + 3, :] = piece
    act = cond_ref[...].astype(F32) + mm(pos_s[...].astype(BF16), weight_s[...].astype(BF16), TN)
    normed = norm_rows(act).astype(BF16)
    projected = mm(normed, proj_ref[...])
    query_s[...] = (projected[:, :width] * (head ** (-0.5) * LOG2E)).astype(BF16)
    key_s[...] = projected[:, width : 2 * width].astype(BF16)
    val_s[:, :width] = projected[:, 2 * width :].astype(BF16)
    stacked = ATOM_HEADS * QUERY_BLOCK
    of_row = lax.broadcasted_iota(jnp.int32, (stacked, width), 0) // QUERY_BLOCK
    of_lane = lax.broadcasted_iota(jnp.int32, (stacked, width), 1) // head
    own_head = of_row == of_lane
    lane = lax.broadcasted_iota(jnp.int32, (stacked, KEY_WINDOW), 1)
    blocks = slots // QUERY_BLOCK
    group = 8
    for first in range(0, blocks, group):
        starts = [
            min(max(b * QUERY_BLOCK - (KEY_WINDOW - QUERY_BLOCK) // 2, 0), slots - KEY_WINDOW)
            for b in range(first, first + group)
        ]
        scores = []
        for k, start in enumerate(starts):
            low = (first + k) * QUERY_BLOCK
            query = query_s[low : low + QUERY_BLOCK, :]
            query = jnp.concatenate([query] * ATOM_HEADS, axis=0)
            query = jnp.where(own_head, query, jnp.zeros_like(query))
            score = mm(query, key_s[start : start + KEY_WINDOW, :], NT)
            scores.append(jnp.where(lane < count - start, score, MASKED_SCORE))
        weights = [jnp.exp2(s - jnp.max(s, axis=-1, keepdims=True)).astype(BF16) for s in scores]
        for k, start in enumerate(starts):
            low = (first + k) * QUERY_BLOCK
            summed = mm(weights[k], val_s[start : start + KEY_WINDOW, :])
            mixed = jnp.where(own_head, summed[:, :width] / summed[:, width:], 0.0)
            mixed = mixed.reshape(ATOM_HEADS, QUERY_BLOCK, width).sum(axis=0)
            mixed_s[low : low + QUERY_BLOCK, :] = mixed.astype(BF16)
    mid = act + mm(mixed_s[...], output_ref[...])
    mid_ref[0] = mid
    feature = jnp.maximum(mm(mid.astype(BF16), to_token_ref[...]), 0.0).astype(BF16)
    onehot = lax.broadcasted_iota(jnp.int32, (tokens, slots), 0) == owner
    members = jnp.sum(onehot.astype(F32), axis=1, keepdims=True)
    token_in_ref[0] = mm(onehot.astype(BF16), feature) / members


def atom_stage(atom_cond, atom_pos, atom_token, pos_weight, atom_proj, atom_output, atom_to_token, tokens, base, samples, all_samples, mid):
    slots, width = atom_cond.shape
    channels = atom_to_token.shape[1]
    whole = lambda a: pl.BlockSpec(a.shape, lambda s: (0,) * a.ndim)
    atom_token = atom_token.reshape(1, slots)
    earlier = () if mid is None else (mid,)
    return pl.pallas_call(
        functools.partial(atom_kernel, base),
        grid=(samples,),
        in_specs=[
            whole(atom_cond),
            whole(atom_pos),
            whole(atom_token),
            whole(pos_weight),
            whole(atom_proj),
            whole(atom_output),
            whole(atom_to_token),
        ] + [pl.BlockSpec(memory_space=pl.ANY)] * len(earlier),
        input_output_aliases={7: 0} if earlier else {},
        out_specs=[
            pl.BlockSpec((1, slots, width), lambda s: (base + s, 0, 0)),
            pl.BlockSpec((1, tokens, channels), lambda s: (s, 0, 0)),
        ],
        out_shape=[
            jax.ShapeDtypeStruct((all_samples, slots, width), F32),
            jax.ShapeDtypeStruct((samples, tokens, channels), F32),
        ],
        scratch_shapes=[
            pltpu.VMEM((slots, width), BF16),
            pltpu.VMEM((slots, width), BF16),
            pltpu.VMEM((slots, 2 * width), BF16),
            pltpu.VMEM((slots, width), BF16),
            pltpu.VMEM((48, slots), F32),
            pltpu.VMEM((48, width), F32),
        ],
        compiler_params=params(),
        cost_estimate=pl.CostEstimate(flops=samples * 6 * 10**9, bytes_accessed=10**6, transcendentals=0),
        name="atom_stage",
    )(atom_cond, atom_pos, atom_token, pos_weight, atom_proj, atom_output, atom_to_token, *earlier)


def project_kernel(token_in_ref, single_ref, ada_ref, proj_ref, *refs):
    heads_ref, gate_ref = refs[-2:]
    samples, tokens, channels = token_in_ref.shape
    copies, heads, _, lanes = heads_ref.shape
    head = channels // heads
    conditioning = 1.0 + mm(single_ref[...], ada_ref[...])
    adapted = (norm_rows(token_in_ref[...]) * conditioning[None]).astype(BF16).reshape(lanes, channels)
    for part in range(3):
        rows = mm(adapted, proj_ref[:, part * channels : (part + 1) * channels])
        if part == 0:
            rows = rows * (head ** (-0.5) * LOG2E)
        turned = rows.T.astype(BF16).reshape(heads, head, lanes)
        for k in range(copies):
            heads_ref[k, :, part * head : (part + 1) * head, :] = turned
    gate = mm(adapted, proj_ref[:, 3 * channels :])
    gate_ref[...] = jax.nn.sigmoid(gate)


def project(token_in, tok_single, ada_weight, tok_proj, heads, copies, half, halves, gate):
    samples, tokens, channels = token_in.shape
    lanes = samples * tokens
    head = channels // heads
    earlier = () if gate is None else (gate,)
    whole = lambda a: pl.BlockSpec(a.shape, lambda i: (0,) * a.ndim)
    args = (token_in, tok_single, ada_weight, tok_proj)
    return pl.pallas_call(
        project_kernel,
        grid=(1,),
        in_specs=[whole(a) for a in args] + [pl.BlockSpec(memory_space=pl.ANY)] * len(earlier),
        out_specs=[
            pl.BlockSpec((copies, heads, 3 * head, lanes), lambda i: (0, 0, 0, 0)),
            pl.BlockSpec((lanes, channels), lambda i: (half, 0)),
        ],
        out_shape=[
            jax.ShapeDtypeStruct((copies, heads, 3 * head, lanes), BF16),
            jax.ShapeDtypeStruct((halves * lanes, channels), F32),
        ],
        input_output_aliases={4: 1} if earlier else {},
        compiler_params=params(),
        cost_estimate=pl.CostEstimate(flops=4 * 10**9, bytes_accessed=8 * 10**6, transcendentals=0),
        name="project",
    )(*args, *earlier)


def attend_kernel(order_ref, heads_ref, near_ref, other_ref, *refs):
    out_ref, query_s, key_s, val_s = refs[-4:]
    peers, head, lanes = out_ref.shape
    samples, _, keys = key_s.shape
    tokens = lanes // samples
    width = val_s.shape[2]
    sources = heads_ref.shape[0]
    cols = near_ref.shape[2]
    step = pl.program_id(0)
    core = order_ref[0]
    first = order_ref[1]

    @pl.when(step == 0)
    def _():
        fill = jnp.zeros((width - head, lanes), F32)
        fill_v = jnp.where(lax.broadcasted_iota(jnp.int32, (width - head, lanes), 0) == 0, 1.0, 0.0)

        def turn(block, below):
            return jnp.concatenate([block.astype(F32), below], axis=0).T.astype(BF16)

        for j in range(sources // 2):
            query = turn(heads_ref[first + j, :head, :], fill)
            for s in range(samples):
                query_s[s, j * tokens : (j + 1) * tokens, :] = query[s * tokens : (s + 1) * tokens, :head]
        for j in range(sources):
            val = turn(heads_ref[j, 2 * head :, :], fill_v)
            for s in range(samples):
                val_s[s, j * tokens : (j + 1) * tokens, :] = val[s * tokens : (s + 1) * tokens]
        for j in range(0, sources, 2):
            for s in range(samples):
                pair = [heads_ref[k, head : 2 * head, s * tokens : (s + 1) * tokens] for k in (j, j + 1)]
                key_s[s, :, j * tokens : (j + 2) * tokens] = jnp.concatenate(pair, axis=1)

    rows = peers * tokens
    results = []
    for s in range(samples):
        query = query_s[s, pl.ds(pl.multiple_of(step * rows, rows), rows), :]
        scores = []
        places = []
        for ref, which in ((near_ref, core), (other_ref, 1 - core)):
            for k in range(2):
                place = pl.ds(pl.multiple_of((2 * k + which) * cols, cols), cols)
                places.append(place)
                scores.append(mm(query, key_s[s, :, place]) + ref[k].astype(F32))
        top = functools.reduce(jnp.maximum, scores)
        top = jnp.max(top, axis=-1, keepdims=True)
        total = 0.0
        for x, place in zip(scores, places):
            total = total + mm(jnp.exp2(x - top).astype(BF16), val_s[s, place, :])
        results.append(total / total[:, head : head + 1])
    for j in range(peers):
        block = jnp.concatenate([r[j * tokens : (j + 1) * tokens] for r in results], axis=0)
        out_ref[j] = block.T[:head].astype(BF16)


def attend(order, qkv, near, other, samples, half, halves, result):
    sources, triple, lanes = qkv.shape
    head = triple // 3
    tokens = lanes // samples
    width = 128
    peers = 4
    rows = peers * tokens
    total = sources * tokens
    cols = near.shape[2]
    earlier = () if result is None else (result,)
    return pl.pallas_call(
        attend_kernel,
        grid_spec=pltpu.PrefetchScalarGridSpec(
            num_scalar_prefetch=1,
            grid=(total // 2 // rows,),
            in_specs=[pl.BlockSpec(qkv.shape, lambda i, *_: (0, 0, 0))]
            + [pl.BlockSpec((2, rows, cols), lambda i, *_: (0, i, 0))] * 2
            + [pl.BlockSpec(memory_space=pl.ANY)] * len(earlier),
            out_specs=pl.BlockSpec((peers, head, lanes), lambda i, *_: (i, half, 0)),
            scratch_shapes=[
                pltpu.VMEM((samples, total // 2, head), BF16),
                pltpu.VMEM((samples, head, total), BF16),
                pltpu.VMEM((samples, total, width), BF16),
            ],
        ),
        out_shape=jax.ShapeDtypeStruct((sources // 2, halves * head, lanes), BF16),
        input_output_aliases={4: 0} if earlier else {},
        compiler_params=params(),
        cost_estimate=pl.CostEstimate(flops=samples * 5 * 10**9, bytes_accessed=10**6, transcendentals=0),
        name="attend",
    )(order, qkv, near, other, *earlier)


def finish_kernel(
    heads_ref, gate_ref, output_ref, trans_in_ref, trans_out_ref, to_atom_ref, mid_ref, owner_ref, update_ref, *refs
):
    token_in_refs, (token_out_ref, atom_ref, feature_s) = refs[:-3], refs[-3:]
    samples, tokens, channels = token_out_ref.shape
    step = pl.program_id(0)

    @pl.when(step == 0)
    def _():
        halves = len(token_in_refs)
        head = heads_ref.shape[1] // halves
        lanes = heads_ref.shape[2]
        attended = [heads_ref[:, k * head : (k + 1) * head, :].reshape(channels, lanes) for k in range(halves)]
        attended = jnp.concatenate([x.astype(F32).T for x in attended], axis=0)
        gated = (gate_ref[...] * attended).astype(BF16)
        token_in = jnp.concatenate([ref[...].reshape(lanes, channels) for ref in token_in_refs], axis=0)
        after = token_in + mm(gated, output_ref[...])
        hidden_in = norm_rows(after).astype(BF16)
        hidden_width = trans_out_ref.shape[0]
        left = mm(hidden_in, trans_in_ref[:, :hidden_width])
        right = mm(hidden_in, trans_in_ref[:, hidden_width:])
        hidden = (jax.nn.silu(left) * right).astype(BF16)
        result = (after + mm(hidden, trans_out_ref[...])).astype(BF16)
        token_out_ref[...] = result.reshape(samples, tokens, channels)
        feature_s[...] = mm(result, to_atom_ref[...]).astype(BF16).reshape(feature_s.shape)

    owner = owner_ref[...]
    slots = owner.shape[1]
    onehot = (lax.broadcasted_iota(jnp.int32, (tokens, slots), 0) == owner).astype(BF16)
    final = norm_rows(mid_ref[0] + mm(onehot, feature_s[step], TN))
    weight = update_ref[...]
    high = final.astype(BF16)
    low = (final - high.astype(F32)).astype(BF16)
    first = weight.astype(BF16)
    second = (weight - first.astype(F32)).astype(BF16)
    update = mm(first, high, NT) + (mm(second, high, NT) + mm(first, low, NT))
    update = update[:3] * (owner < tokens).astype(F32)
    atom_ref[:, pl.ds(step, 1), :] = update.reshape(3, 1, slots)


def finish(
    heads, gate, tok_output, transition_in, transition_out, token_to_atom, atom_mid, atom_token, pos_update, token_in
):
    each, tokens, channels = token_in[0].shape
    samples, slots, width = atom_mid.shape
    owner = atom_token.reshape(1, slots)
    turned = jnp.pad(pos_update.T, ((0, 5), (0, 0)))
    whole = lambda a: pl.BlockSpec(a.shape, lambda s: (0,) * a.ndim)
    args = (heads, gate, tok_output, transition_in, transition_out, token_to_atom)
    return pl.pallas_call(
        finish_kernel,
        grid=(samples,),
        in_specs=[whole(a) for a in args]
        + [pl.BlockSpec((1, slots, width), lambda s: (s, 0, 0)), whole(owner), whole(turned)]
        + [whole(a) for a in token_in],
        out_specs=[
            pl.BlockSpec((samples, tokens, channels), lambda s: (0, 0, 0)),
            pl.BlockSpec((3, samples, slots), lambda s: (0, 0, 0)),
        ],
        out_shape=[
            jax.ShapeDtypeStruct((samples, tokens, channels), BF16),
            jax.ShapeDtypeStruct((3, samples, slots), F32),
        ],
        scratch_shapes=[pltpu.VMEM((samples, tokens, width), BF16)],
        compiler_params=params(),
        cost_estimate=pl.CostEstimate(flops=8 * 10**9, bytes_accessed=10**7, transcendentals=0),
        name="finish",
    )(*args, atom_mid, owner, turned, *token_in)


def exchange(x, axes):
    return lax.all_to_all(x, axes, 0, 0, tiled=True)


def per_device(
    atom_cond, atom_pos, atom_token, pos_weight, atom_proj, atom_output, atom_to_token, tok_single, ada_weight,
    pair_rep, pair_weight, tok_proj, tok_output, transition_in, transition_out, token_to_atom, pos_update,
):
    tokens, channels = tok_single.shape
    heads = pair_weight.shape[1]
    samples = atom_pos.shape[0]
    halves = 2
    each = samples // halves
    pos = jnp.swapaxes(atom_pos, 0, 1)
    order = jnp.stack([lax.axis_index("core"), lax.axis_index("xhi") * heads]).astype(jnp.int32)
    bias = pair_bias(pair_rep, pair_weight, 2)
    near = exchange(bias.reshape((2 * heads,) + bias.shape[2:]), ("xlo", "y", "z"))
    near = near.reshape(2, heads * tokens, near.shape[2])
    other = lax.ppermute(near, "core", [(0, 1), (1, 0)])
    inputs, received = [], []
    mid = gate = None
    for k in range(halves):
        mid, token_in = atom_stage(
            atom_cond, pos, atom_token, pos_weight, atom_proj, atom_output, atom_to_token, tokens, k * each, each,
            samples, mid,
        )
        qkv, gate = project(token_in, tok_single, ada_weight, tok_proj, heads, 2, k, halves, gate)
        inputs.append(token_in)
        received.append(exchange(qkv.reshape((2 * heads,) + qkv.shape[2:]), ("xhi", "y", "z")))
    attended = None
    for k in range(halves):
        attended = attend(order, received[k], near, other, each, k, halves, attended)
    attended = exchange(attended, ("y", "z"))
    token_out, update = finish(
        attended, gate, tok_output, transition_in, transition_out, token_to_atom, mid, atom_token, pos_update, inputs
    )
    return token_out, jnp.swapaxes(update, 0, 1)


def solution(mesh):
    fine = Mesh(mesh.devices.reshape(2, 2, 2, 4, 4), ("xlo", "core", "xhi", "y", "z"))
    tok = ("xhi", "y", "z")
    sample = ("xlo", "core")
    return jax.shard_map(
        per_device,
        mesh=fine,
        in_specs=(
            P(tok, None), P(sample, None, tok), P(tok), P(), P(), P(), P(), P(tok, None), P(),
            P(tok, sample, None), P(), P(), P(), P(), P(), P(), P(),
        ),
        out_specs=(P(sample, tok, None), P(sample, None, tok)),
        check_vma=False,
    )
```

time: 156 us -> 155 us (level)
  waiting for transfers between devices: 57.5 us -> 45.8 us
  Pallas kernels: 68.8 us -> 78.2 us
  starting transfers between devices: 22.5 us -> 27.4 us
  local copies, waits for them, and re-layouts: 5.39 us -> 1.96 us
    ppermute x4 -> x1, waiting for transfers between devices: 15 us -> 0.01 us  [per_device(): other = lax.ppermute(near, 'core', [(0, 1), (1, 0)])]
    all_to_all x3 -> x4, starting transfers between devices: 17.7 us -> 27.4 us  [exchange(): return lax.all_to_all(x, axes, 0, 0, tiled=True)]
    pallas_call x1 -> x2, Pallas kernels: 17.7 us -> 22.5 us  [attend(): pl.pallas_call(attend_kernel, grid_spec=pltpu.PrefetchScalarGridSpec(num_...]
    ppermute x4 -> x1, starting transfers between devices: 4.8 us -> 0.01 us  [per_device(): other = lax.ppermute(near, 'core', [(0, 1), (1, 0)])]
    pallas_call x2 -> x4, Pallas kernels: 29.6 us -> 33 us  [the longest x2 22.8 us: atom_stage(): pl.pallas_call(functools.partial(atom_kernel, base), grid=(samples,), in_...]
    all_to_all x3 -> x4, waiting for transfers between devices: 42.5 us -> 45.8 us  [exchange(): return lax.all_to_all(x, axes, 0, 0, tiled=True)]
    unnamed x35 -> x10, local copies, waits for them, and re-layouts: 3.63 us -> 0.79 us
  transfers between devices with their start and end apart: 7 -> 5, of which waited for: 4 -> 4; matrix products, arithmetic and copies ran while one was open for 1% -> 1% of each run, Pallas kernels for 19% -> 29%
where the time goes in v2:
time: 155 us
  Pallas kernels  78.2 us (50%)
  waiting for transfers between devices  45.8 us (30%)
  starting transfers between devices  27.4 us (18%)
  local copies, waits for them, and re-layouts  1.96 us (1%)
    all_to_all x4, waiting for transfers between devices, exchange(): return lax.all_to_all(x, axes, 0, 0, tiled=True)  45.8 us
    all_to_all x4, starting transfers between devices, exchange(): return lax.all_to_all(x, axes, 0, 0, tiled=True)  27.4 us
    pallas_call x2, Pallas kernels, atom_stage(): pl.pallas_call(functools.partial(atom_kernel, base), grid=(samples,), in_...  22.8 us
    pallas_call x2, Pallas kernels, attend(): pl.pallas_call(attend_kernel, grid_spec=pltpu.PrefetchScalarGridSpec(num_...  22.5 us
    pallas_call x1, Pallas kernels, finish(): pl.pallas_call(finish_kernel, grid=(samples,), in_specs=[whole(a) for a i...  12.3 us
    pallas_call x1, Pallas kernels, pair_bias(): pl.pallas_call(pair_kernel, grid=(rows // step,), in_specs=[pl.BlockSpec(...  10.4 us
    pallas_call x2, Pallas kernels, project(): pl.pallas_call(project_kernel, grid=(1,), in_specs=[whole(a) for a in arg...  10.2 us
  transfers between devices with their start and end apart: 5, of which 4 were waited for; matrix products, arithmetic and copies ran while one was open for 1% of the time, Pallas kernels for 29%

profile of v2, /device:TPU:0, one launch (start us, length us, event | category | flops | bytes accessed | tf_op | source)
XLA Modules:
  0.0 154.7 jit_solution(142984154213393379)
XLA Ops:
  0.6 10.4 %pair_bias.1 = bf16[2,16,64,512]{3,2,1,0:T(8,128)(2,1)} custom-call(bf16[64,512,128]{2,1,0:T(8,128)(2,1)} %pair_ref.1, bf16[16,128]{1,0:T(8,128)(2,1)} %bitcast.19), custom_call_target="tpu_custom_call" | custom-call | flops 10000000000 | bytes 10000000 | tf_op jit(solution)/shard_map/pair_bias/pallas_call | solution.py:66
  11.1 9.5 %all-to-all-start.1 = ((bf16[32,64,512]{2,1,0:T(8,128)(2,1)}), bf16[32,64,512]{2,1,0:T(8,128)(2,1)S(1)}, u32[]{:S(2)}, u32[]{:S(2)}) async-start(bf16[32,64,512]{2,1,0:T(8,128)(2,1)} %bitcast.13), calls=%async_computation.1 | async-start | bytes 4194304 | tf_op jit(solution)/shard_map/all_to_all | solution.py:397
  20.5 0.6 reshape.21.token_ref.owner_ref
  21.1 28.0 %all-to-all-done.1 = bf16[32,64,512]{2,1,0:T(8,128)(2,1)S(1)} async-done(((bf16[32,64,512]{2,1,0:T(8,128)(2,1)}), bf16[32,64,512]{2,1,0:T(8,128)(2,1)S(1)}, u32[]{:S(2)}, u32[]{:S(2)}) %all-to-all-start.1) | async-done | bytes 2097184 | tf_op jit(solution)/shard_map/all_to_all | solution.py:397
  49.1 0.0 collective-permute-start
  49.1 11.7 %atom_stage.2 = (f32[4,1536,128]{2,1,0:T(8,128)}, f32[2,64,768]{2,1,0:T(8,128)}) custom-call(bf16[1536,128]{1,0:T(8,128)(2,1)} %cond_ref.3, f32[3,4,1536]{2,1,0:T(4,128)} %bitcast.17, s32[1,1536]{1,0:T(1,128)} %reshape.21.token_ref.owner_ref, f32[3,128]{1,0:T(4,128)} %pos_weight_ref.3, bf16[128,384]{1,0:T(8,128)(2,1)} %proj_ref.5, ...), custom_call_target="tpu_custom_call" | custom-call | flops 12000000000 | bytes 1000000 | tf_op jit(solution)/shard_map/atom_stage/pallas_call | solution.py:159
  60.9 0.0 copy-done
  60.9 5.1 %project.2 = (bf16[2,16,144,128]{3,2,1,0:T(8,128)(2,1)}, f32[256,768]{1,0:T(8,128)}) custom-call(f32[2,64,768]{2,1,0:T(8,128)} %get-tuple-element.14.token_in_ref.refs_0_, bf16[64,768]{1,0:T(8,128)(2,1)} %single_ref.3, bf16[768,768]{1,0:T(8,128)(2,1)} %ada_ref.3, bf16[768,3072]{1,0:T(8,128)(2,1)} %proj_ref.7), custom_call_target="tpu_custom_call" | custom-call | flops 4000000000 | bytes 8000000 | tf_op jit(solution)/shard_map/project/pallas_call | solution.py:219
  66.0 6.6 %all-to-all-start.2 = ((bf16[32,144,128]{2,1,0:T(8,128)(2,1)}), bf16[32,144,128]{2,1,0:T(8,128)(2,1)S(1)}, u32[]{:S(2)}, u32[]{:S(2)}) async-start(bf16[32,144,128]{2,1,0:T(8,128)(2,1)} %bitcast.15), calls=%async_computation.2 | async-start | bytes 2359296 | tf_op jit(solution)/shard_map/all_to_all | solution.py:397
  72.6 11.1 %atom_stage.3 = (f32[4,1536,128]{2,1,0:T(8,128)}, f32[2,64,768]{2,1,0:T(8,128)}) custom-call(bf16[1536,128]{1,0:T(8,128)(2,1)} %cond_ref.3, f32[3,4,1536]{2,1,0:T(4,128)} %bitcast.18, s32[1,1536]{1,0:T(1,128)} %reshape.21.token_ref.owner_ref, f32[3,128]{1,0:T(4,128)} %pos_weight_ref.3, bf16[128,384]{1,0:T(8,128)(2,1)} %proj_ref.5, ...), custom_call_target="tpu_custom_call", output_to_operand_aliasing={{0}: (7, {})} | custom-call | flops 12000000000 | bytes 1000000 | tf_op jit(solution)/shard_map/atom_stage/pallas_call | solution.py:159
  83.7 5.1 %project.3 = (bf16[2,16,144,128]{3,2,1,0:T(8,128)(2,1)}, f32[256,768]{1,0:T(8,128)}) custom-call(f32[2,64,768]{2,1,0:T(8,128)} %get-tuple-element.13.token_in_ref.refs_1_, bf16[64,768]{1,0:T(8,128)(2,1)} %single_ref.3, bf16[768,768]{1,0:T(8,128)(2,1)} %ada_ref.3, bf16[768,3072]{1,0:T(8,128)(2,1)} %proj_ref.7, ...), custom_call_target="tpu_custom_call", output_to_operand_aliasing={{1}: (4, {})} | custom-call | flops 4000000000 | bytes 8000000 | tf_op jit(solution)/shard_map/project/pallas_call | solution.py:219
  88.8 2.7 %all-to-all-done.2.heads_ref = bf16[32,144,128]{2,1,0:T(8,128)(2,1)S(1)} async-done(((bf16[32,144,128]{2,1,0:T(8,128)(2,1)}), bf16[32,144,128]{2,1,0:T(8,128)(2,1)S(1)}, u32[]{:S(2)}, u32[]{:S(2)}) %all-to-all-start.2) | async-done | bytes 1179680 | tf_op jit(solution)/shard_map/all_to_all | solution.py:397
  91.5 7.1 %all-to-all-start = ((bf16[32,144,128]{2,1,0:T(8,128)(2,1)}), bf16[32,144,128]{2,1,0:T(8,128)(2,1)}, u32[]{:S(2)}, u32[]{:S(2)}) async-start(bf16[32,144,128]{2,1,0:T(8,128)(2,1)} %bitcast.14), calls=%async_computation | async-start | bytes 2359296 | tf_op jit(solution)/shard_map/all_to_all | solution.py:397
  98.6 0.6 pad_add_fusion.order_ref
  99.2 0.0 collective-permute-done.other_ref
  99.2 11.3 %attend.2.refs_0_ = bf16[16,96,128]{2,1,0:T(8,128)(2,1)} custom-call(s32[2]{0:T(128)} %pad_add_fusion.order_ref, bf16[32,144,128]{2,1,0:T(8,128)(2,1)} %copy-done.1, bf16[2,1024,512]{2,1,0:T(8,128)(2,1)} %bitcast.11, bf16[2,1024,512]{2,1,0:T(8,128)(2,1)} %collective-permute-done.other_ref), custom_call_target="tpu_custom_call" | custom-call | flops 10000000000 | bytes 1000000 | tf_op jit(solution)/shard_map/attend/pallas_call | solution.py:303
  110.4 6.6 %all-to-all-done.heads_ref = bf16[32,144,128]{2,1,0:T(8,128)(2,1)} async-done(((bf16[32,144,128]{2,1,0:T(8,128)(2,1)}), bf16[32,144,128]{2,1,0:T(8,128)(2,1)}, u32[]{:S(2)}, u32[]{:S(2)}) %all-to-all-start) | async-done | bytes 1179680 | tf_op jit(solution)/shard_map/all_to_all | solution.py:397
  117.0 11.3 %attend.3 = bf16[16,96,128]{2,1,0:T(8,128)(2,1)} custom-call(s32[2]{0:T(128)} %pad_add_fusion.order_ref, bf16[32,144,128]{2,1,0:T(8,128)(2,1)} %all-to-all-done.heads_ref, bf16[2,1024,512]{2,1,0:T(8,128)(2,1)} %bitcast.12, bf16[2,1024,512]{2,1,0:T(8,128)(2,1)} %collective-permute-done.other_ref, ...), custom_call_target="tpu_custom_call", output_to_operand_aliasing={{}: (4, {})} | custom-call | flops 10000000000 | bytes 1000000 | tf_op jit(solution)/shard_map/attend/pallas_call | solution.py:303
  128.3 4.2 %all-to-all-start.3 = ((bf16[16,96,128]{2,1,0:T(8,128)(2,1)}), bf16[16,96,128]{2,1,0:T(8,128)(2,1)S(1)}, u32[]{:S(2)}, u32[]{:S(2)}) async-start(bf16[16,96,128]{2,1,0:T(8,128)(2,1)} %attend.3), calls=%async_computation.3 | async-start | bytes 786432 | tf_op jit(solution)/shard_map/all_to_all | solution.py:397
  132.5 0.0 copy-done.4
  132.6 0.6 pad.4.update_ref
  133.2 8.5 %all-to-all-done.3.heads_ref = bf16[16,96,128]{2,1,0:T(8,128)(2,1)S(1)} async-done(((bf16[16,96,128]{2,1,0:T(8,128)(2,1)}), bf16[16,96,128]{2,1,0:T(8,128)(2,1)S(1)}, u32[]{:S(2)}, u32[]{:S(2)}) %all-to-all-start.3) | async-done | bytes 393248 | tf_op jit(solution)/shard_map/all_to_all | solution.py:397
  141.7 0.8 copy-done.2
  142.4 12.3 %finish.1 = (bf16[4,64,768]{2,1,0:T(8,128)(2,1)}, f32[3,4,1536]{2,1,0:T(4,128)}) custom-call(bf16[16,96,128]{2,1,0:T(8,128)(2,1)} %copy-done.2, f32[256,768]{1,0:T(8,128)} %get-tuple-element.18.gate_ref, bf16[768,768]{1,0:T(8,128)(2,1)} %output_ref.5, bf16[768,3072]{1,0:T(8,128)(2,1)} %trans_in_ref.1, bf16[1536,768]{1,0:T(8,128)(2,1)} %trans_out_ref.1, ...), custom_call_target="tpu_custom_call" | custom-call | flops 8000000000 | bytes 10000000 | tf_op jit(solution)/shard_map/finish/pallas_call | solution.py:375
  (7 shorter events, 0.0 us)
Async XLA Ops:
  11.1 9.5 %copy-start.3 = (s32[1536]{0:T(1024)S(1)}, s32[1536]{0:T(1024)}, u32[]{:S(2)}) copy-start(s32[1536]{0:T(1024)} %param.19) | copy-start | bytes 18436
  11.1 38.1 %all-to-all-start.1 = ((bf16[32,64,512]{2,1,0:T(8,128)(2,1)}), bf16[32,64,512]{2,1,0:T(8,128)(2,1)S(1)}, u32[]{:S(2)}, u32[]{:S(2)}) async-start(bf16[32,64,512]{2,1,0:T(8,128)(2,1)} %bitcast.13), calls=%async_computation.1 | async-start | bytes 4194304 | tf_op jit(solution)/shard_map/all_to_all | solution.py:397
  49.1 11.8 %copy-start = (bf16[32,64,512]{2,1,0:T(8,128)(2,1)}, bf16[32,64,512]{2,1,0:T(8,128)(2,1)S(1)}, u32[]{:S(2)}) copy-start(bf16[32,64,512]{2,1,0:T(8,128)(2,1)S(1)} %all-to-all-done.1) | copy-start | bytes 6291460
  49.1 50.0 %collective-permute-start = (bf16[2,1024,512]{2,1,0:T(8,128)(2,1)S(1)}, bf16[2,1024,512]{2,1,0:T(8,128)(2,1)}, u32[]{:S(2)}, u32[]{:S(2)}) collective-permute-start(bf16[2,1024,512]{2,1,0:T(8,128)(2,1)S(1)} %bitcast.10), channel_id=1, source_target_pairs={{0,32},{32,0},{1,33},{33,1},{2,34},{34,2},{3,35},{35,3},{4,36},{36... | collective-permute-start | bytes 6291464 | tf_op jit(solution)/shard_map/ppermute | solution.py:414
  66.0 25.5 %all-to-all-start.2 = ((bf16[32,144,128]{2,1,0:T(8,128)(2,1)}), bf16[32,144,128]{2,1,0:T(8,128)(2,1)S(1)}, u32[]{:S(2)}, u32[]{:S(2)}) async-start(bf16[32,144,128]{2,1,0:T(8,128)(2,1)} %bitcast.15), calls=%async_computation.2 | async-start | bytes 2359296 | tf_op jit(solution)/shard_map/all_to_all | solution.py:397
  91.5 7.7 %copy-start.1 = (bf16[32,144,128]{2,1,0:T(8,128)(2,1)}, bf16[32,144,128]{2,1,0:T(8,128)(2,1)S(1)}, u32[]{:S(2)}) copy-start(bf16[32,144,128]{2,1,0:T(8,128)(2,1)S(1)} %all-to-all-done.2.heads_ref) | copy-start | bytes 3538948
  91.5 25.6 %all-to-all-start = ((bf16[32,144,128]{2,1,0:T(8,128)(2,1)}), bf16[32,144,128]{2,1,0:T(8,128)(2,1)}, u32[]{:S(2)}, u32[]{:S(2)}) async-start(bf16[32,144,128]{2,1,0:T(8,128)(2,1)} %bitcast.14), calls=%async_computation | async-start | bytes 2359296 | tf_op jit(solution)/shard_map/all_to_all | solution.py:397
  110.4 22.1 %copy-start.4 = (f32[128,3]{0,1:T(4,128)S(1)}, f32[128,3]{0,1:T(4,128)}, u32[]{:S(2)}) copy-start(f32[128,3]{0,1:T(4,128)} %param.33) | copy-start | bytes 4612
  128.3 13.3 %all-to-all-start.3 = ((bf16[16,96,128]{2,1,0:T(8,128)(2,1)}), bf16[16,96,128]{2,1,0:T(8,128)(2,1)S(1)}, u32[]{:S(2)}, u32[]{:S(2)}) async-start(bf16[16,96,128]{2,1,0:T(8,128)(2,1)} %attend.3), calls=%async_computation.3 | async-start | bytes 786432 | tf_op jit(solution)/shard_map/all_to_all | solution.py:397
  141.7 0.8 copy-start.2

commit v3 on v2

v3 whole, which is shorter than its diff:
```python
import functools

import jax
import jax.numpy as jnp
import numpy as np
from jax import lax
from jax.experimental import pallas as pl
from jax.experimental.pallas import tpu as pltpu
from jax.sharding import Mesh, PartitionSpec as P

ATOM_HEADS = 4
QUERY_BLOCK = 32
KEY_WINDOW = 128
NORM_EPSILON = 1e-05
MASKED_SCORE = -1000000000.0
LOG2E = 1.4426950408889634
F32 = jnp.float32
BF16 = jnp.bfloat16
VMEM_LIMIT = 60 * 1024 * 1024

TN = (((0,), (0,)), ((), ()))
NT = (((1,), (1,)), ((), ()))
NN = (((1,), (0,)), ((), ()))


def flat_row(ref):
    return jnp.concatenate([ref[i : i + 1, :] for i in range(ref.shape[0])], axis=1)


def mm(a, b, dims=NN):
    return lax.dot_general(a, b, dims, preferred_element_type=F32)


def norm_rows(inputs):
    row_mean = jnp.mean(inputs, axis=-1, keepdims=True)
    centered = inputs - row_mean
    variance = jnp.mean(centered * centered, axis=-1, keepdims=True)
    return centered * lax.rsqrt(variance + NORM_EPSILON)


def params():
    return pltpu.CompilerParams(vmem_limit_bytes=VMEM_LIMIT)


def pair_kernel(pair_ref, weight_ref, out_ref, center_s):
    rows, cols, width = pair_ref.shape
    heads = weight_ref.shape[0]

    @pl.when(pl.program_id(0) == 0)
    def _():
        same = lax.broadcasted_iota(jnp.int32, (width, width), 0) == lax.broadcasted_iota(jnp.int32, (width, width), 1)
        center_s[...] = (same.astype(F32) - 1.0 / width).astype(BF16)

    flat = pair_ref[...].reshape(rows * cols, width)
    centered = mm(center_s[...], flat, NT)
    variance = jnp.mean(centered * centered, axis=0, keepdims=True)
    top = mm(weight_ref[...], centered.astype(BF16))
    bias = top * (lax.rsqrt(variance + NORM_EPSILON) * LOG2E)
    for h in range(heads):
        out_ref[h] = bias[h : h + 1].reshape(rows, cols).astype(BF16)


def pair_bias(pair_rep, pair_weight):
    rows, cols, width = pair_rep.shape
    heads = pair_weight.shape[1]
    step = 16
    return pl.pallas_call(
        pair_kernel,
        grid=(rows // step,),
        in_specs=[
            pl.BlockSpec((step, cols, width), lambda i: (i, 0, 0)),
            pl.BlockSpec((heads, width), lambda i: (0, 0)),
        ],
        out_specs=pl.BlockSpec((heads, step, cols), lambda i: (0, i, 0)),
        out_shape=jax.ShapeDtypeStruct((heads, rows, cols), BF16),
        scratch_shapes=[pltpu.VMEM((width, width), BF16)],
        compiler_params=params(),
        cost_estimate=pl.CostEstimate(flops=10**10, bytes_accessed=10**7, transcendentals=0),
        name="pair_bias",
    )(pair_rep, pair_weight.T)


def split_three(value, order):
    first = value.astype(BF16).astype(F32)
    second = (value - first).astype(BF16).astype(F32)
    third = value - first - second
    terms = (first, second, third)
    return [terms[k] for k in order]


def atom_kernel(
    base, cond_ref, pos_ref, token_ref, pos_weight_ref, proj_ref, output_ref, to_token_ref,
    *refs,
):
    mid_ref, token_in_ref, query_s, key_s, val_s, mixed_s, pos_s, weight_s = refs[-8:]
    slots, width = cond_ref.shape
    tokens = token_in_ref.shape[1]
    head = width // ATOM_HEADS
    owner = flat_row(token_ref)
    count = jnp.sum((owner < tokens).astype(jnp.int32))

    @pl.when(pl.program_id(0) == 0)
    def _():
        pos_s[...] = jnp.zeros_like(pos_s)
        weight_s[...] = jnp.zeros_like(weight_s)
        for k, piece in enumerate(split_three(pos_weight_ref[...], (0, 0, 0, 1, 1, 2))):
            weight_s[8 * k : 8 * k + 3, :] = piece
        val_s[:, width:] = jnp.ones((slots, width), BF16)

    position = pos_ref[:, pl.ds(base + pl.program_id(0), 1), :].reshape(3, slots)
    for k, piece in enumerate(split_three(position, (0, 1, 2, 0, 1, 0))):
        pos_s[8 * k : 8 * k + 3, :] = piece
    act = cond_ref[...].astype(F32) + mm(pos_s[...].astype(BF16), weight_s[...].astype(BF16), TN)
    normed = norm_rows(act).astype(BF16)
    projected = mm(normed, proj_ref[...])
    query_s[...] = (projected[:, :width] * (head ** (-0.5) * LOG2E)).astype(BF16)
    key_s[...] = projected[:, width : 2 * width].astype(BF16)
    val_s[:, :width] = projected[:, 2 * width :].astype(BF16)
    stacked = ATOM_HEADS * QUERY_BLOCK
    of_row = lax.broadcasted_iota(jnp.int32, (stacked, width), 0) // QUERY_BLOCK
    of_lane = lax.broadcasted_iota(jnp.int32, (stacked, width), 1) // head
    own_head = of_row == of_lane
    lane = lax.broadcasted_iota(jnp.int32, (stacked, KEY_WINDOW), 1)
    blocks = slots // QUERY_BLOCK
    group = 16
    for first in range(0, blocks, group):
        starts = [
            min(max(b * QUERY_BLOCK - (KEY_WINDOW - QUERY_BLOCK) // 2, 0), slots - KEY_WINDOW)
            for b in range(first, first + group)
        ]
        scores = []
        for k, start in enumerate(starts):
            low = (first + k) * QUERY_BLOCK
            query = query_s[low : low + QUERY_BLOCK, :]
            query = jnp.concatenate([query] * ATOM_HEADS, axis=0)
            query = jnp.where(own_head, query, jnp.zeros_like(query))
            score = mm(query, key_s[start : start + KEY_WINDOW, :], NT)
            scores.append(jnp.where(lane < count - start, score, MASKED_SCORE))
        weights = [jnp.exp2(s - jnp.max(s, axis=-1, keepdims=True)).astype(BF16) for s in scores]
        for k, start in enumerate(starts):
            low = (first + k) * QUERY_BLOCK
            summed = mm(weights[k], val_s[start : start + KEY_WINDOW, :])
            mixed = jnp.where(own_head, summed[:, :width] / summed[:, width:], 0.0)
            mixed = mixed.reshape(ATOM_HEADS, QUERY_BLOCK, width).sum(axis=0)
            mixed_s[low : low + QUERY_BLOCK, :] = mixed.astype(BF16)
    mid = act + mm(mixed_s[...], output_ref[...])
    mid_ref[0] = mid
    feature = jnp.maximum(mm(mid.astype(BF16), to_token_ref[...]), 0.0).astype(BF16)
    onehot = lax.broadcasted_iota(jnp.int32, (tokens, slots), 0) == owner
    members = jnp.sum(onehot.astype(F32), axis=1, keepdims=True)
    token_in_ref[0] = mm(onehot.astype(BF16), feature) / members


def atom_stage(atom_cond, atom_pos, atom_token, pos_weight, atom_proj, atom_output, atom_to_token, tokens, base, samples, all_samples, mid):
    slots, width = atom_cond.shape
    channels = atom_to_token.shape[1]
    whole = lambda a: pl.BlockSpec(a.shape, lambda s: (0,) * a.ndim)
    atom_token = atom_token.reshape(slots // width, width)
    earlier = () if mid is None else (mid,)
    return pl.pallas_call(
        functools.partial(atom_kernel, base),
        grid=(samples,),
        in_specs=[
            whole(atom_cond),
            whole(atom_pos),
            whole(atom_token),
            whole(pos_weight),
            whole(atom_proj),
            whole(atom_output),
            whole(atom_to_token),
        ] + [pl.BlockSpec(memory_space=pl.ANY)] * len(earlier),
        input_output_aliases={7: 0} if earlier else {},
        out_specs=[
            pl.BlockSpec((1, slots, width), lambda s: (base + s, 0, 0)),
            pl.BlockSpec((1, tokens, channels), lambda s: (s, 0, 0)),
        ],
        out_shape=[
            jax.ShapeDtypeStruct((all_samples, slots, width), F32),
            jax.ShapeDtypeStruct((samples, tokens, channels), F32),
        ],
        scratch_shapes=[
            pltpu.VMEM((slots, width), BF16),
            pltpu.VMEM((slots, width), BF16),
            pltpu.VMEM((slots, 2 * width), BF16),
            pltpu.VMEM((slots, width), BF16),
            pltpu.VMEM((48, slots), F32),
            pltpu.VMEM((48, width), F32),
        ],
        compiler_params=params(),
        cost_estimate=pl.CostEstimate(flops=samples * 6 * 10**9, bytes_accessed=10**6, transcendentals=0),
        name="atom_stage",
    )(atom_cond, atom_pos, atom_token, pos_weight, atom_proj, atom_output, atom_to_token, *earlier)


def project_kernel(*refs):
    token_in_refs, (single_ref, ada_ref, proj_ref, heads_ref, gate_ref) = refs[:-5], refs[-5:]
    channels = proj_ref.shape[0]
    heads, triple, lanes = heads_ref.shape
    head = triple // 3
    conditioning = 1.0 + mm(single_ref[...], ada_ref[...])
    adapted = [(norm_rows(ref[...]) * conditioning[None]).astype(BF16).reshape(-1, channels) for ref in token_in_refs]
    adapted = jnp.concatenate(adapted, axis=0)
    for part in range(3):
        rows = mm(adapted, proj_ref[:, part * channels : (part + 1) * channels])
        if part == 0:
            rows = rows * (head ** (-0.5) * LOG2E)
        heads_ref[:, part * head : (part + 1) * head, :] = rows.T.astype(BF16).reshape(heads, head, lanes)
    gate_ref[...] = jax.nn.sigmoid(mm(adapted, proj_ref[:, 3 * channels :]))


def project(token_in, tok_single, ada_weight, tok_proj, heads):
    tokens, channels = tok_single.shape
    lanes = sum(x.shape[0] for x in token_in) * tokens
    head = channels // heads
    return pl.pallas_call(
        project_kernel,
        out_shape=[
            jax.ShapeDtypeStruct((heads, 3 * head, lanes), BF16),
            jax.ShapeDtypeStruct((lanes, channels), F32),
        ],
        compiler_params=params(),
        cost_estimate=pl.CostEstimate(flops=4 * 10**9, bytes_accessed=8 * 10**6, transcendentals=0),
        name="project",
    )(*token_in, tok_single, ada_weight, tok_proj)


def attend_kernel(last, order_ref, own_ref, *refs):
    refs, (out_ref, query_s, key_s, val_s) = refs[:-4], refs[-4:]
    heads_ref, refs = (refs[0], refs[1:]) if last else (own_ref, refs)
    bias_refs, earlier = refs[:4], refs[4:]
    sources, _, lanes = own_ref.shape
    samples, head, keys = key_s.shape
    tokens = lanes // samples
    width = val_s.shape[2]
    rows, cols = bias_refs[0].shape
    step = pl.program_id(0)
    mine = order_ref[0]
    half = 1 - order_ref[1] if last else order_ref[1]

    @pl.when(step == 0)
    def _():
        fill = jnp.zeros((width - head, lanes), F32)
        fill_v = jnp.where(lax.broadcasted_iota(jnp.int32, (width - head, lanes), 0) == 0, 1.0, 0.0)

        def turn(block, below):
            return jnp.concatenate([block.astype(F32), below], axis=0).T.astype(BF16)

        low = 0 if last else head
        for j in range(sources):
            query = turn(own_ref[j, :head, :], fill)
            val = turn(heads_ref[j, low + head :, :], fill_v)
            for s in range(samples):
                query_s[s, j * tokens : (j + 1) * tokens, :] = query[s * tokens : (s + 1) * tokens, :head]
                val_s[s, j * tokens : (j + 1) * tokens, :] = val[s * tokens : (s + 1) * tokens]
        for j in range(0, sources, 2):
            for s in range(samples):
                pair = [heads_ref[k, low : low + head, s * tokens : (s + 1) * tokens] for k in (j, j + 1)]
                key_s[s, :, j * tokens : (j + 2) * tokens] = jnp.concatenate(pair, axis=1)

    swapped = mine // 2 != half
    biases = [jnp.where(swapped, bias_refs[p + 2][...], bias_refs[p][...]).astype(F32) for p in range(2)]
    places = [pl.ds(pl.multiple_of((mine % 2 ^ p) * cols, cols), cols) for p in range(2)]
    lane = lax.broadcasted_iota(jnp.int32, (256, width), 1)
    results = []
    unit = 256
    jobs = [(r, s) for r in range(0, rows, unit) for s in range(samples)]

    def score(job):
        r, s = job
        query = query_s[s, pl.ds(pl.multiple_of(step * rows + r, unit), unit), :]
        return [mm(query, key_s[s, :, place]) + bias[r : r + unit] for place, bias in zip(places, biases)]

    def soften(job, scores):
        r, s = job
        top = jnp.max(jnp.maximum(*scores), axis=-1, keepdims=True)
        total = 0.0
        if last:
            before = earlier[0][s, r : r + unit]
            top_before = before[:, width - 1 :]
            top = jnp.maximum(top, top_before)
            total = before * jnp.exp2(top_before - top)
        return job, top, total, [jnp.exp2(x - top).astype(BF16) for x in scores]

    def gather(state):
        (r, s), top, total, weights = state
        for x, place in zip(weights, places):
            total = total + mm(x, val_s[s, place, :])
        if last:
            results.append(total / total[:, head : head + 1])
        else:
            out_ref[s, r : r + unit] = jnp.where(lane == width - 1, top, total)

    ahead, state = score(jobs[0]), None
    for n, job in enumerate(jobs):
        scores = ahead
        if n + 1 < len(jobs):
            ahead = score(jobs[n + 1])
        if state is not None:
            gather(state)
        state = soften(job, scores)
    gather(state)
    if last:
        for j in range(rows // tokens):
            u, low = j * tokens // unit * samples, j * tokens % unit
            block = jnp.concatenate([r[low : low + tokens] for r in results[u : u + samples]], axis=0)
            out_ref[j] = block.T[:head].astype(BF16)


def attend(order, own, biases, samples, far=None, earlier=None):
    sources, triple, lanes = own.shape
    head = triple // 3
    tokens = lanes // samples
    width = 128
    rows = 256
    total, cols = biases[0].shape
    last = earlier is not None
    whole = lambda a: pl.BlockSpec(a.shape, lambda i, *_: (0,) * a.ndim)
    bias_specs = [pl.BlockSpec((rows, cols), lambda i, *_: (i, 0))] * 4
    running = pl.BlockSpec((samples, rows, width), lambda i, *_: (0, i, 0))
    if last:
        args, in_specs = (own, far, *biases, earlier), [whole(own), whole(far)] + bias_specs + [running]
        out_specs = pl.BlockSpec((rows // tokens, head, lanes), lambda i, *_: (i, 0, 0))
        out_shape = jax.ShapeDtypeStruct((sources, head, lanes), BF16)
    else:
        args, in_specs = (own, *biases), [whole(own)] + bias_specs
        out_specs = running
        out_shape = jax.ShapeDtypeStruct((samples, total, width), F32)
    return pl.pallas_call(
        functools.partial(attend_kernel, last),
        grid_spec=pltpu.PrefetchScalarGridSpec(
            num_scalar_prefetch=1,
            grid=(total // rows,),
            in_specs=in_specs,
            out_specs=out_specs,
            scratch_shapes=[
                pltpu.VMEM((samples, total, head), BF16),
                pltpu.VMEM((samples, head, total), BF16),
                pltpu.VMEM((samples, total, width), BF16),
            ],
        ),
        out_shape=out_shape,
        compiler_params=params(),
        cost_estimate=pl.CostEstimate(flops=10**10, bytes_accessed=10**6, transcendentals=0),
        name="attend",
    )(order, *args)


def finish_kernel(
    heads_ref, gate_ref, output_ref, to_atom_ref, mid_ref, owner_ref, update_ref, trans_in_hbm, trans_out_hbm, *refs
):
    token_in_refs, (token_out_ref, atom_ref, feature_s, trans_in_ref, trans_out_ref, sems) = refs[:-6], refs[-6:]
    samples, tokens, channels = token_out_ref.shape
    step = pl.program_id(0)

    @pl.when(step == 0)
    def _():
        load_in = pltpu.make_async_copy(trans_in_hbm, trans_in_ref, sems.at[0])
        load_out = pltpu.make_async_copy(trans_out_hbm, trans_out_ref, sems.at[1])
        load_in.start()
        load_out.start()
        lanes = heads_ref.shape[2]
        attended = heads_ref[...].reshape(channels, lanes).astype(F32).T
        gated = (gate_ref[...] * attended).astype(BF16)
        token_in = jnp.concatenate([ref[...].reshape(-1, channels) for ref in token_in_refs], axis=0)
        after = token_in + mm(gated, output_ref[...])
        hidden_in = norm_rows(after).astype(BF16)
        hidden_width = trans_out_ref.shape[0]
        load_in.wait()
        left = mm(hidden_in, trans_in_ref[:, :hidden_width])
        right = mm(hidden_in, trans_in_ref[:, hidden_width:])
        hidden = (jax.nn.silu(left) * right).astype(BF16)
        load_out.wait()
        result = (after + mm(hidden, trans_out_ref[...])).astype(BF16)
        token_out_ref[...] = result.reshape(samples, tokens, channels)
        feature_s[...] = mm(result, to_atom_ref[...]).astype(BF16).reshape(feature_s.shape)

    owner = flat_row(owner_ref)
    slots = owner.shape[1]
    onehot = (lax.broadcasted_iota(jnp.int32, (tokens, slots), 0) == owner).astype(BF16)
    final = norm_rows(mid_ref[0] + mm(onehot, feature_s[step], TN))
    weight = update_ref[...]
    high = final.astype(BF16)
    low = (final - high.astype(F32)).astype(BF16)
    first = weight.astype(BF16)
    second = (weight - first.astype(F32)).astype(BF16)
    update = mm(first, high, NT) + (mm(second, high, NT) + mm(first, low, NT))
    update = update * (owner < tokens).astype(F32)
    atom_ref[:, pl.ds(step, 1), :] = update.reshape(3, 1, slots)


def finish(
    heads, gate, tok_output, transition_in, transition_out, token_to_atom, atom_mid, atom_token, pos_update, token_in
):
    each, tokens, channels = token_in[0].shape
    samples, slots, width = atom_mid.shape
    owner = atom_token.reshape(slots // width, width)
    turned = pos_update.T
    whole = lambda a: pl.BlockSpec(a.shape, lambda s: (0,) * a.ndim)
    args = (heads, gate, tok_output, token_to_atom)
    return pl.pallas_call(
        finish_kernel,
        grid=(samples,),
        in_specs=[whole(a) for a in args]
        + [pl.BlockSpec((1, slots, width), lambda s: (s, 0, 0)), whole(owner), whole(turned)]
        + [pl.BlockSpec(memory_space=pl.ANY)] * 2
        + [whole(a) for a in token_in],
        out_specs=[
            pl.BlockSpec((samples, tokens, channels), lambda s: (0, 0, 0)),
            pl.BlockSpec((3, samples, slots), lambda s: (0, 0, 0)),
        ],
        out_shape=[
            jax.ShapeDtypeStruct((samples, tokens, channels), BF16),
            jax.ShapeDtypeStruct((3, samples, slots), F32),
        ],
        scratch_shapes=[
            pltpu.VMEM((samples, tokens, width), BF16),
            pltpu.VMEM(transition_in.shape, BF16),
            pltpu.VMEM(transition_out.shape, BF16),
            pltpu.SemaphoreType.DMA((2,)),
        ],
        compiler_params=params(),
        cost_estimate=pl.CostEstimate(flops=8 * 10**9, bytes_accessed=10**7, transcendentals=0),
        name="finish",
    )(*args, atom_mid, owner, turned, transition_in, transition_out, *token_in)


def swap(x, axis):
    return lax.ppermute(x, axis, [(0, 1), (1, 0)])


def exchange(x, axes):
    return lax.all_to_all(x, axes, 0, 0, tiled=True)


def per_device(
    atom_cond, atom_pos, atom_token, pos_weight, atom_proj, atom_output, atom_to_token, tok_single, ada_weight,
    pair_rep, pair_weight, tok_proj, tok_output, transition_in, transition_out, token_to_atom, pos_update,
):
    tokens, channels = tok_single.shape
    heads = pair_weight.shape[1]
    samples = atom_pos.shape[0]
    halves = 2
    each = samples // halves
    pos = jnp.swapaxes(atom_pos, 0, 1)
    order = jnp.stack([lax.axis_index("xlo") * 2 + lax.axis_index("core"), lax.axis_index("xhi")]).astype(jnp.int32)
    own_bias = exchange(pair_bias(pair_rep, pair_weight), ("y", "z"))
    own_bias = own_bias.reshape(heads * tokens, own_bias.shape[2])
    inputs = []
    mid = None
    for k in range(halves):
        mid, token_in = atom_stage(
            atom_cond, pos, atom_token, pos_weight, atom_proj, atom_output, atom_to_token, tokens, k * each, each,
            samples, mid,
        )
        inputs.append(token_in)
    own_bias, inputs[1] = lax.optimization_barrier((own_bias, inputs[1]))
    across = swap(own_bias, "xlo")
    near = swap(own_bias, "core")
    qkv, gate = project(inputs, tok_single, ada_weight, tok_proj, heads)
    own = exchange(qkv, ("y", "z"))
    far = swap(own[:, channels // heads :], "xhi")
    biases = (own_bias, near, across, swap(across, "core"))
    running = attend(order, own, biases, samples)
    attended = attend(order, own, biases, samples, far, running)
    attended = exchange(attended, ("y", "z"))
    token_out, update = finish(
        attended, gate, tok_output, transition_in, transition_out, token_to_atom, mid, atom_token, pos_update, inputs
    )
    return token_out, jnp.swapaxes(update, 0, 1)


def solution(mesh):
    fine = Mesh(mesh.devices.reshape(2, 2, 2, 4, 4), ("xlo", "core", "xhi", "y", "z"))
    tok = ("xhi", "y", "z")
    sample = ("xlo", "core")
    return jax.shard_map(
        per_device,
        mesh=fine,
        in_specs=(
            P(tok, None), P(sample, None, tok), P(tok), P(), P(), P(), P(), P(tok, None), P(),
            P(tok, sample, None), P(), P(), P(), P(), P(), P(), P(),
        ),
        out_specs=(P(sample, tok, None), P(sample, None, tok)),
        check_vma=False,
    )
```

time: 155 us -> 126 us (0.81)
  waiting for transfers between devices: 45.8 us -> 22.9 us
  blocking collectives: 0 us -> 13.7 us
  Pallas kernels: 78.2 us -> 67.5 us
  starting transfers between devices: 27.4 us -> 20 us
  local copies, waits for them, and re-layouts: 1.96 us -> 0.08 us
    all_to_all x4 -> x2, waiting for transfers between devices: 45.8 us -> 7.27 us  [exchange(): return lax.all_to_all(x, axes, 0, 0, tiled=True)]
    ppermute x1 -> x4, waiting for transfers between devices: 0.01 us -> 15.6 us  [swap(): return lax.ppermute(x, axis, [(0, 1), (1, 0)])]
    all_to_all x0 -> x1, blocking collectives: none -> 13.7 us  [exchange(): return lax.all_to_all(x, axes, 0, 0, tiled=True)]
    all_to_all x4 -> x2, starting transfers between devices: 27.4 us -> 15.3 us  [exchange(): return lax.all_to_all(x, axes, 0, 0, tiled=True)]
    pallas_call x4 -> x3, Pallas kernels: 32.7 us -> 27.5 us  [the longest x2 21.7 us: attend(): pl.pallas_call(functools.partial(attend_kernel, last), grid_spec=pltpu.Pr...]
    ppermute x1 -> x4, starting transfers between devices: 0.01 us -> 4.65 us  [swap(): return lax.ppermute(x, axis, [(0, 1), (1, 0)])]
    pallas_call x1, Pallas kernels: 10.4 us -> 7.41 us  [pair_bias(): pl.pallas_call(pair_kernel, grid=(rows // step,), in_specs=[pl.BlockSpec(...]
    pallas_call x2, Pallas kernels: 22.8 us -> 20.5 us  [atom_stage(): pl.pallas_call(functools.partial(atom_kernel, base), grid=(samples,), in_...]
  transfers between devices with their start and end apart: 5 -> 6, of which waited for: 4 -> 3; matrix products, arithmetic and copies ran while one was open for 1% -> 1% of each run, Pallas kernels for 29% -> 29%
where the time goes in v3:
time: 126 us
  Pallas kernels  67.5 us (54%)
  waiting for transfers between devices  22.9 us (18%)
  starting transfers between devices  20 us (16%)
  blocking collectives  13.7 us (11%)
    pallas_call x2, Pallas kernels, attend(): pl.pallas_call(functools.partial(attend_kernel, last), grid_spec=pltpu.Pr...  21.7 us
    pallas_call x2, Pallas kernels, atom_stage(): pl.pallas_call(functools.partial(atom_kernel, base), grid=(samples,), in_...  20.5 us
    ppermute x4, waiting for transfers between devices, swap(): return lax.ppermute(x, axis, [(0, 1), (1, 0)])  15.6 us
    all_to_all x2, starting transfers between devices, exchange(): return lax.all_to_all(x, axes, 0, 0, tiled=True)  15.3 us
    all_to_all x1, blocking collectives, exchange(): return lax.all_to_all(x, axes, 0, 0, tiled=True)  13.7 us
    pallas_call x1, Pallas kernels, finish(): pl.pallas_call(finish_kernel, grid=(samples,), in_specs=[whole(a) for a i...  12 us
    pallas_call x1, Pallas kernels, pair_bias(): pl.pallas_call(pair_kernel, grid=(rows // step,), in_specs=[pl.BlockSpec(...  7.41 us
    all_to_all x2, waiting for transfers between devices, exchange(): return lax.all_to_all(x, axes, 0, 0, tiled=True)  7.27 us
  transfers between devices with their start and end apart: 6, of which 3 were waited for; matrix products, arithmetic and copies ran while one was open for 1% of the time, Pallas kernels for 29%

profile of v3, /device:TPU:0, one launch (start us, length us, event | category | flops | bytes accessed | tf_op | source)
XLA Modules:
  0.0 125.7 jit_solution(7675661552885077061)
XLA Ops:
  0.6 7.4 %pair_bias.1 = bf16[16,64,512]{2,1,0:T(8,128)(2,1)} custom-call(bf16[64,512,128]{2,1,0:T(8,128)(2,1)} %pair_ref.1, bf16[16,128]{1,0:T(8,128)(2,1)} %bitcast.17), custom_call_target="tpu_custom_call" | custom-call | flops 10000000000 | bytes 10000000 | tf_op jit(solution)/shard_map/pair_bias/pallas_call | solution.py:67
  8.0 8.1 %all-to-all-start = ((bf16[16,64,512]{2,1,0:T(8,128)(2,1)}), bf16[16,64,512]{2,1,0:T(8,128)(2,1)S(1)}, u32[]{:S(2)}, u32[]{:S(2)}) async-start(bf16[16,64,512]{2,1,0:T(8,128)(2,1)} %pair_bias.1), calls=%async_computation | async-start | bytes 2097152 | tf_op jit(solution)/shard_map/all_to_all | solution.py:432
  16.2 10.2 %atom_stage.2 = (f32[4,1536,128]{2,1,0:T(8,128)}, f32[2,64,768]{2,1,0:T(8,128)}) custom-call(bf16[1536,128]{1,0:T(8,128)(2,1)} %cond_ref.3, f32[3,4,1536]{2,1,0:T(4,128)} %bitcast.12, s32[12,128]{1,0:T(8,128)} %bitcast.14, f32[3,128]{1,0:T(4,128)} %pos_weight_ref.3, bf16[128,384]{1,0:T(8,128)(2,1)} %proj_ref.3, bf16[128,128]{1,0:T(8,128)(2,1)} %output_ref.4, ...), custom_call_target="tpu_custom_call" | custom-call | flops 12000000000 | bytes 1000000 | tf_op jit(solution)/shard_map/atom_stage/pallas_call | solution.py:160
  26.4 10.3 %atom_stage.3 = (f32[4,1536,128]{2,1,0:T(8,128)}, f32[2,64,768]{2,1,0:T(8,128)}) custom-call(bf16[1536,128]{1,0:T(8,128)(2,1)} %cond_ref.3, f32[3,4,1536]{2,1,0:T(4,128)} %bitcast.13, s32[12,128]{1,0:T(8,128)} %bitcast.15, f32[3,128]{1,0:T(4,128)} %pos_weight_ref.3, bf16[128,384]{1,0:T(8,128)(2,1)} %proj_ref.3, ...), custom_call_target="tpu_custom_call", output_to_operand_aliasing={{0}: (7, {})} | custom-call | flops 12000000000 | bytes 1000000 | tf_op jit(solution)/shard_map/atom_stage/pallas_call | solution.py:160
  36.7 0.0 all-to-all-done
  36.7 1.6 %collective-permute-start.2 = (bf16[1024,512]{1,0:T(8,128)(2,1)S(1)}, bf16[1024,512]{1,0:T(8,128)(2,1)}, u32[]{:S(2)}, u32[]{:S(2)}) collective-permute-start(bf16[1024,512]{1,0:T(8,128)(2,1)S(1)} %bitcast.8), channel_id=1, source_target_pairs={{0,64},{64,0},{1,65},{65,1},{2,66},{66,2},{3,67},{67,3},{4,68},{68... | collective-permute-start | bytes 3145736 | tf_op jit(solution)/shard_map/ppermute | solution.py:428
  38.3 5.8 %project.1 = (bf16[16,144,256]{2,1,0:T(8,128)(2,1)}, f32[256,768]{1,0:T(8,128)}) custom-call(f32[2,64,768]{2,1,0:T(8,128)} %get-tuple-element.12.refs_0_, f32[2,64,768]{2,1,0:T(8,128)} %get-tuple-element.15.refs_1_, bf16[64,768]{1,0:T(8,128)(2,1)} %refs_2_.1, bf16[768,768]{1,0:T(8,128)(2,1)} %refs_3_.1, bf16[768,3072]{1,0:T(8,128)(2,1)} %refs_4_.1), custom_call_target="tpu_custom_call" | custom-call | flops 4000000000 | bytes 8000000 | tf_op jit(solution)/shard_map/project/pallas_call | solution.py:215
  44.1 7.2 %all-to-all-start.1 = ((bf16[16,144,256]{2,1,0:T(8,128)(2,1)}), bf16[16,144,256]{2,1,0:T(8,128)(2,1)S(1)}, u32[]{:S(2)}, u32[]{:S(2)}) async-start(bf16[16,144,256]{2,1,0:T(8,128)(2,1)} %get-tuple-element.16), calls=%async_computation.1 | async-start | bytes 2359296 | tf_op jit(solution)/shard_map/all_to_all | solution.py:432
  51.4 0.0 copy-done.1
  51.4 0.1 collective-permute-start.1
  51.5 10.1 %collective-permute-done.2.refs_2_.refs_3_ = bf16[1024,512]{1,0:T(8,128)(2,1)} collective-permute-done((bf16[1024,512]{1,0:T(8,128)(2,1)S(1)}, bf16[1024,512]{1,0:T(8,128)(2,1)}, u32[]{:S(2)}, u32[]{:S(2)}) %collective-permute-start.2) | collective-permute-done | bytes 1048608 | tf_op jit(solution)/shard_map/ppermute | solution.py:428
  61.5 0.0 collective-permute-start.3
  61.5 0.6 pad_add_fusion.order_ref
  62.2 7.3 %all-to-all-done.1.own_ref = bf16[16,144,256]{2,1,0:T(8,128)(2,1)S(1)} async-done(((bf16[16,144,256]{2,1,0:T(8,128)(2,1)}), bf16[16,144,256]{2,1,0:T(8,128)(2,1)S(1)}, u32[]{:S(2)}, u32[]{:S(2)}) %all-to-all-start.1) | async-done | bytes 1179680 | tf_op jit(solution)/shard_map/all_to_all | solution.py:432
  69.4 0.1 slice.4
  69.5 3.0 %collective-permute-start = (bf16[16,96,256]{2,1,0:T(8,128)(2,1)S(1)}, bf16[16,96,256]{2,1,0:T(8,128)(2,1)}, u32[]{:S(2)}, u32[]{:S(2)}) collective-permute-start(bf16[16,96,256]{2,1,0:T(8,128)(2,1)S(1)} %slice.4), channel_id=1, source_target_pairs={{0,16},{16,0},{1,17},{17,1},{2,18},{18,2},{3,19},{19,3},{4,20},{20... | collective-permute-start | bytes 2359304 | tf_op jit(solution)/shard_map/ppermute | solution.py:428
  72.5 0.0 collective-permute-done.1.refs_1_.refs_2_
  72.5 0.0 collective-permute-done.3.refs_3_.refs_4_
  72.5 0.0 copy-done
  72.5 9.9 %attend.2.refs_5_ = f32[4,1024,128]{2,1,0:T(8,128)} custom-call(s32[2]{0:T(128)} %pad_add_fusion.order_ref, bf16[16,144,256]{2,1,0:T(8,128)(2,1)} %copy-done, bf16[1024,512]{1,0:T(8,128)(2,1)} %bitcast.10, bf16[1024,512]{1,0:T(8,128)(2,1)} %collective-permute-done.1.refs_1_.refs_2_, bf16[1024,512]{1,0:T(8,128)(2,1)} %collective-permute-done.2.refs_2_.refs_3_, ...), custom_call_target="tpu_custom_call" | custom-call | flops 10000000000 | bytes 1000000 | tf_op jit(solution)/shard_map/attend/pallas_call | solution.py:328
  82.4 5.5 %collective-permute-done.refs_0_ = bf16[16,96,256]{2,1,0:T(8,128)(2,1)} collective-permute-done((bf16[16,96,256]{2,1,0:T(8,128)(2,1)S(1)}, bf16[16,96,256]{2,1,0:T(8,128)(2,1)}, u32[]{:S(2)}, u32[]{:S(2)}) %collective-permute-start) | collective-permute-done | bytes 786464 | tf_op jit(solution)/shard_map/ppermute | solution.py:428
  87.9 11.8 %attend.3 = bf16[16,48,256]{2,1,0:T(8,128)(2,1)} custom-call(s32[2]{0:T(128)} %pad_add_fusion.order_ref, bf16[16,144,256]{2,1,0:T(8,128)(2,1)} %copy-done, bf16[16,96,256]{2,1,0:T(8,128)(2,1)} %collective-permute-done.refs_0_, bf16[1024,512]{1,0:T(8,128)(2,1)} %bitcast.11, bf16[1024,512]{1,0:T(8,128)(2,1)} %collective-permute-done.1.refs_1_.refs_2_, ...), custom_call_target="tpu_custom_call" | custom-call | flops 10000000000 | bytes 1000000 | tf_op jit(solution)/shard_map/attend/pallas_call | solution.py:328
  99.7 13.7 %all_to_all.15.heads_ref = bf16[16,48,256]{2,1,0:T(8,128)(2,1)} all-to-all(bf16[16,48,256]{2,1,0:T(8,128)(2,1)} %attend.3), channel_id=1, replica_groups=mesh['xlo'=2,'core'=2,'xhi'=2,'y'=4,'z'=4] {'y','z'}, dimensions={0} | all-to-all | bytes 786432 | tf_op jit(solution)/shard_map/all_to_all | solution.py:432
  113.5 12.0 %finish.1 = (bf16[4,64,768]{2,1,0:T(8,128)(2,1)}, f32[3,4,1536]{2,1,0:T(4,128)}) custom-call(bf16[16,48,256]{2,1,0:T(8,128)(2,1)} %all_to_all.15.heads_ref, f32[256,768]{1,0:T(8,128)} %get-tuple-element.18.gate_ref, bf16[768,768]{1,0:T(8,128)(2,1)} %output_ref.5, bf16[768,128]{1,0:T(8,128)(2,1)} %to_atom_ref.1, f32[4,1536,128]{2,1,0:T(8,128)} %get-tuple-element.19.mid_ref, ...), custom_call_target="tpu_custom_call" | custom-call | flops 8000000000 | bytes 10000000 | tf_op jit(solution)/shard_map/finish/pallas_call | solution.py:400
  (2 shorter events, 0.0 us)
Async XLA Ops:
  8.0 28.7 %all-to-all-start = ((bf16[16,64,512]{2,1,0:T(8,128)(2,1)}), bf16[16,64,512]{2,1,0:T(8,128)(2,1)S(1)}, u32[]{:S(2)}, u32[]{:S(2)}) async-start(bf16[16,64,512]{2,1,0:T(8,128)(2,1)} %pair_bias.1), calls=%async_computation | async-start | bytes 2097152 | tf_op jit(solution)/shard_map/all_to_all | solution.py:432
  36.7 14.6 %copy-start.1 = (bf16[16,64,512]{2,1,0:T(8,128)(2,1)}, bf16[16,64,512]{2,1,0:T(8,128)(2,1)S(1)}, u32[]{:S(2)}) copy-start(bf16[16,64,512]{2,1,0:T(8,128)(2,1)S(1)} %all-to-all-done) | copy-start | bytes 3145732
  36.7 24.8 %collective-permute-start.2 = (bf16[1024,512]{1,0:T(8,128)(2,1)S(1)}, bf16[1024,512]{1,0:T(8,128)(2,1)}, u32[]{:S(2)}, u32[]{:S(2)}) collective-permute-start(bf16[1024,512]{1,0:T(8,128)(2,1)S(1)} %bitcast.8), channel_id=1, source_target_pairs={{0,64},{64,0},{1,65},{65,1},{2,66},{66,2},{3,67},{67,3},{4,68},{68... | collective-permute-start | bytes 3145736 | tf_op jit(solution)/shard_map/ppermute | solution.py:428
  44.1 25.3 %all-to-all-start.1 = ((bf16[16,144,256]{2,1,0:T(8,128)(2,1)}), bf16[16,144,256]{2,1,0:T(8,128)(2,1)S(1)}, u32[]{:S(2)}, u32[]{:S(2)}) async-start(bf16[16,144,256]{2,1,0:T(8,128)(2,1)} %get-tuple-element.16), calls=%async_computation.1 | async-start | bytes 2359296 | tf_op jit(solution)/shard_map/all_to_all | solution.py:432
  51.4 21.1 %collective-permute-start.1 = (bf16[1024,512]{1,0:T(8,128)(2,1)S(1)}, bf16[1024,512]{1,0:T(8,128)(2,1)}, u32[]{:S(2)}, u32[]{:S(2)}) collective-permute-start(bf16[1024,512]{1,0:T(8,128)(2,1)S(1)} %bitcast.9), channel_id=1, source_target_pairs={{0,32},{32,0},{1,33},{33,1},{2,34},{34,2},{3,35},{35,3},{4,36},{36... | collective-permute-start | bytes 3145736 | tf_op jit(solution)/shard_map/ppermute | solution.py:428
  61.5 11.0 %collective-permute-start.3 = (bf16[1024,512]{1,0:T(8,128)(2,1)}, bf16[1024,512]{1,0:T(8,128)(2,1)}, u32[]{:S(2)}, u32[]{:S(2)}) collective-permute-start(bf16[1024,512]{1,0:T(8,128)(2,1)} %collective-permute-done.2.refs_2_.refs_3_), channel_id=1, source_target_pairs={{0,32},{32,0},{1,33},{33,1},{2,34},{34,2},{3,35},{35,3},{4,36},{36... | collective-permute-start | bytes 3145736 | tf_op jit(solution)/shard_map/ppermute | solution.py:428
  69.4 3.1 %copy-start = (bf16[16,144,256]{2,1,0:T(8,128)(2,1)}, bf16[16,144,256]{2,1,0:T(8,128)(2,1)S(1)}, u32[]{:S(2)}) copy-start(bf16[16,144,256]{2,1,0:T(8,128)(2,1)S(1)} %all-to-all-done.1.own_ref) | copy-start | bytes 3538948
  69.5 18.4 %collective-permute-start = (bf16[16,96,256]{2,1,0:T(8,128)(2,1)S(1)}, bf16[16,96,256]{2,1,0:T(8,128)(2,1)}, u32[]{:S(2)}, u32[]{:S(2)}) collective-permute-start(bf16[16,96,256]{2,1,0:T(8,128)(2,1)S(1)} %slice.4), channel_id=1, source_target_pairs={{0,16},{16,0},{1,17},{17,1},{2,18},{18,2},{3,19},{19,3},{4,20},{20... | collective-permute-start | bytes 2359304 | tf_op jit(solution)/shard_map/ppermute | solution.py:428

commit v4 on v3

--- a/solution.py
+++ b/solution.py
@@ -16,7 +16,10 @@
 LOG2E = 1.4426950408889634
 F32 = jnp.float32
 BF16 = jnp.bfloat16
-VMEM_LIMIT = 60 * 1024 * 1024
+VMEM_LIMIT = 117 * 512 * 1024
+PAIR_VMEM_LIMIT = 60 * 1024 * 1024
+ATTEND_VMEM_LIMIT = 44 * 1024 * 1024
+FINISH_VMEM_LIMIT = 52 * 1024 * 1024
 
 TN = (((0,), (0,)), ((), ()))
 NT = (((1,), (1,)), ((), ()))
@@ -38,8 +41,8 @@
     return centered * lax.rsqrt(variance + NORM_EPSILON)
 
 
-def params():
-    return pltpu.CompilerParams(vmem_limit_bytes=VMEM_LIMIT)
+def params(limit=VMEM_LIMIT):
+    return pltpu.CompilerParams(vmem_limit_bytes=limit)
 
 
 def pair_kernel(pair_ref, weight_ref, out_ref, center_s):
@@ -63,7 +66,7 @@
 def pair_bias(pair_rep, pair_weight):
     rows, cols, width = pair_rep.shape
     heads = pair_weight.shape[1]
-    step = 16
+    step = 32
     return pl.pallas_call(
         pair_kernel,
         grid=(rows // step,),
@@ -74,7 +77,7 @@
         out_specs=pl.BlockSpec((heads, step, cols), lambda i: (0, i, 0)),
         out_shape=jax.ShapeDtypeStruct((heads, rows, cols), BF16),
         scratch_shapes=[pltpu.VMEM((width, width), BF16)],
-        compiler_params=params(),
+        compiler_params=params(PAIR_VMEM_LIMIT),
         cost_estimate=pl.CostEstimate(flops=10**10, bytes_accessed=10**7, transcendentals=0),
         name="pair_bias",
     )(pair_rep, pair_weight.T)
@@ -89,25 +92,31 @@
 
 
 def atom_kernel(
-    base, cond_ref, pos_ref, token_ref, pos_weight_ref, proj_ref, output_ref, to_token_ref,
-    *refs,
+    cond_ref, pos_ref, token_ref, pos_weight_ref, proj_ref, output_ref, to_token_ref, single_ref, ada_hbm, tok_proj_hbm,
+    mid_ref, token_in_ref, heads_ref, adapted_ref,
+    query_s, key_s, val_s, mixed_s, pos_s, weight_s, token_s, ada_ref, tok_proj_ref, sems,
 ):
-    mid_ref, token_in_ref, query_s, key_s, val_s, mixed_s, pos_s, weight_s = refs[-8:]
     slots, width = cond_ref.shape
-    tokens = token_in_ref.shape[1]
+    tokens, channels = token_in_ref.shape[1:]
+    heads, triple, lanes = heads_ref.shape
+    sample = pl.program_id(0)
+    load_ada = pltpu.make_async_copy(ada_hbm, ada_ref, sems.at[0])
+    load_proj = pltpu.make_async_copy(tok_proj_hbm.at[:, pl.ds(0, 3 * channels)], tok_proj_ref, sems.at[1])
     head = width // ATOM_HEADS
     owner = flat_row(token_ref)
     count = jnp.sum((owner < tokens).astype(jnp.int32))
 
-    @pl.when(pl.program_id(0) == 0)
+    @pl.when(sample == 0)
     def _():
+        load_ada.start()
+        load_proj.start()
         pos_s[...] = jnp.zeros_like(pos_s)
         weight_s[...] = jnp.zeros_like(weight_s)
         for k, piece in enumerate(split_three(pos_weight_ref[...], (0, 0, 0, 1, 1, 2))):
             weight_s[8 * k : 8 * k + 3, :] = piece
         val_s[:, width:] = jnp.ones((slots, width), BF16)
 
-    position = pos_ref[:, pl.ds(base + pl.program_id(0), 1), :].reshape(3, slots)
+    position = pos_ref[:, pl.ds(sample, 1), :].reshape(3, slots)
     for k, piece in enumerate(split_three(position, (0, 1, 2, 0, 1, 0))):
         pos_s[8 * k : 8 * k + 3, :] = piece
     act = cond_ref[...].astype(F32) + mm(pos_s[...].astype(BF16), weight_s[...].astype(BF16), TN)
@@ -148,35 +157,52 @@
     feature = jnp.maximum(mm(mid.astype(BF16), to_token_ref[...]), 0.0).astype(BF16)
     onehot = lax.broadcasted_iota(jnp.int32, (tokens, slots), 0) == owner
     members = jnp.sum(onehot.astype(F32), axis=1, keepdims=True)
-    token_in_ref[0] = mm(onehot.astype(BF16), feature) / members
-
-
-def atom_stage(atom_cond, atom_pos, atom_token, pos_weight, atom_proj, atom_output, atom_to_token, tokens, base, samples, all_samples, mid):
+    token_in = mm(onehot.astype(BF16), feature) / members
+    token_in_ref[0] = token_in
+    token_s[pl.ds(pl.multiple_of(sample * tokens, tokens), tokens), :] = norm_rows(token_in)
+
+    @pl.when(sample == pl.num_programs(0) - 1)
+    def _():
+        load_ada.wait()
+        load_proj.wait()
+        conditioning = 1.0 + mm(single_ref[...], ada_ref[...])
+        normed_tokens = token_s[...].reshape(lanes // tokens, tokens, channels)
+        adapted = (normed_tokens * conditioning[None]).astype(BF16).reshape(lanes, channels)
+        adapted_ref[...] = adapted
+        size = triple // 3
+        for part in range(3):
+            rows = mm(adapted, tok_proj_ref[:, part * channels : (part + 1) * channels])
+            if part == 0:
+                rows = rows * (size ** (-0.5) * LOG2E)
+            heads_ref[:, part * size : (part + 1) * size, :] = rows.T.astype(BF16).reshape(heads, size, lanes)
+
+
+def atom_stage(
+    atom_cond, atom_pos, atom_token, pos_weight, atom_proj, atom_output, atom_to_token, tok_single, ada_weight, tok_proj, heads
+):
+    samples = atom_pos.shape[1]
     slots, width = atom_cond.shape
-    channels = atom_to_token.shape[1]
+    tokens, channels = tok_single.shape
+    lanes = samples * tokens
+    triple = 3 * channels // heads
     whole = lambda a: pl.BlockSpec(a.shape, lambda s: (0,) * a.ndim)
     atom_token = atom_token.reshape(slots // width, width)
-    earlier = () if mid is None else (mid,)
+    args = (atom_cond, atom_pos, atom_token, pos_weight, atom_proj, atom_output, atom_to_token, tok_single)
     return pl.pallas_call(
-        functools.partial(atom_kernel, base),
+        atom_kernel,
         grid=(samples,),
-        in_specs=[
-            whole(atom_cond),
-            whole(atom_pos),
-            whole(atom_token),
-            whole(pos_weight),
-            whole(atom_proj),
-            whole(atom_output),
-            whole(atom_to_token),
-        ] + [pl.BlockSpec(memory_space=pl.ANY)] * len(earlier),
-        input_output_aliases={7: 0} if earlier else {},
+        in_specs=[whole(a) for a in args] + [pl.BlockSpec(memory_space=pl.ANY)] * 2,
         out_specs=[
-            pl.BlockSpec((1, slots, width), lambda s: (base + s, 0, 0)),
+            pl.BlockSpec((1, slots, width), lambda s: (s, 0, 0)),
             pl.BlockSpec((1, tokens, channels), lambda s: (s, 0, 0)),
+            pl.BlockSpec((heads, triple, lanes), lambda s: (0, 0, 0)),
+            pl.BlockSpec((lanes, channels), lambda s: (0, 0)),
         ],
         out_shape=[
-            jax.ShapeDtypeStruct((all_samples, slots, width), F32),
+            jax.ShapeDtypeStruct((samples, slots, width), F32),
             jax.ShapeDtypeStruct((samples, tokens, channels), F32),
+            jax.ShapeDtypeStruct((heads, triple, lanes), BF16),
+            jax.ShapeDtypeStruct((lanes, channels), BF16),
         ],
         scratch_shapes=[
             pltpu.VMEM((slots, width), BF16),
@@ -185,43 +211,49 @@
             pltpu.VMEM((slots, width), BF16),
             pltpu.VMEM((48, slots), F32),
             pltpu.VMEM((48, width), F32),
+            pltpu.VMEM((lanes, channels), F32),
+            pltpu.VMEM((channels, channels), BF16),
+            pltpu.VMEM((channels, 3 * channels), BF16),
+            pltpu.SemaphoreType.DMA((2,)),
         ],
         compiler_params=params(),
-        cost_estimate=pl.CostEstimate(flops=samples * 6 * 10**9, bytes_accessed=10**6, transcendentals=0),
+        cost_estimate=pl.CostEstimate(flops=20 * 10**9, bytes_accessed=10**7, transcendentals=0),
         name="atom_stage",
-    )(atom_cond, atom_pos, atom_token, pos_weight, atom_proj, atom_output, atom_to_token, *earlier)
-
-
-def project_kernel(*refs):
-    token_in_refs, (single_ref, ada_ref, proj_ref, heads_ref, gate_ref) = refs[:-5], refs[-5:]
-    channels = proj_ref.shape[0]
-    heads, triple, lanes = heads_ref.shape
-    head = triple // 3
-    conditioning = 1.0 + mm(single_ref[...], ada_ref[...])
-    adapted = [(norm_rows(ref[...]) * conditioning[None]).astype(BF16).reshape(-1, channels) for ref in token_in_refs]
-    adapted = jnp.concatenate(adapted, axis=0)
-    for part in range(3):
-        rows = mm(adapted, proj_ref[:, part * channels : (part + 1) * channels])
-        if part == 0:
-            rows = rows * (head ** (-0.5) * LOG2E)
-        heads_ref[:, part * head : (part + 1) * head, :] = rows.T.astype(BF16).reshape(heads, head, lanes)
-    gate_ref[...] = jax.nn.sigmoid(mm(adapted, proj_ref[:, 3 * channels :]))
-
-
-def project(token_in, tok_single, ada_weight, tok_proj, heads):
-    tokens, channels = tok_single.shape
-    lanes = sum(x.shape[0] for x in token_in) * tokens
-    head = channels // heads
+    )(*args, ada_weight, tok_proj)
+
+
+def gate_kernel(adapted_ref, proj_ref, update_ref, gate_ref, terms_ref):
+    gate_ref[...] = jax.nn.sigmoid(mm(adapted_ref[...], proj_ref[...]))
+    weight = update_ref[...]
+    first = weight.astype(BF16).astype(F32)
+    terms_ref[...] = jnp.zeros_like(terms_ref)
+    terms_ref[0:3, :] = first
+    terms_ref[8:11, :] = weight - first
+
+
+def project_gate(adapted, tok_proj, pos_update):
+    lanes, channels = adapted.shape
+    turned = pos_update.T
     return pl.pallas_call(
-        project_kernel,
+        gate_kernel,
+        grid=(1,),
+        in_specs=[
+            pl.BlockSpec((lanes, channels), lambda i: (0, 0)),
+            pl.BlockSpec((channels, channels), lambda i: (0, 3)),
+            pl.BlockSpec(turned.shape, lambda i: (0, 0)),
+        ],
+        out_specs=[
+            pl.BlockSpec((lanes, channels), lambda i: (0, 0)),
+            pl.BlockSpec((16, turned.shape[1]), lambda i: (0, 0)),
+        ],
         out_shape=[
-            jax.ShapeDtypeStruct((heads, 3 * head, lanes), BF16),
             jax.ShapeDtypeStruct((lanes, channels), F32),
+            jax.ShapeDtypeStruct((16, turned.shape[1]), F32),
         ],
         compiler_params=params(),
-        cost_estimate=pl.CostEstimate(flops=4 * 10**9, bytes_accessed=8 * 10**6, transcendentals=0),
-        name="project",
-    )(*token_in, tok_single, ada_weight, tok_proj)
+        cost_estimate=pl.CostEstimate(flops=10**9, bytes_accessed=2 * 10**6, transcendentals=0),
+        name="project_gate",
+    )(adapted, tok_proj, turned)
 
 
 def attend_kernel(last, order_ref, own_ref, *refs):
@@ -339,7 +371,7 @@
             ],
         ),
         out_shape=out_shape,
-        compiler_params=params(),
+        compiler_params=params(ATTEND_VMEM_LIMIT),
         cost_estimate=pl.CostEstimate(flops=10**10, bytes_accessed=10**6, transcendentals=0),
         name="attend",
     )(order, *args)
@@ -354,22 +386,32 @@
 
     @pl.when(step == 0)
     def _():
-        load_in = pltpu.make_async_copy(trans_in_hbm, trans_in_ref, sems.at[0])
-        load_out = pltpu.make_async_copy(trans_out_hbm, trans_out_ref, sems.at[1])
-        load_in.start()
-        load_out.start()
+        hidden_width = trans_out_ref.shape[0]
+        chunk = hidden_width // 3
+        loads = []
+        for k in range(3):
+            for n, low in enumerate((k * chunk, hidden_width + k * chunk)):
+                place = pl.ds(low, chunk)
+                loads.append(pltpu.make_async_copy(trans_in_hbm.at[:, place], trans_in_ref.at[:, place], sems.at[2 * k + n]))
+        loads.append(pltpu.make_async_copy(trans_out_hbm, trans_out_ref, sems.at[6]))
+        for load in loads:
+            load.start()
         lanes = heads_ref.shape[2]
         attended = heads_ref[...].reshape(channels, lanes).astype(F32).T
         gated = (gate_ref[...] * attended).astype(BF16)
         token_in = jnp.concatenate([ref[...].reshape(-1, channels) for ref in token_in_refs], axis=0)
         after = token_in + mm(gated, output_ref[...])
         hidden_in = norm_rows(after).astype(BF16)
-        hidden_width = trans_out_ref.shape[0]
-        load_in.wait()
-        left = mm(hidden_in, trans_in_ref[:, :hidden_width])
-        right = mm(hidden_in, trans_in_ref[:, hidden_width:])
-        hidden = (jax.nn.silu(left) * right).astype(BF16)
-        load_out.wait()
+        hidden = []
+        for k in range(3):
+            low = k * chunk
+            loads[2 * k].wait()
+            left = mm(hidden_in, trans_in_ref[:, low : low + chunk])
+            loads[2 * k + 1].wait()
+            right = mm(hidden_in, trans_in_ref[:, hidden_width + low : hidden_width + low + chunk])
+            hidden.append((jax.nn.silu(left) * right).astype(BF16))
+        hidden = jnp.concatenate(hidden, axis=1)
+        loads[6].wait()
         result = (after + mm(hidden, trans_out_ref[...])).astype(BF16)
         token_out_ref[...] = result.reshape(samples, tokens, channels)
         feature_s[...] = mm(result, to_atom_ref[...]).astype(BF16).reshape(feature_s.shape)
@@ -378,12 +420,11 @@
     slots = owner.shape[1]
     onehot = (lax.broadcasted_iota(jnp.int32, (tokens, slots), 0) == owner).astype(BF16)
     final = norm_rows(mid_ref[0] + mm(onehot, feature_s[step], TN))
-    weight = update_ref[...]
     high = final.astype(BF16)
     low = (final - high.astype(F32)).astype(BF16)
-    first = weight.astype(BF16)
-    second = (weight - first.astype(F32)).astype(BF16)
-    update = mm(first, high, NT) + (mm(second, high, NT) + mm(first, low, NT))
+    terms = update_ref[...].astype(BF16)
+    update = mm(terms, high, NT)
+    update = update[:3] + (update[8:11] + mm(terms, low, NT)[:3])
     update = update * (owner < tokens).astype(F32)
     atom_ref[:, pl.ds(step, 1), :] = update.reshape(3, 1, slots)
 
@@ -394,7 +435,7 @@
     each, tokens, channels = token_in[0].shape
     samples, slots, width = atom_mid.shape
     owner = atom_token.reshape(slots // width, width)
-    turned = pos_update.T
+    turned = pos_update
     whole = lambda a: pl.BlockSpec(a.shape, lambda s: (0,) * a.ndim)
     args = (heads, gate, tok_output, token_to_atom)
     return pl.pallas_call(
@@ -416,9 +457,9 @@
             pltpu.VMEM((samples, tokens, width), BF16),
             pltpu.VMEM(transition_in.shape, BF16),
             pltpu.VMEM(transition_out.shape, BF16),
-            pltpu.SemaphoreType.DMA((2,)),
-        ],
-        compiler_params=params(),
+            pltpu.SemaphoreType.DMA((7,)),
+        ],
+        compiler_params=params(FINISH_VMEM_LIMIT),
         cost_estimate=pl.CostEstimate(flops=8 * 10**9, bytes_accessed=10**7, transcendentals=0),
         name="finish",
     )(*args, atom_mid, owner, turned, transition_in, transition_out, *token_in)
@@ -439,32 +480,27 @@
     tokens, channels = tok_single.shape
     heads = pair_weight.shape[1]
     samples = atom_pos.shape[0]
-    halves = 2
-    each = samples // halves
     pos = jnp.swapaxes(atom_pos, 0, 1)
     order = jnp.stack([lax.axis_index("xlo") * 2 + lax.axis_index("core"), lax.axis_index("xhi")]).astype(jnp.int32)
     own_bias = exchange(pair_bias(pair_rep, pair_weight), ("y", "z"))
     own_bias = own_bias.reshape(heads * tokens, own_bias.shape[2])
-    inputs = []
-    mid = None
-    for k in range(halves):
-        mid, token_in = atom_stage(
-            atom_cond, pos, atom_token, pos_weight, atom_proj, atom_output, atom_to_token, tokens, k * each, each,
-            samples, mid,
-        )
-        inputs.append(token_in)
-    own_bias, inputs[1] = lax.optimization_barrier((own_bias, inputs[1]))
+    mid, token_in, qkv, adapted = atom_stage(
+        atom_cond, pos, atom_token, pos_weight, atom_proj, atom_output, atom_to_token, tok_single, ada_weight, tok_proj,
+        heads,
+    )
+    own_bias, qkv = lax.optimization_barrier((own_bias, qkv))
     across = swap(own_bias, "xlo")
     near = swap(own_bias, "core")
-    qkv, gate = project(inputs, tok_single, ada_weight, tok_proj, heads)
     own = exchange(qkv, ("y", "z"))
+    gate, terms = project_gate(adapted, tok_proj, pos_update)
+    across, gate = lax.optimization_barrier((across, gate))
     far = swap(own[:, channels // heads :], "xhi")
     biases = (own_bias, near, across, swap(across, "core"))
     running = attend(order, own, biases, samples)
     attended = attend(order, own, biases, samples, far, running)
     attended = exchange(attended, ("y", "z"))
     token_out, update = finish(
-        attended, gate, tok_output, transition_in, transition_out, token_to_atom, mid, atom_token, pos_update, inputs
+        attended, gate, tok_output, transition_in, transition_out, token_to_atom, mid, atom_token, terms, [token_in]
     )
     return token_out, jnp.swapaxes(update, 0, 1)
 

time: 126 us -> 122 us (0.968)
  Pallas kernels: 67.5 us -> 60.8 us
  blocking collectives: 13.7 us -> 16.4 us
    ppermute x4, waiting for transfers between devices: 15.6 us -> 21.4 us  [swap(): return lax.ppermute(x, axis, [(0, 1), (1, 0)])]
    all_to_all x2, waiting for transfers between devices: 7.27 us -> 2.09 us  [exchange(): return lax.all_to_all(x, axes, 0, 0, tiled=True)]
    pallas_call x2, Pallas kernels: 21.7 us -> 18.4 us  [attend(): pl.pallas_call(functools.partial(attend_kernel, last), grid_spec=pltpu.Pr...]
    all_to_all x1, blocking collectives: 13.7 us -> 16.4 us  [exchange(): return lax.all_to_all(x, axes, 0, 0, tiled=True)]
    pallas_call x3 -> x2, Pallas kernels: 26.4 us -> 24.3 us  [the longest x1 21.6 us: atom_stage(): pl.pallas_call(atom_kernel, grid=(samples,), in_specs=[whole(a) for a in...]
  transfers between devices with their start and end apart: 6 -> 6, of which waited for: 3 -> 3; matrix products, arithmetic and copies ran while one was open for 1% -> 0% of each run, Pallas kernels for 29% -> 27%
where the time goes in v4:
time: 122 us
  Pallas kernels  60.8 us (50%)
  waiting for transfers between devices  23.5 us (19%)
  starting transfers between devices  19.9 us (16%)
  blocking collectives  16.4 us (13%)
    pallas_call x1, Pallas kernels, atom_stage(): pl.pallas_call(atom_kernel, grid=(samples,), in_specs=[whole(a) for a in...  21.6 us
    ppermute x4, waiting for transfers between devices, swap(): return lax.ppermute(x, axis, [(0, 1), (1, 0)])  21.4 us
    pallas_call x2, Pallas kernels, attend(): pl.pallas_call(functools.partial(attend_kernel, last), grid_spec=pltpu.Pr...  18.4 us
    all_to_all x1, blocking collectives, exchange(): return lax.all_to_all(x, axes, 0, 0, tiled=True)  16.4 us
    all_to_all x2, starting transfers between devices, exchange(): return lax.all_to_all(x, axes, 0, 0, tiled=True)  15.3 us
    pallas_call x1, Pallas kernels, finish(): pl.pallas_call(finish_kernel, grid=(samples,), in_specs=[whole(a) for a i...  11 us
    pallas_call x1, Pallas kernels, pair_bias(): pl.pallas_call(pair_kernel, grid=(rows // step,), in_specs=[pl.BlockSpec(...  6.97 us
    ppermute x4, starting transfers between devices, swap(): return lax.ppermute(x, axis, [(0, 1), (1, 0)])  4.58 us
  transfers between devices with their start and end apart: 6, of which 3 were waited for; matrix products, arithmetic and copies ran while one was open for 0% of the time, Pallas kernels for 27%

profile of v4, /device:TPU:0, one launch (start us, length us, event | category | flops | bytes accessed | tf_op | source)
XLA Modules:
  0.0 121.7 jit_solution(15438823011123880756)
XLA Ops:
  0.6 7.0 %pair_bias.1 = bf16[16,64,512]{2,1,0:T(8,128)(2,1)} custom-call(bf16[64,512,128]{2,1,0:T(8,128)(2,1)} %pair_ref.1, bf16[16,128]{1,0:T(8,128)(2,1)} %bitcast.16), custom_call_target="tpu_custom_call" | custom-call | flops 10000000000 | bytes 10000000 | tf_op jit(solution)/shard_map/pair_bias/pallas_call | solution.py:70
  7.6 8.1 %all-to-all-start = ((bf16[16,64,512]{2,1,0:T(8,128)(2,1)}), bf16[16,64,512]{2,1,0:T(8,128)(2,1)S(1)}, u32[]{:S(2)}, u32[]{:S(2)}) async-start(bf16[16,64,512]{2,1,0:T(8,128)(2,1)} %pair_bias.1), calls=%async_computation | async-start | bytes 2097152 | tf_op jit(solution)/shard_map/all_to_all | solution.py:473
  15.7 21.6 %atom_stage.1 = (f32[4,1536,128]{2,1,0:T(8,128)}, f32[4,64,768]{2,1,0:T(8,128)}, bf16[16,144,256]{2,1,0:T(8,128)(2,1)}, bf16[256,768]{1,0:T(8,128)(2,1)}) custom-call(bf16[1536,128]{1,0:T(8,128)(2,1)} %cond_ref.1, f32[3,4,1536]{2,1,0:T(4,128)} %bitcast.15, s32[12,128]{1,0:T(8,128)} %bitcast.12, f32[3,128]{1,0:T(4,128)} %pos_weight_ref.1, ...), custom_call_target="tpu_custom_call" | custom-call | flops 20000000000 | bytes 10000000 | tf_op jit(solution)/shard_map/atom_stage/pallas_call | solution.py:191
  37.4 0.0 all-to-all-done
  37.4 1.6 %collective-permute-start.2 = (bf16[1024,512]{1,0:T(8,128)(2,1)S(1)}, bf16[1024,512]{1,0:T(8,128)(2,1)S(1)}, u32[]{:S(2)}, u32[]{:S(2)}) collective-permute-start(bf16[1024,512]{1,0:T(8,128)(2,1)S(1)} %bitcast.8), channel_id=1, source_target_pairs={{0,64},{64,0},{1,65},{65,1},{2,66},{66,2},{3,67},{67,3},{4,68},{68... | collective-permute-start | bytes 3145736 | tf_op jit(solution)/shard_map/ppermute | solution.py:469
  38.9 7.2 %all-to-all-start.1 = ((bf16[16,144,256]{2,1,0:T(8,128)(2,1)}), bf16[16,144,256]{2,1,0:T(8,128)(2,1)S(1)}, u32[]{:S(2)}, u32[]{:S(2)}) async-start(bf16[16,144,256]{2,1,0:T(8,128)(2,1)} %get-tuple-element.15), calls=%async_computation.1 | async-start | bytes 2359296 | tf_op jit(solution)/shard_map/all_to_all | solution.py:473
  46.2 2.7 %project_gate.1 = (f32[256,768]{1,0:T(8,128)}, f32[16,128]{1,0:T(8,128)}) custom-call(bf16[256,768]{1,0:T(8,128)(2,1)} %get-tuple-element.17.adapted_ref, bf16[768,3072]{1,0:T(8,128)(2,1)} %proj_ref.3, f32[3,128]{1,0:T(4,128)} %bitcast.14), custom_call_target="tpu_custom_call" | custom-call | flops 1000000000 | bytes 2000000 | tf_op jit(solution)/shard_map/project_gate/pallas_call | solution.py:237
  48.9 0.0 collective-permute-start.1
  48.9 13.2 %collective-permute-done.2.refs_2_.refs_3_ = bf16[1024,512]{1,0:T(8,128)(2,1)S(1)} collective-permute-done((bf16[1024,512]{1,0:T(8,128)(2,1)S(1)}, bf16[1024,512]{1,0:T(8,128)(2,1)S(1)}, u32[]{:S(2)}, u32[]{:S(2)}) %collective-permute-start.2) | collective-permute-done | bytes 1048608 | tf_op jit(solution)/shard_map/ppermute | solution.py:469
  62.1 0.0 collective-permute-start.3
  62.1 0.1 pad_add_fusion.order_ref
  62.2 2.1 %all-to-all-done.1.own_ref = bf16[16,144,256]{2,1,0:T(8,128)(2,1)S(1)} async-done(((bf16[16,144,256]{2,1,0:T(8,128)(2,1)}), bf16[16,144,256]{2,1,0:T(8,128)(2,1)S(1)}, u32[]{:S(2)}, u32[]{:S(2)}) %all-to-all-start.1) | async-done | bytes 1179680 | tf_op jit(solution)/shard_map/all_to_all | solution.py:473
  64.2 0.1 slice.4
  64.3 3.0 %collective-permute-start = (bf16[16,96,256]{2,1,0:T(8,128)(2,1)S(1)}, bf16[16,96,256]{2,1,0:T(8,128)(2,1)S(1)}, u32[]{:S(2)}, u32[]{:S(2)}) collective-permute-start(bf16[16,96,256]{2,1,0:T(8,128)(2,1)S(1)} %slice.4), channel_id=1, source_target_pairs={{0,16},{16,0},{1,17},{17,1},{2,18},{18,2},{3,19},{19,3},{4,20},{20... | collective-permute-start | bytes 2359304 | tf_op jit(solution)/shard_map/ppermute | solution.py:469
  67.3 0.0 collective-permute-done.1.refs_1_.refs_2_
  67.3 0.0 collective-permute-done.3.refs_3_.refs_4_
  67.3 8.3 %attend.2.refs_5_ = f32[4,1024,128]{2,1,0:T(8,128)S(1)} custom-call(s32[2]{0:T(128)S(1)} %pad_add_fusion.order_ref, bf16[16,144,256]{2,1,0:T(8,128)(2,1)S(1)} %all-to-all-done.1.own_ref, bf16[1024,512]{1,0:T(8,128)(2,1)S(1)} %bitcast.10, bf16[1024,512]{1,0:T(8,128)(2,1)} %collective-permute-done.1.refs_1_.refs_2_, ...), custom_call_target="tpu_custom_call" | custom-call | flops 10000000000 | bytes 1000000 | tf_op jit(solution)/shard_map/attend/pallas_call | solution.py:360
  75.7 0.0 copy-start.1
  75.7 0.0 copy-start.2
  75.7 0.0 copy-start.3
  75.7 8.2 %collective-permute-done.refs_0_ = bf16[16,96,256]{2,1,0:T(8,128)(2,1)S(1)} collective-permute-done((bf16[16,96,256]{2,1,0:T(8,128)(2,1)S(1)}, bf16[16,96,256]{2,1,0:T(8,128)(2,1)S(1)}, u32[]{:S(2)}, u32[]{:S(2)}) %collective-permute-start) | collective-permute-done | bytes 786464 | tf_op jit(solution)/shard_map/ppermute | solution.py:469
  84.0 10.1 %attend.3 = bf16[16,48,256]{2,1,0:T(8,128)(2,1)S(1)} custom-call(s32[2]{0:T(128)S(1)} %pad_add_fusion.order_ref, bf16[16,144,256]{2,1,0:T(8,128)(2,1)S(1)} %all-to-all-done.1.own_ref, bf16[16,96,256]{2,1,0:T(8,128)(2,1)S(1)} %collective-permute-done.refs_0_, bf16[1024,512]{1,0:T(8,128)(2,1)S(1)} %bitcast.11, ...), custom_call_target="tpu_custom_call" | custom-call | flops 10000000000 | bytes 1000000 | tf_op jit(solution)/shard_map/attend/pallas_call | solution.py:360
  94.1 16.4 %all_to_all.15.heads_ref = bf16[16,48,256]{2,1,0:T(8,128)(2,1)S(1)} all-to-all(bf16[16,48,256]{2,1,0:T(8,128)(2,1)S(1)} %attend.3), channel_id=1, replica_groups=mesh['xlo'=2,'core'=2,'xhi'=2,'y'=4,'z'=4] {'y','z'}, dimensions={0} | all-to-all | bytes 786432 | tf_op jit(solution)/shard_map/all_to_all | solution.py:473
  110.5 11.0 %finish.1 = (bf16[4,64,768]{2,1,0:T(8,128)(2,1)}, f32[3,4,1536]{2,1,0:T(4,128)}) custom-call(bf16[16,48,256]{2,1,0:T(8,128)(2,1)S(1)} %all_to_all.15.heads_ref, f32[256,768]{1,0:T(8,128)S(1)} %copy-done, bf16[768,768]{1,0:T(8,128)(2,1)} %output_ref.3, bf16[768,128]{1,0:T(8,128)(2,1)S(1)} %copy-done.1, f32[4,1536,128]{2,1,0:T(8,128)} %get-tuple-element.21.mid_ref, ...), custom_call_target="tpu_custom_call" | custom-call | flops 8000000000 | bytes 10000000 | tf_op jit(solution)/shard_map/finish/pallas_call | solution.py:441
  (5 shorter events, 0.0 us)
Async XLA Ops:
  7.6 29.8 %all-to-all-start = ((bf16[16,64,512]{2,1,0:T(8,128)(2,1)}), bf16[16,64,512]{2,1,0:T(8,128)(2,1)S(1)}, u32[]{:S(2)}, u32[]{:S(2)}) async-start(bf16[16,64,512]{2,1,0:T(8,128)(2,1)} %pair_bias.1), calls=%async_computation | async-start | bytes 2097152 | tf_op jit(solution)/shard_map/all_to_all | solution.py:473
  37.4 24.7 %collective-permute-start.2 = (bf16[1024,512]{1,0:T(8,128)(2,1)S(1)}, bf16[1024,512]{1,0:T(8,128)(2,1)S(1)}, u32[]{:S(2)}, u32[]{:S(2)}) collective-permute-start(bf16[1024,512]{1,0:T(8,128)(2,1)S(1)} %bitcast.8), channel_id=1, source_target_pairs={{0,64},{64,0},{1,65},{65,1},{2,66},{66,2},{3,67},{67,3},{4,68},{68... | collective-permute-start | bytes 3145736 | tf_op jit(solution)/shard_map/ppermute | solution.py:469
  38.9 25.3 %all-to-all-start.1 = ((bf16[16,144,256]{2,1,0:T(8,128)(2,1)}), bf16[16,144,256]{2,1,0:T(8,128)(2,1)S(1)}, u32[]{:S(2)}, u32[]{:S(2)}) async-start(bf16[16,144,256]{2,1,0:T(8,128)(2,1)} %get-tuple-element.15), calls=%async_computation.1 | async-start | bytes 2359296 | tf_op jit(solution)/shard_map/all_to_all | solution.py:473
  48.9 18.4 %collective-permute-start.1 = (bf16[1024,512]{1,0:T(8,128)(2,1)S(1)}, bf16[1024,512]{1,0:T(8,128)(2,1)}, u32[]{:S(2)}, u32[]{:S(2)}) collective-permute-start(bf16[1024,512]{1,0:T(8,128)(2,1)S(1)} %bitcast.9), channel_id=1, source_target_pairs={{0,32},{32,0},{1,33},{33,1},{2,34},{34,2},{3,35},{35,3},{4,36},{36... | collective-permute-start | bytes 3145736 | tf_op jit(solution)/shard_map/ppermute | solution.py:469
  62.1 5.3 %collective-permute-start.3 = (bf16[1024,512]{1,0:T(8,128)(2,1)S(1)}, bf16[1024,512]{1,0:T(8,128)(2,1)}, u32[]{:S(2)}, u32[]{:S(2)}) collective-permute-start(bf16[1024,512]{1,0:T(8,128)(2,1)S(1)} %collective-permute-done.2.refs_2_.refs_3_), channel_id=1, source_target_pairs={{0,32},{32,0},{1,33},{33,1},{2,34},{34,2},{3,35},{35,3},{4,36},{36... | collective-permute-start | bytes 3145736 | tf_op jit(solution)/shard_map/ppermute | solution.py:469
  64.3 19.6 %collective-permute-start = (bf16[16,96,256]{2,1,0:T(8,128)(2,1)S(1)}, bf16[16,96,256]{2,1,0:T(8,128)(2,1)S(1)}, u32[]{:S(2)}, u32[]{:S(2)}) collective-permute-start(bf16[16,96,256]{2,1,0:T(8,128)(2,1)S(1)} %slice.4), channel_id=1, source_target_pairs={{0,16},{16,0},{1,17},{17,1},{2,18},{18,2},{3,19},{19,3},{4,20},{20... | collective-permute-start | bytes 2359304 | tf_op jit(solution)/shard_map/ppermute | solution.py:469
  75.7 34.8 %copy-start = (f32[256,768]{1,0:T(8,128)S(1)}, f32[256,768]{1,0:T(8,128)}, u32[]{:S(2)}) copy-start(f32[256,768]{1,0:T(8,128)} %get-tuple-element.20.gate_ref) | copy-start | bytes 2359300
  75.7 34.8 %copy-start.1 = (bf16[768,128]{1,0:T(8,128)(2,1)S(1)}, bf16[768,128]{1,0:T(8,128)(2,1)}, u32[]{:S(2)}) copy-start(bf16[768,128]{1,0:T(8,128)(2,1)} %to_atom_ref.1) | copy-start | bytes 589828
  75.7 34.8 %copy-start.2 = (s32[1536]{0:T(1024)S(1)}, s32[1536]{0:T(1024)}, u32[]{:S(2)}) copy-start(s32[1536]{0:T(1024)} %param.19) | copy-start | bytes 18436
  75.7 34.8 %copy-start.3 = (f32[16,128]{1,0:T(8,128)S(1)}, f32[16,128]{1,0:T(8,128)}, u32[]{:S(2)}) copy-start(f32[16,128]{1,0:T(8,128)} %get-tuple-element.22.update_ref) | copy-start | bytes 24580

commit v5 on v4

--- a/solution.py
+++ b/solution.py
@@ -257,17 +257,37 @@
 
 
 def attend_kernel(last, order_ref, own_ref, *refs):
-    refs, (out_ref, query_s, key_s, val_s) = refs[:-4], refs[-4:]
+    refs, (out_ref, query_s, key_s, val_s, bias_s, sems) = refs[:-6], refs[-6:]
     heads_ref, refs = (refs[0], refs[1:]) if last else (own_ref, refs)
     bias_refs, earlier = refs[:4], refs[4:]
     sources, _, lanes = own_ref.shape
     samples, head, keys = key_s.shape
     tokens = lanes // samples
     width = val_s.shape[2]
-    rows, cols = bias_refs[0].shape
+    rows = out_ref.shape[0] * tokens if last else out_ref.shape[1]
+    cols = bias_s.shape[2]
+    unit = 256
     step = pl.program_id(0)
     mine = order_ref[0]
     half = 1 - order_ref[1] if last else order_ref[1]
+
+    swapped = mine // 2 != half
+
+    def load(p, n, other):
+        place = pl.ds(pl.multiple_of(n * unit, unit), unit)
+        return pltpu.make_async_copy(bias_refs[p + 2 * other].at[place], bias_s.at[p, place], sems.at[p, n])
+
+    @pl.when((step == 0) & swapped)
+    def _():
+        for n in range(sources * tokens // unit):
+            for p in range(2):
+                load(p, n, 1).start()
+
+    @pl.when((step == 0) & jnp.logical_not(swapped))
+    def _():
+        for n in range(sources * tokens // unit):
+            for p in range(2):
+                load(p, n, 0).start()
 
     @pl.when(step == 0)
     def _():
@@ -289,18 +309,20 @@
                 pair = [heads_ref[k, low : low + head, s * tokens : (s + 1) * tokens] for k in (j, j + 1)]
                 key_s[s, :, j * tokens : (j + 2) * tokens] = jnp.concatenate(pair, axis=1)
 
-    swapped = mine // 2 != half
-    biases = [jnp.where(swapped, bias_refs[p + 2][...], bias_refs[p][...]).astype(F32) for p in range(2)]
     places = [pl.ds(pl.multiple_of((mine % 2 ^ p) * cols, cols), cols) for p in range(2)]
     lane = lax.broadcasted_iota(jnp.int32, (256, width), 1)
     results = []
-    unit = 256
     jobs = [(r, s) for r in range(0, rows, unit) for s in range(samples)]
 
     def score(job):
         r, s = job
         query = query_s[s, pl.ds(pl.multiple_of(step * rows + r, unit), unit), :]
-        return [mm(query, key_s[s, :, place]) + bias[r : r + unit] for place, bias in zip(places, biases)]
+        block = step * (rows // unit) + r // unit
+        if s == 0:
+            for p in range(2):
+                load(p, block, 0).wait()
+        block = pl.ds(pl.multiple_of(block * unit, unit), unit)
+        return [mm(query, key_s[s, :, place]) + bias_s[p, block, :].astype(F32) for p, place in enumerate(places)]
 
     def soften(job, scores):
         r, s = job
@@ -338,23 +360,28 @@
             out_ref[j] = block.T[:head].astype(BF16)
 
 
-def attend(order, own, biases, samples, far=None, earlier=None):
+def attend(order, own, biases, samples, far=None, earlier=None, part=0, result=None):
     sources, triple, lanes = own.shape
     head = triple // 3
     tokens = lanes // samples
     width = 128
-    rows = 256
     total, cols = biases[0].shape
     last = earlier is not None
-    whole = lambda a: pl.BlockSpec(a.shape, lambda i, *_: (0,) * a.ndim)
-    bias_specs = [pl.BlockSpec((rows, cols), lambda i, *_: (i, 0))] * 4
-    running = pl.BlockSpec((samples, rows, width), lambda i, *_: (0, i, 0))
+    rows = 512 if last else 256
+    each = far.shape[2] // tokens if last else samples
+    spans = each * tokens
+    before = () if result is None else (result,)
+    own_spec = pl.BlockSpec((sources, triple, spans), lambda i, *_: (0, 0, part))
+    bias_specs = [pl.BlockSpec(memory_space=pl.ANY)] * 4
+    running = pl.BlockSpec((each, rows, width), lambda i, *_: (part, i, 0))
     if last:
-        args, in_specs = (own, far, *biases, earlier), [whole(own), whole(far)] + bias_specs + [running]
-        out_specs = pl.BlockSpec((rows // tokens, head, lanes), lambda i, *_: (i, 0, 0))
+        args = (own, far, *biases, earlier, *before)
+        in_specs = [own_spec, pl.BlockSpec(far.shape, lambda i, *_: (0, 0, 0))] + bias_specs + [running]
+        in_specs += [pl.BlockSpec(memory_space=pl.ANY)] * len(before)
+        out_specs = pl.BlockSpec((rows // tokens, head, spans), lambda i, *_: (i, 0, part))
         out_shape = jax.ShapeDtypeStruct((sources, head, lanes), BF16)
     else:
-        args, in_specs = (own, *biases), [whole(own)] + bias_specs
+        args, in_specs = (own, *biases), [own_spec] + bias_specs
         out_specs = running
         out_shape = jax.ShapeDtypeStruct((samples, total, width), F32)
     return pl.pallas_call(
@@ -365,14 +392,17 @@
             in_specs=in_specs,
             out_specs=out_specs,
             scratch_shapes=[
-                pltpu.VMEM((samples, total, head), BF16),
-                pltpu.VMEM((samples, head, total), BF16),
-                pltpu.VMEM((samples, total, width), BF16),
+                pltpu.VMEM((each, total, head), BF16),
+                pltpu.VMEM((each, head, total), BF16),
+                pltpu.VMEM((each, total, width), BF16),
+                pltpu.VMEM((2, total, cols), BF16),
+                pltpu.SemaphoreType.DMA((2, total // 256)),
             ],
         ),
         out_shape=out_shape,
+        input_output_aliases={8: 0} if before else {},
         compiler_params=params(ATTEND_VMEM_LIMIT),
-        cost_estimate=pl.CostEstimate(flops=10**10, bytes_accessed=10**6, transcendentals=0),
+        cost_estimate=pl.CostEstimate(flops=each * 25 * 10**8, bytes_accessed=10**6, transcendentals=0),
         name="attend",
     )(order, *args)
 
@@ -494,10 +524,14 @@
     own = exchange(qkv, ("y", "z"))
     gate, terms = project_gate(adapted, tok_proj, pos_update)
     across, gate = lax.optimization_barrier((across, gate))
-    far = swap(own[:, channels // heads :], "xhi")
+    parts = 2
+    spans = samples * tokens // parts
+    fars = [swap(own[:, channels // heads :, k * spans : (k + 1) * spans], "xhi") for k in range(parts)]
     biases = (own_bias, near, across, swap(across, "core"))
     running = attend(order, own, biases, samples)
-    attended = attend(order, own, biases, samples, far, running)
+    attended = None
+    for k in range(parts):
+        attended = attend(order, own, biases, samples, fars[k], running, k, attended)
     attended = exchange(attended, ("y", "z"))
     token_out, update = finish(
         attended, gate, tok_output, transition_in, transition_out, token_to_atom, mid, atom_token, terms, [token_in]

time: 122 us -> 118 us (0.967)
  waiting for transfers between devices: 23.5 us -> 17.5 us
    ppermute x4 -> x5, waiting for transfers between devices: 21.4 us -> 15.5 us  [swap(): return lax.ppermute(x, axis, [(0, 1), (1, 0)])]
    pallas_call x2 -> x3, Pallas kernels: 18.4 us -> 19.2 us  [attend(): pl.pallas_call(functools.partial(attend_kernel, last), grid_spec=pltpu.Pr...]
    ppermute x4 -> x5, starting transfers between devices: 4.58 us -> 5.19 us  [swap(): return lax.ppermute(x, axis, [(0, 1), (1, 0)])]
  transfers between devices with their start and end apart: 6 -> 7, of which waited for: 3 -> 4; matrix products, arithmetic and copies ran while one was open for 0% -> 0% of each run, Pallas kernels for 27% -> 32%
where the time goes in v5:
time: 118 us; the launch traced here: 117 us
  Pallas kernels  61.5 us (52%)
  starting transfers between devices  20.5 us (17%)
  waiting for transfers between devices  17.5 us (15%)
  blocking collectives  16.4 us (14%)
    pallas_call x1, Pallas kernels, atom_stage(): pl.pallas_call(atom_kernel, grid=(samples,), in_specs=[whole(a) for a in...  21.6 us
    pallas_call x3, Pallas kernels, attend(): pl.pallas_call(functools.partial(attend_kernel, last), grid_spec=pltpu.Pr...  19.2 us
    all_to_all x1, blocking collectives, exchange(): return lax.all_to_all(x, axes, 0, 0, tiled=True)  16.4 us
    ppermute x5, waiting for transfers between devices, swap(): return lax.ppermute(x, axis, [(0, 1), (1, 0)])  15.5 us
    all_to_all x2, starting transfers between devices, exchange(): return lax.all_to_all(x, axes, 0, 0, tiled=True)  15.3 us
    pallas_call x1, Pallas kernels, finish(): pl.pallas_call(finish_kernel, grid=(samples,), in_specs=[whole(a) for a i...  11 us
    pallas_call x1, Pallas kernels, pair_bias(): pl.pallas_call(pair_kernel, grid=(rows // step,), in_specs=[pl.BlockSpec(...  7 us
    ppermute x5, starting transfers between devices, swap(): return lax.ppermute(x, axis, [(0, 1), (1, 0)])  5.19 us
  transfers between devices with their start and end apart: 7, of which 4 were waited for; matrix products, arithmetic and copies ran while one was open for 0% of the time, Pallas kernels for 32%

profile of v5, /device:TPU:0, one launch (start us, length us, event | category | flops | bytes accessed | tf_op | source)
XLA Modules:
  0.0 117.2 jit_solution(5194741667654191459)
XLA Ops:
  0.6 7.0 %pair_bias.1 = bf16[16,64,512]{2,1,0:T(8,128)(2,1)} custom-call(bf16[64,512,128]{2,1,0:T(8,128)(2,1)} %pair_ref.1, bf16[16,128]{1,0:T(8,128)(2,1)} %bitcast.17), custom_call_target="tpu_custom_call" | custom-call | flops 10000000000 | bytes 10000000 | tf_op jit(solution)/shard_map/pair_bias/pallas_call | solution.py:70
  7.6 8.1 %all-to-all-start = ((bf16[16,64,512]{2,1,0:T(8,128)(2,1)}), bf16[16,64,512]{2,1,0:T(8,128)(2,1)S(1)}, u32[]{:S(2)}, u32[]{:S(2)}) async-start(bf16[16,64,512]{2,1,0:T(8,128)(2,1)} %pair_bias.1), calls=%async_computation | async-start | bytes 2097152 | tf_op jit(solution)/shard_map/all_to_all | solution.py:503
  15.8 21.6 %atom_stage.1 = (f32[4,1536,128]{2,1,0:T(8,128)}, f32[4,64,768]{2,1,0:T(8,128)}, bf16[16,144,256]{2,1,0:T(8,128)(2,1)}, bf16[256,768]{1,0:T(8,128)(2,1)}) custom-call(bf16[1536,128]{1,0:T(8,128)(2,1)} %cond_ref.1, f32[3,4,1536]{2,1,0:T(4,128)} %bitcast.16, s32[12,128]{1,0:T(8,128)} %bitcast.13, f32[3,128]{1,0:T(4,128)} %pos_weight_ref.1, ...), custom_call_target="tpu_custom_call" | custom-call | flops 20000000000 | bytes 10000000 | tf_op jit(solution)/shard_map/atom_stage/pallas_call | solution.py:191
  37.4 0.0 all-to-all-done
  37.4 1.6 %collective-permute-start.2 = (bf16[1024,512]{1,0:T(8,128)(2,1)S(1)}, bf16[1024,512]{1,0:T(8,128)(2,1)S(1)}, u32[]{:S(2)}, u32[]{:S(2)}) collective-permute-start(bf16[1024,512]{1,0:T(8,128)(2,1)S(1)} %bitcast.8), channel_id=1, source_target_pairs={{0,64},{64,0},{1,65},{65,1},{2,66},{66,2},{3,67},{67,3},{4,68},{68... | collective-permute-start | bytes 3145736 | tf_op jit(solution)/shard_map/ppermute | solution.py:499
  39.0 7.2 %all-to-all-start.1 = ((bf16[16,144,256]{2,1,0:T(8,128)(2,1)}), bf16[16,144,256]{2,1,0:T(8,128)(2,1)S(1)}, u32[]{:S(2)}, u32[]{:S(2)}) async-start(bf16[16,144,256]{2,1,0:T(8,128)(2,1)} %get-tuple-element.15), calls=%async_computation.1 | async-start | bytes 2359296 | tf_op jit(solution)/shard_map/all_to_all | solution.py:503
  46.2 2.7 %project_gate.1 = (f32[256,768]{1,0:T(8,128)}, f32[16,128]{1,0:T(8,128)}) custom-call(bf16[256,768]{1,0:T(8,128)(2,1)} %get-tuple-element.17.adapted_ref, bf16[768,3072]{1,0:T(8,128)(2,1)} %proj_ref.3, f32[3,128]{1,0:T(4,128)} %bitcast.15), custom_call_target="tpu_custom_call" | custom-call | flops 1000000000 | bytes 2000000 | tf_op jit(solution)/shard_map/project_gate/pallas_call | solution.py:237
  48.9 0.0 collective-permute-start.1
  48.9 13.2 %collective-permute-done.2.refs_2_.refs_3_ = bf16[1024,512]{1,0:T(8,128)(2,1)S(1)} collective-permute-done((bf16[1024,512]{1,0:T(8,128)(2,1)S(1)}, bf16[1024,512]{1,0:T(8,128)(2,1)S(1)}, u32[]{:S(2)}, u32[]{:S(2)}) %collective-permute-start.2) | collective-permute-done | bytes 1048608 | tf_op jit(solution)/shard_map/ppermute | solution.py:499
  62.1 0.1 pad_add_fusion.order_ref
  62.2 2.1 %all-to-all-done.1.own_ref = bf16[16,144,256]{2,1,0:T(8,128)(2,1)S(1)} async-done(((bf16[16,144,256]{2,1,0:T(8,128)(2,1)}), bf16[16,144,256]{2,1,0:T(8,128)(2,1)S(1)}, u32[]{:S(2)}, u32[]{:S(2)}) %all-to-all-start.1) | async-done | bytes 1179680 | tf_op jit(solution)/shard_map/all_to_all | solution.py:503
  64.3 0.1 fusion
  64.4 2.8 %collective-permute-start.4 = (bf16[16,96,128]{2,1,0:T(8,128)(2,1)S(1)}, bf16[16,96,128]{2,1,0:T(8,128)(2,1)S(1)}, u32[]{:S(2)}, u32[]{:S(2)}) collective-permute-start(bf16[16,96,128]{2,1,0:T(8,128)(2,1)S(1)} %get-tuple-element.26), channel_id=1, source_target_pairs={{0,16},{16,0},{1,17},{17,1},{2,18},{18,2},{3,19},{19,3},{4,20},{20... | collective-permute-start | bytes 1179656 | tf_op jit(solution)/shard_map/ppermute | solution.py:499
  67.2 0.8 collective-permute-start
  68.0 7.8 %attend.3.refs_5_ = f32[4,1024,128]{2,1,0:T(8,128)S(1)} custom-call(s32[2]{0:T(128)S(1)} %pad_add_fusion.order_ref, bf16[16,144,256]{2,1,0:T(8,128)(2,1)S(1)} %all-to-all-done.1.own_ref, bf16[1024,512]{1,0:T(8,128)(2,1)S(1)} %bitcast.10, bf16[1024,512]{1,0:T(8,128)(2,1)} %collective-permute-done.1.refs_1_.refs_2_, ...), custom_call_target="tpu_custom_call" | custom-call | flops 10000000000 | bytes 1000000 | tf_op jit(solution)/shard_map/attend/pallas_call | solution.py:387
  75.9 2.2 %collective-permute-done.4.refs_0_ = bf16[16,96,128]{2,1,0:T(8,128)(2,1)S(1)} collective-permute-done((bf16[16,96,128]{2,1,0:T(8,128)(2,1)S(1)}, bf16[16,96,128]{2,1,0:T(8,128)(2,1)S(1)}, u32[]{:S(2)}, u32[]{:S(2)}) %collective-permute-start.4) | collective-permute-done | bytes 393248 | tf_op jit(solution)/shard_map/ppermute | solution.py:499
  78.1 5.7 %attend.4.refs_6_ = bf16[16,48,256]{2,1,0:T(8,128)(2,1)S(1)} custom-call(s32[2]{0:T(128)S(1)} %pad_add_fusion.order_ref, bf16[16,144,256]{2,1,0:T(8,128)(2,1)S(1)} %all-to-all-done.1.own_ref, bf16[16,96,128]{2,1,0:T(8,128)(2,1)S(1)} %collective-permute-done.4.refs_0_, bf16[1024,512]{1,0:T(8,128)(2,1)S(1)} %bitcast.11, ...), custom_call_target="tpu_custom_call" | custom-call | flops 5000000000 | bytes 1000000 | tf_op jit(solution)/shard_map/attend/pallas_call | solution.py:387
  83.8 0.0 copy-start.1
  83.8 0.0 copy-start.2
  83.8 0.0 copy-start.3
  83.8 0.1 collective-permute-done.refs_0_
  83.9 5.7 %attend.5 = bf16[16,48,256]{2,1,0:T(8,128)(2,1)S(1)} custom-call(s32[2]{0:T(128)S(1)} %pad_add_fusion.order_ref, bf16[16,144,256]{2,1,0:T(8,128)(2,1)S(1)} %all-to-all-done.1.own_ref, bf16[16,96,128]{2,1,0:T(8,128)(2,1)S(1)} %collective-permute-done.refs_0_, bf16[1024,512]{1,0:T(8,128)(2,1)S(1)} %bitcast.12, ...), custom_call_target="tpu_custom_call", output_to_operand_aliasing={{}: (8, {})} | custom-call | flops 5000000000 | bytes 1000000 | tf_op jit(solution)/shard_map/attend/pallas_call | solution.py:387
  89.5 16.4 %all_to_all.15.heads_ref = bf16[16,48,256]{2,1,0:T(8,128)(2,1)S(1)} all-to-all(bf16[16,48,256]{2,1,0:T(8,128)(2,1)S(1)} %attend.5), channel_id=1, replica_groups=mesh['xlo'=2,'core'=2,'xhi'=2,'y'=4,'z'=4] {'y','z'}, dimensions={0} | all-to-all | bytes 786432 | tf_op jit(solution)/shard_map/all_to_all | solution.py:503
  106.0 11.0 %finish.1 = (bf16[4,64,768]{2,1,0:T(8,128)(2,1)}, f32[3,4,1536]{2,1,0:T(4,128)}) custom-call(bf16[16,48,256]{2,1,0:T(8,128)(2,1)S(1)} %all_to_all.15.heads_ref, f32[256,768]{1,0:T(8,128)S(1)} %copy-done, bf16[768,768]{1,0:T(8,128)(2,1)} %output_ref.3, bf16[768,128]{1,0:T(8,128)(2,1)S(1)} %copy-done.1, f32[4,1536,128]{2,1,0:T(8,128)} %get-tuple-element.21.mid_ref, ...), custom_call_target="tpu_custom_call" | custom-call | flops 8000000000 | bytes 10000000 | tf_op jit(solution)/shard_map/finish/pallas_call | solution.py:471
  (8 shorter events, 0.0 us)
Async XLA Ops:
  7.6 29.8 %all-to-all-start = ((bf16[16,64,512]{2,1,0:T(8,128)(2,1)}), bf16[16,64,512]{2,1,0:T(8,128)(2,1)S(1)}, u32[]{:S(2)}, u32[]{:S(2)}) async-start(bf16[16,64,512]{2,1,0:T(8,128)(2,1)} %pair_bias.1), calls=%async_computation | async-start | bytes 2097152 | tf_op jit(solution)/shard_map/all_to_all | solution.py:503
  37.4 24.7 %collective-permute-start.2 = (bf16[1024,512]{1,0:T(8,128)(2,1)S(1)}, bf16[1024,512]{1,0:T(8,128)(2,1)S(1)}, u32[]{:S(2)}, u32[]{:S(2)}) collective-permute-start(bf16[1024,512]{1,0:T(8,128)(2,1)S(1)} %bitcast.8), channel_id=1, source_target_pairs={{0,64},{64,0},{1,65},{65,1},{2,66},{66,2},{3,67},{67,3},{4,68},{68... | collective-permute-start | bytes 3145736 | tf_op jit(solution)/shard_map/ppermute | solution.py:499
  39.0 25.3 %all-to-all-start.1 = ((bf16[16,144,256]{2,1,0:T(8,128)(2,1)}), bf16[16,144,256]{2,1,0:T(8,128)(2,1)S(1)}, u32[]{:S(2)}, u32[]{:S(2)}) async-start(bf16[16,144,256]{2,1,0:T(8,128)(2,1)} %get-tuple-element.15), calls=%async_computation.1 | async-start | bytes 2359296 | tf_op jit(solution)/shard_map/all_to_all | solution.py:503
  48.9 19.1 %collective-permute-start.1 = (bf16[1024,512]{1,0:T(8,128)(2,1)S(1)}, bf16[1024,512]{1,0:T(8,128)(2,1)}, u32[]{:S(2)}, u32[]{:S(2)}) collective-permute-start(bf16[1024,512]{1,0:T(8,128)(2,1)S(1)} %bitcast.9), channel_id=1, source_target_pairs={{0,32},{32,0},{1,33},{33,1},{2,34},{34,2},{3,35},{35,3},{4,36},{36... | collective-permute-start | bytes 3145736 | tf_op jit(solution)/shard_map/ppermute | solution.py:499
  62.1 5.9 %collective-permute-start.3 = (bf16[1024,512]{1,0:T(8,128)(2,1)S(1)}, bf16[1024,512]{1,0:T(8,128)(2,1)}, u32[]{:S(2)}, u32[]{:S(2)}) collective-permute-start(bf16[1024,512]{1,0:T(8,128)(2,1)S(1)} %collective-permute-done.2.refs_2_.refs_3_), channel_id=1, source_target_pairs={{0,32},{32,0},{1,33},{33,1},{2,34},{34,2},{3,35},{35,3},{4,36},{36... | collective-permute-start | bytes 3145736 | tf_op jit(solution)/shard_map/ppermute | solution.py:499
  64.4 13.6 %collective-permute-start.4 = (bf16[16,96,128]{2,1,0:T(8,128)(2,1)S(1)}, bf16[16,96,128]{2,1,0:T(8,128)(2,1)S(1)}, u32[]{:S(2)}, u32[]{:S(2)}) collective-permute-start(bf16[16,96,128]{2,1,0:T(8,128)(2,1)S(1)} %get-tuple-element.26), channel_id=1, source_target_pairs={{0,16},{16,0},{1,17},{17,1},{2,18},{18,2},{3,19},{19,3},{4,20},{20... | collective-permute-start | bytes 1179656 | tf_op jit(solution)/shard_map/ppermute | solution.py:499
  67.2 16.6 %collective-permute-start = (bf16[16,96,128]{2,1,0:T(8,128)(2,1)S(1)}, bf16[16,96,128]{2,1,0:T(8,128)(2,1)S(1)}, u32[]{:S(2)}, u32[]{:S(2)}) collective-permute-start(bf16[16,96,128]{2,1,0:T(8,128)(2,1)S(1)} %get-tuple-element.27), channel_id=1, source_target_pairs={{0,16},{16,0},{1,17},{17,1},{2,18},{18,2},{3,19},{19,3},{4,20},{20... | collective-permute-start | bytes 1179656 | tf_op jit(solution)/shard_map/ppermute | solution.py:499
  83.7 22.2 %copy-start = (f32[256,768]{1,0:T(8,128)S(1)}, f32[256,768]{1,0:T(8,128)}, u32[]{:S(2)}) copy-start(f32[256,768]{1,0:T(8,128)} %get-tuple-element.20.gate_ref) | copy-start | bytes 2359300
  83.8 22.2 %copy-start.1 = (bf16[768,128]{1,0:T(8,128)(2,1)S(1)}, bf16[768,128]{1,0:T(8,128)(2,1)}, u32[]{:S(2)}) copy-start(bf16[768,128]{1,0:T(8,128)(2,1)} %to_atom_ref.1) | copy-start | bytes 589828
  83.8 22.2 %copy-start.2 = (s32[1536]{0:T(1024)S(1)}, s32[1536]{0:T(1024)}, u32[]{:S(2)}) copy-start(s32[1536]{0:T(1024)} %param.19) | copy-start | bytes 18436
  83.8 22.2 %copy-start.3 = (f32[16,128]{1,0:T(8,128)S(1)}, f32[16,128]{1,0:T(8,128)}, u32[]{:S(2)}) copy-start(f32[16,128]{1,0:T(8,128)} %get-tuple-element.22.update_ref) | copy-start | bytes 24580

commit v6 on v5

--- a/solution.py
+++ b/solution.py
@@ -16,7 +16,7 @@
 LOG2E = 1.4426950408889634
 F32 = jnp.float32
 BF16 = jnp.bfloat16
-VMEM_LIMIT = 117 * 512 * 1024
+VMEM_LIMIT = 52 * 1024 * 1024
 PAIR_VMEM_LIMIT = 60 * 1024 * 1024
 ATTEND_VMEM_LIMIT = 44 * 1024 * 1024
 FINISH_VMEM_LIMIT = 52 * 1024 * 1024

time: 118 us -> 117 us (level)
  Pallas kernels: 61.5 us -> 59.2 us
    pallas_call x1, Pallas kernels: 21.6 us -> 20.2 us  [atom_stage(): pl.pallas_call(atom_kernel, grid=(samples,), in_specs=[whole(a) for a in...]
  transfers between devices with their start and end apart: 7 -> 7, of which waited for: 4 -> 4; matrix products, arithmetic and copies ran while one was open for 0% -> 0% of each run, Pallas kernels for 32% -> 30%
where the time goes in v6:
time: 117 us; the launch traced here: 116 us
  Pallas kernels  59.2 us (51%)
  starting transfers between devices  20.7 us (18%)
  waiting for transfers between devices  17.7 us (15%)
  blocking collectives  16.4 us (14%)
    pallas_call x1, Pallas kernels, atom_stage(): pl.pallas_call(atom_kernel, grid=(samples,), in_specs=[whole(a) for a in...  20.2 us
    pallas_call x3, Pallas kernels, attend(): pl.pallas_call(functools.partial(attend_kernel, last), grid_spec=pltpu.Pr...  19.2 us
    all_to_all x1, blocking collectives, exchange(): return lax.all_to_all(x, axes, 0, 0, tiled=True)  16.4 us
    ppermute x5, waiting for transfers between devices, swap(): return lax.ppermute(x, axis, [(0, 1), (1, 0)])  15.7 us
    all_to_all x2, starting transfers between devices, exchange(): return lax.all_to_all(x, axes, 0, 0, tiled=True)  15.5 us
    pallas_call x1, Pallas kernels, finish(): pl.pallas_call(finish_kernel, grid=(samples,), in_specs=[whole(a) for a i...  11 us
    pallas_call x1, Pallas kernels, pair_bias(): pl.pallas_call(pair_kernel, grid=(rows // step,), in_specs=[pl.BlockSpec(...  7.01 us
    ppermute x5, starting transfers between devices, swap(): return lax.ppermute(x, axis, [(0, 1), (1, 0)])  5.18 us
  transfers between devices with their start and end apart: 7, of which 4 were waited for; matrix products, arithmetic and copies ran while one was open for 0% of the time, Pallas kernels for 30%

profile of v6, /device:TPU:0, one launch (start us, length us, event | category | flops | bytes accessed | tf_op | source)
XLA Modules:
  0.0 116.2 jit_solution(6359911891470465140)
XLA Ops:
  0.6 7.0 %pair_bias.1 = bf16[16,64,512]{2,1,0:T(8,128)(2,1)} custom-call(bf16[64,512,128]{2,1,0:T(8,128)(2,1)} %pair_ref.1, bf16[16,128]{1,0:T(8,128)(2,1)} %bitcast.17), custom_call_target="tpu_custom_call" | custom-call | flops 10000000000 | bytes 10000000 | tf_op jit(solution)/shard_map/pair_bias/pallas_call | solution.py:70
  7.6 0.0 copy-start.7
  7.7 0.0 copy-start.9
  7.7 0.0 copy-start.10
  7.7 8.3 %all-to-all-start = ((bf16[16,64,512]{2,1,0:T(8,128)(2,1)}), bf16[16,64,512]{2,1,0:T(8,128)(2,1)S(1)}, u32[]{:S(2)}, u32[]{:S(2)}) async-start(bf16[16,64,512]{2,1,0:T(8,128)(2,1)} %pair_bias.1), calls=%async_computation | async-start | bytes 2097152 | tf_op jit(solution)/shard_map/all_to_all | solution.py:503
  16.1 20.2 %atom_stage.1 = (f32[4,1536,128]{2,1,0:T(8,128)}, f32[4,64,768]{2,1,0:T(8,128)}, bf16[16,144,256]{2,1,0:T(8,128)(2,1)}, bf16[256,768]{1,0:T(8,128)(2,1)S(1)}) custom-call(bf16[1536,128]{1,0:T(8,128)(2,1)S(1)} %copy-done.3, f32[3,4,1536]{2,1,0:T(4,128)S(1)} %bitcast.14, s32[12,128]{1,0:T(8,128)S(1)} %bitcast.15, f32[3,128]{1,0:T(4,128)S(1)} %copy-done.11, ...), custom_call_target="tpu_custom_call" | custom-call | flops 20000000000 | bytes 10000000 | tf_op jit(solution)/shard_map/atom_stage/pallas_call | solution.py:191
  36.3 1.6 %collective-permute-start.2 = (bf16[1024,512]{1,0:T(8,128)(2,1)S(1)}, bf16[1024,512]{1,0:T(8,128)(2,1)}, u32[]{:S(2)}, u32[]{:S(2)}) collective-permute-start(bf16[1024,512]{1,0:T(8,128)(2,1)S(1)} %bitcast.8), channel_id=1, source_target_pairs={{0,64},{64,0},{1,65},{65,1},{2,66},{66,2},{3,67},{67,3},{4,68},{68... | collective-permute-start | bytes 3145736 | tf_op jit(solution)/shard_map/ppermute | solution.py:499
  37.8 7.2 %all-to-all-start.1 = ((bf16[16,144,256]{2,1,0:T(8,128)(2,1)}), bf16[16,144,256]{2,1,0:T(8,128)(2,1)S(1)}, u32[]{:S(2)}, u32[]{:S(2)}) async-start(bf16[16,144,256]{2,1,0:T(8,128)(2,1)} %get-tuple-element.15), calls=%async_computation.1 | async-start | bytes 2359296 | tf_op jit(solution)/shard_map/all_to_all | solution.py:503
  45.1 1.8 %project_gate.1 = (f32[256,768]{1,0:T(8,128)S(1)}, f32[16,128]{1,0:T(8,128)S(1)}) custom-call(bf16[256,768]{1,0:T(8,128)(2,1)S(1)} %get-tuple-element.17.adapted_ref, bf16[768,3072]{1,0:T(8,128)(2,1)} %proj_ref.3, f32[3,128]{1,0:T(4,128)S(1)} %bitcast.13), custom_call_target="tpu_custom_call" | custom-call | flops 1000000000 | bytes 2000000 | tf_op jit(solution)/shard_map/project_gate/pallas_call | solution.py:237
  46.8 0.9 copy-done.1
  47.7 13.3 %collective-permute-done.2.refs_2_.refs_3_ = bf16[1024,512]{1,0:T(8,128)(2,1)} collective-permute-done((bf16[1024,512]{1,0:T(8,128)(2,1)S(1)}, bf16[1024,512]{1,0:T(8,128)(2,1)}, u32[]{:S(2)}, u32[]{:S(2)}) %collective-permute-start.2) | collective-permute-done | bytes 1048608 | tf_op jit(solution)/shard_map/ppermute | solution.py:499
  61.1 0.1 pad_add_fusion.order_ref
  61.2 2.0 %all-to-all-done.1.own_ref = bf16[16,144,256]{2,1,0:T(8,128)(2,1)S(1)} async-done(((bf16[16,144,256]{2,1,0:T(8,128)(2,1)}), bf16[16,144,256]{2,1,0:T(8,128)(2,1)S(1)}, u32[]{:S(2)}, u32[]{:S(2)}) %all-to-all-start.1) | async-done | bytes 1179680 | tf_op jit(solution)/shard_map/all_to_all | solution.py:503
  63.1 0.1 fusion
  63.3 2.8 %collective-permute-start.4 = (bf16[16,96,128]{2,1,0:T(8,128)(2,1)S(1)}, bf16[16,96,128]{2,1,0:T(8,128)(2,1)S(1)}, u32[]{:S(2)}, u32[]{:S(2)}) collective-permute-start(bf16[16,96,128]{2,1,0:T(8,128)(2,1)S(1)} %get-tuple-element.26), channel_id=1, source_target_pairs={{0,16},{16,0},{1,17},{17,1},{2,18},{18,2},{3,19},{19,3},{4,20},{20... | collective-permute-start | bytes 1179656 | tf_op jit(solution)/shard_map/ppermute | solution.py:499
  66.1 0.8 collective-permute-start
  66.9 7.8 %attend.3.refs_5_ = f32[4,1024,128]{2,1,0:T(8,128)S(1)} custom-call(s32[2]{0:T(128)S(1)} %pad_add_fusion.order_ref, bf16[16,144,256]{2,1,0:T(8,128)(2,1)S(1)} %all-to-all-done.1.own_ref, bf16[1024,512]{1,0:T(8,128)(2,1)S(1)} %bitcast.10, bf16[1024,512]{1,0:T(8,128)(2,1)S(1)} %collective-permute-done.1.refs_1_.refs_2_, ...), custom_call_target="tpu_custom_call" | custom-call | flops 10000000000 | bytes 1000000 | tf_op jit(solution)/shard_map/attend/pallas_call | solution.py:387
  74.7 2.2 %collective-permute-done.4.refs_0_ = bf16[16,96,128]{2,1,0:T(8,128)(2,1)S(1)} collective-permute-done((bf16[16,96,128]{2,1,0:T(8,128)(2,1)S(1)}, bf16[16,96,128]{2,1,0:T(8,128)(2,1)S(1)}, u32[]{:S(2)}, u32[]{:S(2)}) %collective-permute-start.4) | collective-permute-done | bytes 393248 | tf_op jit(solution)/shard_map/ppermute | solution.py:499
  76.9 5.7 %attend.4.refs_6_ = bf16[16,48,256]{2,1,0:T(8,128)(2,1)S(1)} custom-call(s32[2]{0:T(128)S(1)} %pad_add_fusion.order_ref, bf16[16,144,256]{2,1,0:T(8,128)(2,1)S(1)} %all-to-all-done.1.own_ref, bf16[16,96,128]{2,1,0:T(8,128)(2,1)S(1)} %collective-permute-done.4.refs_0_, bf16[1024,512]{1,0:T(8,128)(2,1)S(1)} %bitcast.11, ...), custom_call_target="tpu_custom_call" | custom-call | flops 5000000000 | bytes 1000000 | tf_op jit(solution)/shard_map/attend/pallas_call | solution.py:387
  82.7 0.0 copy-start.5
  82.7 0.2 collective-permute-done.refs_0_
  82.8 5.7 %attend.5 = bf16[16,48,256]{2,1,0:T(8,128)(2,1)S(1)} custom-call(s32[2]{0:T(128)S(1)} %pad_add_fusion.order_ref, bf16[16,144,256]{2,1,0:T(8,128)(2,1)S(1)} %all-to-all-done.1.own_ref, bf16[16,96,128]{2,1,0:T(8,128)(2,1)S(1)} %collective-permute-done.refs_0_, bf16[1024,512]{1,0:T(8,128)(2,1)S(1)} %bitcast.12, ...), custom_call_target="tpu_custom_call", output_to_operand_aliasing={{}: (8, {})} | custom-call | flops 5000000000 | bytes 1000000 | tf_op jit(solution)/shard_map/attend/pallas_call | solution.py:387
  88.6 16.4 %all_to_all.15.heads_ref = bf16[16,48,256]{2,1,0:T(8,128)(2,1)S(1)} all-to-all(bf16[16,48,256]{2,1,0:T(8,128)(2,1)S(1)} %attend.5), channel_id=1, replica_groups=mesh['xlo'=2,'core'=2,'xhi'=2,'y'=4,'z'=4] {'y','z'}, dimensions={0} | all-to-all | bytes 786432 | tf_op jit(solution)/shard_map/all_to_all | solution.py:503
  105.0 11.0 %finish.1 = (bf16[4,64,768]{2,1,0:T(8,128)(2,1)}, f32[3,4,1536]{2,1,0:T(4,128)}) custom-call(bf16[16,48,256]{2,1,0:T(8,128)(2,1)S(1)} %all_to_all.15.heads_ref, f32[256,768]{1,0:T(8,128)S(1)} %copy-done.2, bf16[768,768]{1,0:T(8,128)(2,1)} %output_ref.3, bf16[768,128]{1,0:T(8,128)(2,1)S(1)} %copy-done.5, f32[4,1536,128]{2,1,0:T(8,128)} %get-tuple-element.21.mid_ref, ...), custom_call_target="tpu_custom_call" | custom-call | flops 8000000000 | bytes 10000000 | tf_op jit(solution)/shard_map/finish/pallas_call | solution.py:471
  (24 shorter events, 0.1 us)
Async XLA Ops:
  7.6 8.4 %copy-start.3 = (bf16[1536,128]{1,0:T(8,128)(2,1)S(1)}, bf16[1536,128]{1,0:T(8,128)(2,1)}, u32[]{:S(2)}) copy-start(bf16[1536,128]{1,0:T(8,128)(2,1)} %cond_ref.1) | copy-start | bytes 1179652
  7.6 8.4 %copy-start.4 = (bf16[128,768]{1,0:T(8,128)(2,1)S(1)}, bf16[128,768]{1,0:T(8,128)(2,1)}, u32[]{:S(2)}) copy-start(bf16[128,768]{1,0:T(8,128)(2,1)} %to_token_ref.1) | copy-start | bytes 589828
  7.6 8.4 %copy-start.6 = (bf16[128,384]{1,0:T(8,128)(2,1)S(1)}, bf16[128,384]{1,0:T(8,128)(2,1)}, u32[]{:S(2)}) copy-start(bf16[128,384]{1,0:T(8,128)(2,1)} %proj_ref.2) | copy-start | bytes 294916
  7.6 8.4 %copy-start.7 = (bf16[64,768]{1,0:T(8,128)(2,1)S(1)}, bf16[64,768]{1,0:T(8,128)(2,1)}, u32[]{:S(2)}) copy-start(bf16[64,768]{1,0:T(8,128)(2,1)} %single_ref.1) | copy-start | bytes 294916
  7.7 8.4 %copy-start.8 = (f32[4,3,1536]{2,0,1:T(4,128)S(1)}, f32[4,3,1536]{2,0,1:T(4,128)}, u32[]{:S(2)}) copy-start(f32[4,3,1536]{2,0,1:T(4,128)} %param.18) | copy-start | bytes 221188
  7.7 8.4 %copy-start.9 = (bf16[128,128]{1,0:T(8,128)(2,1)S(1)}, bf16[128,128]{1,0:T(8,128)(2,1)}, u32[]{:S(2)}) copy-start(bf16[128,128]{1,0:T(8,128)(2,1)} %output_ref.2) | copy-start | bytes 98308
  7.7 8.4 %copy-start.10 = (s32[1536]{0:T(1024)S(1)}, s32[1536]{0:T(1024)}, u32[]{:S(2)}) copy-start(s32[1536]{0:T(1024)} %param.19) | copy-start | bytes 18436
  7.7 8.4 %copy-start.11 = (f32[3,128]{1,0:T(4,128)S(1)}, f32[3,128]{1,0:T(4,128)}, u32[]{:S(2)}) copy-start(f32[3,128]{1,0:T(4,128)} %pos_weight_ref.1) | copy-start | bytes 4612
  7.7 28.5 %all-to-all-start = ((bf16[16,64,512]{2,1,0:T(8,128)(2,1)}), bf16[16,64,512]{2,1,0:T(8,128)(2,1)S(1)}, u32[]{:S(2)}, u32[]{:S(2)}) async-start(bf16[16,64,512]{2,1,0:T(8,128)(2,1)} %pair_bias.1), calls=%async_computation | async-start | bytes 2097152 | tf_op jit(solution)/shard_map/all_to_all | solution.py:503
  36.2 8.8 %copy-start = (f32[128,3]{0,1:T(4,128)S(1)}, f32[128,3]{0,1:T(4,128)}, u32[]{:S(2)}) copy-start(f32[128,3]{0,1:T(4,128)} %param.33) | copy-start | bytes 4612
  36.3 24.8 %collective-permute-start.2 = (bf16[1024,512]{1,0:T(8,128)(2,1)S(1)}, bf16[1024,512]{1,0:T(8,128)(2,1)}, u32[]{:S(2)}, u32[]{:S(2)}) collective-permute-start(bf16[1024,512]{1,0:T(8,128)(2,1)S(1)} %bitcast.8), channel_id=1, source_target_pairs={{0,64},{64,0},{1,65},{65,1},{2,66},{66,2},{3,67},{67,3},{4,68},{68... | collective-permute-start | bytes 3145736 | tf_op jit(solution)/shard_map/ppermute | solution.py:499
  37.8 25.3 %all-to-all-start.1 = ((bf16[16,144,256]{2,1,0:T(8,128)(2,1)}), bf16[16,144,256]{2,1,0:T(8,128)(2,1)S(1)}, u32[]{:S(2)}, u32[]{:S(2)}) async-start(bf16[16,144,256]{2,1,0:T(8,128)(2,1)} %get-tuple-element.15), calls=%async_computation.1 | async-start | bytes 2359296 | tf_op jit(solution)/shard_map/all_to_all | solution.py:503
  46.8 0.9 copy-start.1
  47.7 19.2 %collective-permute-start.1 = (bf16[1024,512]{1,0:T(8,128)(2,1)S(1)}, bf16[1024,512]{1,0:T(8,128)(2,1)S(1)}, u32[]{:S(2)}, u32[]{:S(2)}) collective-permute-start(bf16[1024,512]{1,0:T(8,128)(2,1)S(1)} %bitcast.9), channel_id=1, source_target_pairs={{0,32},{32,0},{1,33},{33,1},{2,34},{34,2},{3,35},{35,3},{4,36},{36... | collective-permute-start | bytes 3145736 | tf_op jit(solution)/shard_map/ppermute | solution.py:499
  61.1 5.8 %collective-permute-start.3 = (bf16[1024,512]{1,0:T(8,128)(2,1)}, bf16[1024,512]{1,0:T(8,128)(2,1)}, u32[]{:S(2)}, u32[]{:S(2)}) collective-permute-start(bf16[1024,512]{1,0:T(8,128)(2,1)} %collective-permute-done.2.refs_2_.refs_3_), channel_id=1, source_target_pairs={{0,32},{32,0},{1,33},{33,1},{2,34},{34,2},{3,35},{35,3},{4,36},{36... | collective-permute-start | bytes 3145736 | tf_op jit(solution)/shard_map/ppermute | solution.py:499
  63.3 13.6 %collective-permute-start.4 = (bf16[16,96,128]{2,1,0:T(8,128)(2,1)S(1)}, bf16[16,96,128]{2,1,0:T(8,128)(2,1)S(1)}, u32[]{:S(2)}, u32[]{:S(2)}) collective-permute-start(bf16[16,96,128]{2,1,0:T(8,128)(2,1)S(1)} %get-tuple-element.26), channel_id=1, source_target_pairs={{0,16},{16,0},{1,17},{17,1},{2,18},{18,2},{3,19},{19,3},{4,20},{20... | collective-permute-start | bytes 1179656 | tf_op jit(solution)/shard_map/ppermute | solution.py:499
  66.1 16.7 %collective-permute-start = (bf16[16,96,128]{2,1,0:T(8,128)(2,1)S(1)}, bf16[16,96,128]{2,1,0:T(8,128)(2,1)S(1)}, u32[]{:S(2)}, u32[]{:S(2)}) collective-permute-start(bf16[16,96,128]{2,1,0:T(8,128)(2,1)S(1)} %get-tuple-element.27), channel_id=1, source_target_pairs={{0,16},{16,0},{1,17},{17,1},{2,18},{18,2},{3,19},{19,3},{4,20},{20... | collective-permute-start | bytes 1179656 | tf_op jit(solution)/shard_map/ppermute | solution.py:499
  82.6 22.4 %copy-start.2 = (f32[256,768]{1,0:T(8,128)S(1)}, f32[256,768]{1,0:T(8,128)}, u32[]{:S(2)}) copy-start(f32[256,768]{1,0:T(8,128)} %copy-done.1) | copy-start | bytes 2359300
  82.7 22.4 %copy-start.5 = (bf16[768,128]{1,0:T(8,128)(2,1)S(1)}, bf16[768,128]{1,0:T(8,128)(2,1)}, u32[]{:S(2)}) copy-start(bf16[768,128]{1,0:T(8,128)(2,1)} %to_atom_ref.1) | copy-start | bytes 589828
